TPU v7x, 512 devices: a whole 4x8x8 slice. The times are simulated.
512 devices in a mesh: sect: 2 (over core), grp: 64 (over y, z), tp: 4 (over x).
Axes of the slice: x: 4, y: 8, z: 8, core: 2. Of those that a mesh axis runs over, the one named last changes fastest.
Arguments:
- keys: bfloat16 [256, 256, 4096], P(('sect', 'grp'), 'tp'), may hold values from -4 to 4
- values: bfloat16 [256, 256, 4096], P(('sect', 'grp'), 'tp'), may hold values from -4 to 4
- frozen_query_projection: bfloat16 [8, 256, 4096], P('sect', None, 'grp'), may hold values from -32 to 32
- context_gradient: bfloat16 [8, 256, 4096], P('sect', None, 'grp'), may hold values from -48 to 48
- hidden: bfloat16 [8, 256, 4096], P('sect', None, 'grp'), may hold values from -6 to 6
- adapter_down_weight: bfloat16 [4096, 64], P('grp'), may hold values from -0.09375 to 0.09375
- adapter_up_weight: bfloat16 [64, 4096], P(None, 'grp'), may hold values from -0.09375 to 0.09375
- owner: int32 [256], P(('sect', 'grp')), may hold values from 0 to 4, as said below
- counts: int32 [128], P(('sect', 'grp')), may hold values from 1 to 2, as said below
- target_length: int32 [8], P('sect'), may hold values from 64 to 256
Outputs:
- adapted_query_gradient: bfloat16 [8, 256, 4096], P('sect', 'tp', 'grp')
- grad_keys: bfloat16 [256, 256, 4096], P(('sect', 'grp'), 'tp')
- grad_values: bfloat16 [256, 256, 4096], P(('sect', 'grp'), 'tp')
- grad_a: float32 [4096, 64], P('grp')
- grad_b: float32 [64, 4096], P(None, 'grp')
Inputs may be any that keep to these rules, and one draw needn't show every extreme that they name: `owner`: for live slots, the question among the 4 of the same half that reads the passage; every question is named by exactly 28 live slots; empty slots hold 4. `counts`: in each aligned block of four devices of a half exactly one device has 1 live slots and the others 2; live slots are the first ones of a device.
All inputs are finite; a program needn't handle non-finite values.
Results may differ from a plain program's by a relative error of at most 0.017.
The roundings to bfloat16 on the way count: a program that leaves them out, or rounds other values in their place, can miss the bound.
Values may be sent and summed in bfloat16 or wider, within the bound.
No kernel may reach another device: no remote copies, remote signals or barrier semaphores. Data moves between devices by JAX's collectives and lax.ppermute only.
A program may use at most 64 MiB of HBM per device.

v0:
```python
import jax
import jax.numpy as jnp
from jax import lax
from jax.sharding import PartitionSpec as P

HEAD_DIMENSION = 64


def passage_order(owner_all, counts_all, questions, per_question):
    slot_count = owner_all.shape[0]
    per_device = slot_count // counts_all.shape[0]
    position = jnp.arange(slot_count, dtype=jnp.int32) % per_device
    live = position < jnp.repeat(counts_all, per_device)
    sort_key = jnp.where(live, owner_all, questions)
    order = jnp.argsort(sort_key, stable=True)
    return order[: questions * per_question].reshape(questions, per_question)


def select_rows(table, chosen, head_count):
    picked = table[chosen]
    q_count, p_count, span, width = picked.shape
    return picked.reshape(q_count, p_count * span, head_count, width // head_count)


def place_rows(grads, chosen, total_slots, span):
    q_count, k_count, head_count, head_size = grads.shape
    flat_rows = grads.reshape(q_count * (k_count // span), span, head_count * head_size)
    empty = jnp.zeros((total_slots, span, head_count * head_size), grads.dtype)
    return empty.at[chosen.reshape(-1)].set(flat_rows)


def local(
    keys,
    values,
    frozen_query_projection,
    context_gradient,
    hidden,
    adapter_down_weight,
    adapter_up_weight,
    owner,
    counts,
    target_length,
):
    group_count = lax.axis_size("grp")
    token_split = lax.axis_size("tp")
    questions, targets, local_width = frozen_query_projection.shape
    slots_dev, span, width = keys.shape
    head_count = local_width // HEAD_DIMENSION
    per_question = (group_count * slots_dev - group_count // 4) // questions
    owner_all, counts_all = (
        lax.all_gather(owner, "grp", axis=0, tiled=True),
        lax.all_gather(counts, "grp", axis=0, tiled=True),
    )
    chosen = passage_order(owner_all, counts_all, questions, per_question)
    partial_latent = jnp.einsum(
        "vcu,uk->vck", hidden, adapter_down_weight, preferred_element_type=jnp.float32
    )
    adapter_latent = lax.psum(partial_latent, "grp").astype(jnp.bfloat16)
    raised_latent = jnp.einsum(
        "okh,hp->okp", adapter_latent, adapter_up_weight, preferred_element_type=jnp.float32
    )
    query = (frozen_query_projection.astype(jnp.float32) + raised_latent).astype(jnp.bfloat16)
    query_heads = query.reshape(questions, targets, head_count, HEAD_DIMENSION)
    step_ids = lax.broadcasted_iota(jnp.int32, (questions, targets), 1)
    keep = step_ids < target_length[:, None]
    upstream = jnp.where(keep[:, :, None], context_gradient, jnp.zeros_like(context_gradient))
    grad_heads = upstream.reshape(questions, targets, head_count, HEAD_DIMENSION)
    key_table, value_table = (
        lax.all_to_all(keys, "grp", split_axis=2, concat_axis=0, tiled=True),
        lax.all_to_all(values, "grp", split_axis=2, concat_axis=0, tiled=True),
    )
    total_slots = key_table.shape[0]
    key_sel = select_rows(key_table, chosen, head_count)
    scores = jnp.einsum("qthd,qkhd->qhtk", query_heads, key_sel, preferred_element_type=jnp.float32)
    local_top = jnp.max(scores, axis=3)
    row_top = lax.pmax(local_top, "tp")
    exp_scores = jnp.exp(scores - row_top[..., None])
    row_mass = lax.psum(jnp.sum(exp_scores, axis=3), "tp")
    weights = exp_scores / row_mass[..., None]
    weights_low = weights.astype(jnp.bfloat16)
    value_sel = select_rows(value_table, chosen, head_count)
    value_grad = jnp.einsum(
        "qhtk,qthd->qkhd", weights_low, grad_heads, preferred_element_type=jnp.float32
    ).astype(jnp.bfloat16)
    value_slots = place_rows(value_grad, chosen, total_slots, span)
    partial_out = jnp.einsum(
        "qhtk,qkhd->qthd", weights_low, value_sel, preferred_element_type=jnp.float32
    )
    grad_float = grad_heads.astype(jnp.float32)
    attended = lax.psum(partial_out, "tp")
    delta = jnp.sum(grad_float * attended, axis=3)
    delta_rows = jnp.transpose(delta, (0, 2, 1))
    prob_grad = jnp.einsum(
        "qthd,qkhd->qhtk", grad_heads, value_sel, preferred_element_type=jnp.float32
    )
    score_grad = (weights * (prob_grad - delta_rows[..., None])).astype(jnp.bfloat16)
    query_part = jnp.einsum(
        "qhtk,qkhd->qthd", score_grad, key_sel, preferred_element_type=jnp.float32
    )
    query_part = query_part.reshape(questions, targets, local_width)
    adapted_query_gradient = lax.psum_scatter(
        query_part, "tp", scatter_dimension=1, tiled=True
    ).astype(jnp.bfloat16)
    key_grad = jnp.einsum(
        "qhtk,qthd->qkhd", score_grad, query_heads, preferred_element_type=jnp.float32
    ).astype(jnp.bfloat16)
    key_slots = place_rows(key_grad, chosen, total_slots, span)
    key_back, value_back = (
        lax.all_to_all(key_slots, "grp", split_axis=0, concat_axis=2, tiled=True),
        lax.all_to_all(value_slots, "grp", split_axis=0, concat_axis=2, tiled=True),
    )
    latent_part_grad = jnp.einsum(
        "byh,uh->byu", adapted_query_gradient, adapter_up_weight, preferred_element_type=jnp.float32
    )
    adapter_latent_gradient = lax.psum(latent_part_grad, "grp").astype(jnp.bfloat16)
    row_count = targets // token_split
    row_start = lax.axis_index("tp") * row_count
    hidden_rows = lax.dynamic_slice_in_dim(hidden, row_start, row_count, 1)
    latent_rows = lax.dynamic_slice_in_dim(adapter_latent, row_start, row_count, 1)
    grad_a_part = jnp.einsum(
        "qtd,qtr->dr", hidden_rows, adapter_latent_gradient, preferred_element_type=jnp.float32
    )
    grad_b_part = jnp.einsum(
        "qtr,qtc->rc", latent_rows, adapted_query_gradient, preferred_element_type=jnp.float32
    )
    grad_a, grad_b = (
        lax.psum(grad_a_part.astype(jnp.bfloat16), ("sect", "tp")).astype(jnp.float32),
        lax.psum(grad_b_part.astype(jnp.bfloat16), ("sect", "tp")).astype(jnp.float32),
    )
    return (adapted_query_gradient, key_back, value_back, grad_a, grad_b)


def solution(mesh):
    return jax.shard_map(
        local,
        mesh=mesh,
        in_specs=(
            P(("sect", "grp"), "tp", None),
            P(("sect", "grp"), "tp", None),
            P("sect", None, "grp"),
            P("sect", None, "grp"),
            P("sect", None, "grp"),
            P("grp", None),
            P(None, "grp"),
            P(("sect", "grp")),
            P(("sect", "grp")),
            P("sect"),
        ),
        out_specs=(
            P("sect", "tp", "grp"),
            P(("sect", "grp"), "tp", None),
            P(("sect", "grp"), "tp", None),
            P("grp", None),
            P(None, "grp"),
        ),
        check_vma=False,
    )
```

profile of v0, /device:TPU:1, one launch (start us, length us, event | category | flops | bytes accessed | tf_op | source)
XLA Modules:
  0.0 917.1 jit_solution(17706118781307895371)
XLA Ops:
  7.2 5.1 copy.53
  14.6 17.1 %all-to-all-start = ((bf16[64,2,4096]{2,1,0:T(2,128)(2,1)}), bf16[64,2,4096]{2,1,0:T(2,128)(2,1)S(1)}, u32[]{:S(2)}, u32[]{:S(2)}) async-start(bf16[64,2,4096]{2,1,0:T(2,128)(2,1)} %reshape.199), calls=%async_computation | async-start | bytes 2097152 | tf_op jit(solution)/shard_map/all_to_all | solution.py:69
  35.3 34.5 %all-reduce.2 = (s32[128]{0:T(128)S(1)}, s32[64]{0:T(128)S(1)}) all-reduce(s32[128]{0:T(128)S(1)} %dynamic-update-slice.1, s32[64]{0:T(128)S(1)} %dynamic-update-slice), channel_id=1, replica_groups=mesh['sect'=2,'grp'=64,'tp'=4] {'grp'}, use_global_device_ids=true, to_apply=%add.1 | all-reduce | flops 192 | bytes 1536
  73.9 5.0 copy.59
  81.3 219.3 %all-reduce.8 = bf16[4,256,64]{1,2,0:T(8,128)(2,1)S(1)} all-reduce(f32[4,256,64]{1,2,0:T(8,128)S(1)} %fusion.17), channel_id=1, replica_groups=mesh['sect'=2,'grp'=64,'tp'=4] {'grp'}, use_global_device_ids=true, to_apply=%region_1.2 | all-reduce | flops 65536 | bytes 393216 | tf_op jit(solution)/shard_map/psum | solution.py:58
  302.4 8.9 all-to-all-start.1
  313.5 3.7 copy.54
  319.6 4.2 fusion.23
  323.8 8.7 pmax.7
  332.5 4.2 fusion.1
  336.7 6.3 psum.43
  343.1 5.1 fusion.4
  348.1 5.1 reshape.202
  353.2 3.7 copy.60
  356.9 3.7 gather_fusion.1
  360.6 2.8 fusion.3
  365.6 10.4 %scatter_fusion.1 = bf16[128,64,64]{2,1,0:T(8,128)(2,1)S(1)} fusion(bf16[128,64,64]{2,1,0:T(8,128)(2,1)S(1)} %broadcast.55.clone.1, s32[112]{0:T(128)S(1)} %copy-done.18, bf16[112,64,64]{2,1,0:T(8,128)(2,1)} %bitcast.99), kind=kCustom, calls=%fused_computation.3 | custom fusion | bytes 2752960 | tf_op jit(solution)/shard_map/scatter | solution.py:29
  378.3 11.8 %all-to-all-start.3 = ((bf16[64,2,4096]{2,1,0:T(2,128)(2,1)}), bf16[64,2,4096]{2,1,0:T(2,128)(2,1)S(1)}, u32[]{:S(2)}, u32[]{:S(2)}) async-start(bf16[64,2,4096]{2,1,0:T(2,128)(2,1)} %reshape.205), calls=%async_computation.3 | async-start | bytes 2097152 | tf_op jit(solution)/shard_map/all_to_all | solution.py:110
  390.2 4.0 convolution_bitcast_fusion.1
  394.2 119.1 %all-reduce.7.cloned.1.call-done = f32[4,256,1,64]{1,3,0,2:T(8,128)} async-done(((f32[4,256,1,64]{1,3,0,2:T(8,128)}), f32[4,256,1,64]{1,3,0,2:T(8,128)}) %all-reduce.7.cloned.1.call-update) | async-done | bytes 262160 | tf_op jit(solution)/shard_map/psum | solution.py:90
  514.3 4.5 multiply_convert_fusion
  523.6 10.4 %scatter_fusion = bf16[128,64,64]{2,1,0:T(8,128)(2,1)S(1)} fusion(bf16[128,64,64]{2,1,0:T(8,128)(2,1)S(1)} %broadcast.55.clone, s32[112]{0:T(128)S(1)} %copy-done.19, bf16[112,64,64]{2,1,0:T(8,128)(2,1)} %bitcast.98), kind=kCustom, calls=%fused_computation.2 | custom fusion | bytes 2752960 | tf_op jit(solution)/shard_map/scatter | solution.py:29
  536.3 13.4 %all-to-all-start.2 = ((bf16[64,2,4096]{2,1,0:T(2,128)(2,1)}), bf16[64,2,4096]{2,1,0:T(2,128)(2,1)}, u32[]{:S(2)}, u32[]{:S(2)}) async-start(bf16[64,2,4096]{2,1,0:T(2,128)(2,1)} %reshape.203), calls=%async_computation.2 | async-start | bytes 2097152 | tf_op jit(solution)/shard_map/all_to_all | solution.py:109
  550.0 3.3 convolution_bitcast_fusion
  554.6 26.7 %reduce-scatter.4.cloned.1.call-done = f32[64,256]{1,0:T(8,128)} async-done(((f32[256,256]{1,0:T(8,128)}), f32[64,256]{1,0:T(8,128)}) %reduce-scatter.4.cloned.1.call-update) | async-done | bytes 65552
  583.2 224.9 %psum.45 = bf16[4,64,64]{2,1,0:T(8,128)(2,1)S(1)} all-reduce(f32[4,64,64]{2,1,0:T(8,128)S(1)} %fusion.14), channel_id=1, replica_groups=mesh['sect'=2,'grp'=64,'tp'=4] {'grp'}, use_global_device_ids=true, to_apply=%region_11.12 | all-reduce | flops 16384 | bytes 98304 | tf_op jit(solution)/shard_map/psum | solution.py:115
  808.7 81.4 %all-reduce.3 = (bf16[64,64]{1,0:T(8,128)(2,1)S(1)}, bf16[64,64]{1,0:T(8,128)(2,1)S(1)}) all-reduce(bf16[64,64]{1,0:T(8,128)(2,1)S(1)} %fusion.6, bf16[64,64]{1,0:T(8,128)(2,1)S(1)} %fusion.7), channel_id=1, replica_groups=mesh['sect'=2,'grp'=64,'tp'=4] {'sect','tp'}, use_global_device_ids=true, to_apply=%region_12.13 | all-reduce | flops 8192 | bytes 32768 | tf_op jit(solution)/shard_map/psum | solution.py:127
  892.7 2.7 copy.70
  895.4 4.1 all_to_all.67
  899.6 3.8 reshape.204
  903.4 2.7 copy.67
  906.1 4.1 all_to_all.63
  (93 shorter events, 36.6 us)
Async XLA Ops:
  7.2 66.5 %copy-start = (bf16[4,256,64]{1,2,0:T(8,128)(2,1)S(1)}, bf16[4,256,64]{1,2,0:T(8,128)(2,1)}, u32[]{:S(2)}) copy-start(bf16[4,256,64]{1,2,0:T(8,128)(2,1)} %param.14) | copy-start | bytes 393220
  12.3 22.8 %copy-start.20 = (s32[2]{0:T(128)S(1)}, s32[2]{0:T(128)}, u32[]{:S(2)}) copy-start(s32[2]{0:T(128)} %param.17) | copy-start | bytes 28
  12.3 61.4 %copy-start.17 = (bf16[64,64]{1,0:T(8,128)(2,1)S(1)}, bf16[64,64]{1,0:T(8,128)(2,1)}, u32[]{:S(2)}) copy-start(bf16[64,64]{1,0:T(8,128)(2,1)} %param.15) | copy-start | bytes 24580
  14.6 287.8 %all-to-all-start = ((bf16[64,2,4096]{2,1,0:T(2,128)(2,1)}), bf16[64,2,4096]{2,1,0:T(2,128)(2,1)S(1)}, u32[]{:S(2)}, u32[]{:S(2)}) async-start(bf16[64,2,4096]{2,1,0:T(2,128)(2,1)} %reshape.199), calls=%async_computation | async-start | bytes 2097152 | tf_op jit(solution)/shard_map/all_to_all | solution.py:69
  79.0 222.3 %copy-start.8 = (bf16[64,64]{1,0:T(8,128)(2,1)S(1)}, bf16[64,64]{1,0:T(8,128)(2,1)}, u32[]{:S(2)}) copy-start(bf16[64,64]{1,0:T(8,128)(2,1)} %param.16) | copy-start | bytes 24580
  81.3 230.0 %copy-start.21 = (s32[4]{0:T(128)S(1)}, s32[4]{0:T(128)}, u32[]{:S(2)}) copy-start(s32[4]{0:T(128)} %param.19) | copy-start | bytes 52
  300.6 11.5 %copy-start.6 = (bf16[4,256,64]{1,2,0:T(8,128)(2,1)}, bf16[4,256,64]{1,2,0:T(8,128)(2,1)S(1)}, u32[]{:S(2)}) copy-start(bf16[4,256,64]{1,2,0:T(8,128)(2,1)S(1)} %all-reduce.8) | copy-start | bytes 393220
  302.4 45.7 %all-to-all-start.1 = ((bf16[64,2,4096]{2,1,0:T(2,128)(2,1)}), bf16[64,2,4096]{2,1,0:T(2,128)(2,1)}, u32[]{:S(2)}, u32[]{:S(2)}) async-start(bf16[64,2,4096]{2,1,0:T(2,128)(2,1)} %reshape.201), calls=%async_computation.1 | async-start | bytes 2097152 | tf_op jit(solution)/shard_map/all_to_all | solution.py:70
  312.1 5.1 copy-start.15
  319.6 4.2 copy-start.2
  332.5 10.5 %copy-start.9 = (f32[4,256]{1,0:T(4,128)}, f32[4,256]{1,0:T(4,128)S(1)}, u32[]{:S(2)}) copy-start(f32[4,256]{1,0:T(4,128)S(1)} %pmax.7) | copy-start | bytes 12292
  343.0 5.1 copy-start.13
  353.2 3.7 copy-start.16
  356.9 3.7 copy-start.5
  356.9 3.7 copy-start.11
  363.4 2.2 copy-start.18
  378.3 11.9 %copy-start.4 = (bf16[112,64,64]{2,1,0:T(8,128)(2,1)S(1)}, bf16[112,64,64]{2,1,0:T(8,128)(2,1)}, u32[]{:S(2)}) copy-start(bf16[112,64,64]{2,1,0:T(8,128)(2,1)} %gather_fusion.1) | copy-start | bytes 2752516
  378.3 158.0 %all-to-all-start.3 = ((bf16[64,2,4096]{2,1,0:T(2,128)(2,1)}), bf16[64,2,4096]{2,1,0:T(2,128)(2,1)S(1)}, u32[]{:S(2)}, u32[]{:S(2)}) async-start(bf16[64,2,4096]{2,1,0:T(2,128)(2,1)} %reshape.205), calls=%async_computation.3 | async-start | bytes 2097152 | tf_op jit(solution)/shard_map/all_to_all | solution.py:110
  390.1 123.2 %all-reduce.7.cloned.1.call-start = ((), (), s32[]{:S(2)}) async-start(), calls=%async_computation.5 | async-start | bytes 524288 | tf_op jit(solution)/shard_map/psum | solution.py:90
  390.2 123.1 %copy-start.12 = (pred[4,256]{1,0:T(4,128)(4,1)S(1)}, pred[4,256]{1,0:T(4,128)(4,1)}, u32[]{:S(2)}) copy-start(pred[4,256]{1,0:T(4,128)(4,1)} %iota_compare_fusion) | copy-start | bytes 3076
  390.2 124.1 %copy-start.10 = (f32[4,256]{1,0:T(4,128)S(1)}, f32[4,256]{1,0:T(4,128)}, u32[]{:S(2)}) copy-start(f32[4,256]{1,0:T(4,128)} %copy-done.9) | copy-start | bytes 12292
  390.2 124.1 %copy-start.14 = (f32[4,256]{1,0:T(4,128)S(1)}, f32[4,256]{1,0:T(4,128)}, u32[]{:S(2)}) copy-start(f32[4,256]{1,0:T(4,128)} %copy-done.13) | copy-start | bytes 12292
  518.8 1.8 copy-start.1
  521.4 2.2 copy-start.19
  536.3 13.7 %copy-start.3 = (bf16[112,64,64]{2,1,0:T(8,128)(2,1)S(1)}, bf16[112,64,64]{2,1,0:T(8,128)(2,1)}, u32[]{:S(2)}) copy-start(bf16[112,64,64]{2,1,0:T(8,128)(2,1)} %copy-done.2) | copy-start | bytes 2752516
  536.3 363.3 %all-to-all-start.2 = ((bf16[64,2,4096]{2,1,0:T(2,128)(2,1)}), bf16[64,2,4096]{2,1,0:T(2,128)(2,1)}, u32[]{:S(2)}, u32[]{:S(2)}) async-start(bf16[64,2,4096]{2,1,0:T(2,128)(2,1)} %reshape.203), calls=%async_computation.2 | async-start | bytes 2097152 | tf_op jit(solution)/shard_map/all_to_all | solution.py:109
  549.7 31.6 %reduce-scatter.4.cloned.1.call-start = ((), (), s32[]{:S(2)}) async-start(), calls=%async_computation.6 | async-start | bytes 327680
  553.2 255.0 %copy-start.7 = (bf16[4,256,64]{1,2,0:T(8,128)(2,1)S(1)}, bf16[4,256,64]{1,2,0:T(8,128)(2,1)}, u32[]{:S(2)}) copy-start(bf16[4,256,64]{1,2,0:T(8,128)(2,1)} %copy-done.6) | copy-start | bytes 393220
Sparse Core Ops, SparseCore 0:
  394.3 118.9 all-reduce.6
  554.7 26.5 reduce-scatter.3
where the time goes:
time: 919 us; the launch traced here: 917 us
  blocking collectives  575 us (63%)
  waiting for transfers between devices  146 us (16%)
  local copies, waits for them, and re-layouts  91.4 us (10%)
  starting transfers between devices  51.5 us (6%)
  matrix products  21.5 us (2%)
  other arithmetic  15.9 us (2%)
  between operations  15.8 us (2%)
    psum x1, blocking collectives, local(): lax.psum(latent_part_grad, 'grp').astype(jnp.bfloat16)  225 us
    psum x1, blocking collectives, local(): adapter_latent = lax.psum(partial_latent, 'grp').astype(jnp.bfloat16)  219 us
    psum x1, waiting for transfers between devices, local(): attended = lax.psum(partial_out, 'tp')  119 us
    psum x1, blocking collectives, local(): lax.psum(grad_a_part.astype(jnp.bfloat16), ('sect', 'tp'))  81.4 us
    unnamed x63, local copies, waits for them, and re-layouts  38.1 us
    unnamed x1, blocking collectives  34.5 us
    unnamed x3, waiting for transfers between devices  26.8 us
    scatter x2, local copies, waits for them, and re-layouts, place_rows(): return empty.at[chosen.reshape(-1)].set(flat_rows)  20.8 us
  transfers between devices with their start and end apart: 6, of which 2 were waited for; matrix products, arithmetic and copies ran while one was open for 8% of the time, Pallas kernels for 0%

commit v1 on v0

v1 whole, which is shorter than its diff:
```python
import functools

import jax
import jax.numpy as jnp
from jax import lax
from jax.experimental import pallas as pl
from jax.experimental.pallas import tpu as pltpu
from jax.sharding import PartitionSpec as P

HEAD = 64
BF16 = jnp.bfloat16
F32 = jnp.float32
VMEM_LIMIT = 32 * 1024 * 1024


def pack_kernel(k_ref, v_ref, o_ref):
    slots, span, width = k_ref.shape
    for pair in range(width // (2 * HEAD)):
        low = pair * 2 * HEAD
        for slot in range(slots):
            rows = pl.ds(slot * span, span)
            k = k_ref[slot, :, low : low + 2 * HEAD]
            v = v_ref[slot, :, low : low + 2 * HEAD]
            o_ref[2 * pair, rows, :] = jnp.concatenate([k[:, :HEAD], v[:, :HEAD]], axis=1)
            o_ref[2 * pair + 1, rows, :] = jnp.concatenate([k[:, HEAD:], v[:, HEAD:]], axis=1)


def unpack_kernel(i_ref, k_ref, v_ref):
    slots, span, width = k_ref.shape
    for pair in range(width // (2 * HEAD)):
        low = pair * 2 * HEAD
        for slot in range(slots):
            rows = pl.ds(slot * span, span)
            even = i_ref[2 * pair, rows, :]
            odd = i_ref[2 * pair + 1, rows, :]
            k_ref[slot, :, low : low + 2 * HEAD] = jnp.concatenate([even[:, :HEAD], odd[:, :HEAD]], axis=1)
            v_ref[slot, :, low : low + 2 * HEAD] = jnp.concatenate([even[:, HEAD:], odd[:, HEAD:]], axis=1)


PACK_HEADS = 16


def pack(keys, values):
    slots, span, width = keys.shape
    heads = width // HEAD
    part = pl.BlockSpec((slots, span, PACK_HEADS * HEAD), lambda i: (0, 0, i))
    return pl.pallas_call(
        pack_kernel,
        grid=(heads // PACK_HEADS,),
        in_specs=[part, part],
        out_specs=pl.BlockSpec((PACK_HEADS, slots * span, 2 * HEAD), lambda i: (i, 0, 0)),
        out_shape=jax.ShapeDtypeStruct((heads, slots * span, 2 * HEAD), keys.dtype),
        compiler_params=pltpu.CompilerParams(vmem_limit_bytes=VMEM_LIMIT),
        cost_estimate=pl.CostEstimate(flops=0, bytes_accessed=8 * slots * span * width, transcendentals=0),
        name="pack",
    )(keys, values)


def unpack(table, slots):
    heads, rows, _ = table.shape
    span = rows // slots
    part = pl.BlockSpec((slots, span, PACK_HEADS * HEAD), lambda i: (0, 0, i))
    shape = jax.ShapeDtypeStruct((slots, span, heads * HEAD), table.dtype)
    return pl.pallas_call(
        unpack_kernel,
        grid=(heads // PACK_HEADS,),
        in_specs=[pl.BlockSpec((PACK_HEADS, rows, 2 * HEAD), lambda i: (i, 0, 0))],
        out_specs=[part, part],
        out_shape=[shape, shape],
        compiler_params=pltpu.CompilerParams(vmem_limit_bytes=VMEM_LIMIT),
        cost_estimate=pl.CostEstimate(flops=0, bytes_accessed=8 * slots * span * heads * HEAD, transcendentals=0),
        name="unpack",
    )(table)


CHUNK_SLOTS = 4


def two_sided(q_ref, u_ref):
    q, u = q_ref[0], u_ref[0]
    zero = jnp.zeros_like(q)
    return jnp.concatenate(
        [jnp.concatenate([q, zero], axis=1), jnp.concatenate([zero, u], axis=1)], axis=0
    )


def gathered(chosen_ref, t_ref, question, per_question, chunk):
    return jnp.concatenate(
        [
            t_ref[chosen_ref[question * per_question + chunk * CHUNK_SLOTS + i]]
            for i in range(CHUNK_SLOTS)
        ],
        axis=0,
    )


def stats_kernel(per_question, chosen_ref, q_ref, u_ref, t_ref, o_ref):
    question = pl.program_id(0)
    targets = q_ref.shape[2]
    both = two_sided(q_ref, u_ref)
    top = jnp.full((1, targets), -jnp.inf, F32)
    mass = jnp.zeros((1, targets), F32)
    dot = jnp.zeros((1, targets), F32)
    for chunk in range(per_question // CHUNK_SLOTS):
        rows = gathered(chosen_ref, t_ref, question, per_question, chunk)
        prod = jnp.dot(rows, both, preferred_element_type=F32)
        scores, prob_grad = prod[:, :targets], prod[:, targets:]
        new_top = jnp.maximum(top, jnp.max(scores, axis=0, keepdims=True))
        scale = jnp.exp(top - new_top)
        exp_scores = jnp.exp(scores - new_top)
        mass = mass * scale + jnp.sum(exp_scores, axis=0, keepdims=True)
        dot = dot * scale + jnp.sum(exp_scores * prob_grad, axis=0, keepdims=True)
        top = new_top
    o_ref[0] = jnp.concatenate([top, mass, dot, jnp.zeros((5, targets), F32)], axis=0)


def grad_kernel(per_question, chosen_ref, q_ref, u_ref, s_ref, t_ref, dq_ref, o_ref):
    question = pl.program_id(0)
    targets = q_ref.shape[2]
    peers, _, pair_width = dq_ref.shape
    piece = targets // peers

    @pl.when(question == 0)
    def _():
        o_ref[...] = jnp.zeros_like(o_ref)

    both = two_sided(q_ref, u_ref)
    top, inverse, delta = s_ref[0, 0:1, :], s_ref[0, 1:2, :], s_ref[0, 2:3, :]
    dq = jnp.zeros((2 * HEAD, targets), F32)
    for chunk in range(per_question // CHUNK_SLOTS):
        rows = gathered(chosen_ref, t_ref, question, per_question, chunk)
        span = t_ref.shape[1]
        prod = jnp.dot(rows, both, preferred_element_type=F32)
        scores, prob_grad = prod[:, :targets], prod[:, targets:]
        weights = jnp.exp(scores - top) * inverse
        score_grad = (weights * (prob_grad - delta)).astype(BF16)
        pair = jnp.concatenate([score_grad, weights.astype(BF16)], axis=1)
        out = lax.dot_general(
            pair, both, (((1,), (1,)), ((), ())), preferred_element_type=F32
        ).astype(BF16)
        for i in range(CHUNK_SLOTS):
            o_ref[chosen_ref[question * per_question + chunk * CHUNK_SLOTS + i]] = out[
                i * span : (i + 1) * span
            ]
        dq = dq + lax.dot_general(
            rows, score_grad, (((0,), (0,)), ((), ())), preferred_element_type=F32
        )

    for side in range(pair_width // piece):

        @pl.when(question % (pair_width // piece) == side)
        def _():
            for peer in range(peers):
                dq_ref[peer, :, side * piece : (side + 1) * piece] = dq[
                    :HEAD, peer * piece : (peer + 1) * piece
                ]


def attend_stats(chosen, query_t, upstream_t, table, per_question):
    questions, size, targets = query_t.shape
    one = pl.BlockSpec((1, size, targets), lambda q, c: (q, 0, 0))
    whole = pl.BlockSpec(table.shape, lambda q, c: (0, 0, 0))
    keys = per_question * table.shape[1]
    return pl.pallas_call(
        functools.partial(stats_kernel, per_question),
        grid_spec=pltpu.PrefetchScalarGridSpec(
            num_scalar_prefetch=1,
            grid=(questions,),
            in_specs=[one, one, whole],
            out_specs=pl.BlockSpec((1, 8, targets), lambda q, c: (q, 0, 0)),
        ),
        out_shape=jax.ShapeDtypeStruct((questions, 8, targets), F32),
        compiler_params=pltpu.CompilerParams(vmem_limit_bytes=VMEM_LIMIT),
        cost_estimate=pl.CostEstimate(
            flops=8 * questions * targets * keys * HEAD,
            bytes_accessed=2 * table.size,
            transcendentals=questions * targets * keys,
        ),
        name="stats",
    )(chosen, query_t, upstream_t, table)


def attend_grads(chosen, query_t, upstream_t, stats, table, per_question, peers):
    questions, size, targets = query_t.shape
    one = pl.BlockSpec((1, size, targets), lambda q, c: (q, 0, 0))
    whole = pl.BlockSpec(table.shape, lambda q, c: (0, 0, 0))
    keys = per_question * table.shape[1]
    piece = targets // peers
    in_block = 128 // piece
    return pl.pallas_call(
        functools.partial(grad_kernel, per_question),
        grid_spec=pltpu.PrefetchScalarGridSpec(
            num_scalar_prefetch=1,
            grid=(questions,),
            in_specs=[one, one, pl.BlockSpec((1, 8, targets), lambda q, c: (q, 0, 0)), whole],
            out_specs=[
                pl.BlockSpec((peers, HEAD, 128), lambda q, c: (0, 0, q // in_block)),
                whole,
            ],
        ),
        out_shape=[
            jax.ShapeDtypeStruct((peers, HEAD, questions * piece), F32),
            jax.ShapeDtypeStruct(table.shape, BF16),
        ],
        compiler_params=pltpu.CompilerParams(vmem_limit_bytes=VMEM_LIMIT),
        cost_estimate=pl.CostEstimate(
            flops=24 * questions * targets * keys * HEAD,
            bytes_accessed=4 * table.size,
            transcendentals=questions * targets * keys,
        ),
        name="grads",
    )(chosen, query_t, upstream_t, stats, table)


def swap_sum(x, axis, shift, radix):
    size = lax.axis_size(axis)
    got = [x] + [
        lax.ppermute(x, axis, [(i, i ^ (k << shift)) for i in range(size)]) for k in range(1, radix)
    ]
    while len(got) > 1:
        got = [a + b for a, b in zip(got[0::2], got[1::2])]
    return got[0]


def group_sum(x):
    size, shift = lax.axis_size("grp"), 0
    while (1 << shift) < size:
        radix = min(4, size >> shift)
        x = swap_sum(x, "grp", shift, radix)
        shift += radix.bit_length() - 1
    return x


def gather_tp(x):
    size, here = lax.axis_size("tp"), lax.axis_index("tp")
    got = [x] + [
        lax.ppermute(x, "tp", [(i, (i + k) % size) for i in range(size)]) for k in range(1, size)
    ]
    order = (here - jnp.arange(size, dtype=jnp.int32)) % size
    return jnp.stack(got)[order]


def scatter_sum_tp(x):
    size, here = lax.axis_size("tp"), lax.axis_index("tp")
    own = lax.dynamic_index_in_dim(x, here, 0, keepdims=False)
    for k in range(1, size):
        sent = lax.dynamic_index_in_dim(x, (here + k) % size, 0, keepdims=False)
        own = own + lax.ppermute(sent, "tp", [(i, (i + k) % size) for i in range(size)])
    return own


def local(
    keys,
    values,
    frozen_query_projection,
    context_gradient,
    hidden,
    adapter_down_weight,
    adapter_up_weight,
    owner,
    counts,
    target_length,
):
    group_count, token_split = lax.axis_size("grp"), lax.axis_size("tp")
    questions, targets, _ = frozen_query_projection.shape
    slots_dev, span, _ = keys.shape
    total_slots = group_count * slots_dev
    per_question = (total_slots - group_count // 4) // questions
    piece = targets // token_split

    packed = pack(keys, values)
    table = lax.all_to_all(packed, "grp", split_axis=0, concat_axis=0, tiled=True)
    table = table.reshape(total_slots, span, 2 * HEAD)

    start = lax.axis_index("tp") * piece
    hidden_t = jnp.swapaxes(hidden, 1, 2)
    hidden_cut = lax.dynamic_slice_in_dim(hidden_t, start, piece, 2)
    hidden_cut = jnp.transpose(hidden_cut, (1, 0, 2)).reshape(HEAD, questions * piece)
    latent_part = lax.dot_general(
        adapter_down_weight, hidden_cut, (((0,), (0,)), ((), ())), preferred_element_type=F32
    )
    live = jnp.arange(slots_dev, dtype=jnp.int32) < counts[0]
    tag = jnp.where(live, owner, questions).astype(F32)
    own_slots = lax.axis_index("grp") * slots_dev
    tag_row = jnp.zeros((questions * piece,), F32)
    tag_row = lax.dynamic_update_slice(tag_row, tag, (own_slots,))
    tags = jnp.pad(tag_row[None], ((0, 7), (0, 0)))
    summed = group_sum(jnp.concatenate([latent_part, tags], axis=0))
    latent_cut = summed[:HEAD].astype(BF16)

    slot_key = summed[HEAD, :total_slots].astype(jnp.int32)
    slot_ids = jnp.arange(total_slots, dtype=jnp.int32)
    same = (slot_key[:, None] == slot_key[None, :]) & (slot_ids[None, :] < slot_ids[:, None])
    rank = jnp.sum(same.astype(jnp.int32), axis=1)
    place = slot_key * per_question + rank
    wanted = jnp.arange(questions * per_question, dtype=jnp.int32)
    hit = (place[None, :] == wanted[:, None]) & (slot_key < questions)[None, :]
    chosen = jnp.sum(jnp.where(hit, slot_ids[None, :], 0), axis=1)

    latent_all = gather_tp(latent_cut).reshape(token_split, HEAD, questions, piece)
    latent_t = jnp.transpose(latent_all, (2, 1, 0, 3)).reshape(questions, HEAD, targets)
    raised = jnp.einsum("rd,qrt->qdt", adapter_up_weight, latent_t, preferred_element_type=F32)
    frozen_t = jnp.swapaxes(frozen_query_projection, 1, 2)
    query_t = (frozen_t.astype(F32) + raised).astype(BF16)
    step_ids = lax.broadcasted_iota(jnp.int32, (questions, 1, targets), 2)
    keep = step_ids < target_length[:, None, None]
    upstream_t = jnp.swapaxes(context_gradient, 1, 2)
    upstream_t = jnp.where(keep, upstream_t, jnp.zeros_like(upstream_t))

    stats = attend_stats(chosen, query_t, upstream_t, table, per_question)
    size = lax.axis_size("tp")
    parts = [stats] + [
        lax.ppermute(stats, "tp", [(i, i ^ k) for i in range(size)]) for k in range(1, size)
    ]
    tops = [p[:, 0] for p in parts]
    top = functools.reduce(jnp.maximum, tops)
    scales = [jnp.exp(t - top) for t in tops]
    mass = sum(p[:, 1] * s for p, s in zip(parts, scales))
    inverse = 1.0 / mass
    delta = sum(p[:, 2] * s for p, s in zip(parts, scales)) * inverse
    zeros = jnp.zeros_like(top)
    row_stats = jnp.stack([top, inverse, delta] + [zeros] * 5, axis=1)

    dq_parts, grad_table = attend_grads(
        chosen, query_t, upstream_t, row_stats, table, per_question, token_split
    )
    back = lax.all_to_all(
        grad_table.reshape(group_count, slots_dev * span, 2 * HEAD),
        "grp",
        split_axis=0,
        concat_axis=0,
        tiled=True,
    )
    grad_keys, grad_values = unpack(back, slots_dev)

    dq_t = scatter_sum_tp(dq_parts).astype(BF16)
    adapted = jnp.transpose(dq_t.reshape(HEAD, questions, piece), (1, 2, 0))
    latent_grad_part = jnp.dot(adapter_up_weight, dq_t, preferred_element_type=F32)
    latent_grad = group_sum(latent_grad_part).astype(BF16)
    last = (((1,), (1,)), ((), ()))
    grad_a = lax.dot_general(hidden_cut, latent_grad, last, preferred_element_type=F32)
    grad_b = lax.dot_general(latent_cut, dq_t, last, preferred_element_type=F32)
    both = jnp.concatenate([grad_a, grad_b], axis=1)
    both = swap_sum(swap_sum(both, "tp", 0, token_split), "sect", 0, lax.axis_size("sect"))
    return (adapted, grad_keys, grad_values, both[:, :HEAD], both[:, HEAD:])


def solution(mesh):
    return jax.shard_map(
        local,
        mesh=mesh,
        in_specs=(
            P(("sect", "grp"), "tp", None),
            P(("sect", "grp"), "tp", None),
            P("sect", None, "grp"),
            P("sect", None, "grp"),
            P("sect", None, "grp"),
            P("grp", None),
            P(None, "grp"),
            P(("sect", "grp")),
            P(("sect", "grp")),
            P("sect"),
        ),
        out_specs=(
            P("sect", "tp", "grp"),
            P(("sect", "grp"), "tp", None),
            P(("sect", "grp"), "tp", None),
            P("grp", None),
            P(None, "grp"),
        ),
        check_vma=False,
    )
```

time: 919 us -> 278 us (0.30)
  blocking collectives: 575 us -> 0 us
  starting transfers between devices: 51.5 us -> 145 us
  local copies, waits for them, and re-layouts: 91.4 us -> 6.93 us
  waiting for transfers between devices: 146 us -> 105 us
  matrix products: 21.5 us -> 0.8 us
  Pallas kernels: 0 us -> 16.4 us
  other arithmetic: 15.9 us -> 0.71 us
  between operations: 15.8 us -> 2.02 us
    psum x4 -> x0, blocking collectives: 532 us -> none  [the longest x1 225 us: local(): lax.psum(latent_part_grad, 'grp').astype(jnp.bfloat16)]
    psum x1 -> x0, waiting for transfers between devices: 119 us -> none  [local(): attended = lax.psum(partial_out, 'tp')]
    ppermute x0 -> x31, starting transfers between devices: none -> 116 us  [the longest x22 86.8 us: swap_sum(): lax.ppermute(x, axis, [(i, i ^ k << shift) for i in range(size)])]
    ppermute x0 -> x31, waiting for transfers between devices: none -> 105 us  [the longest x22 97.4 us: swap_sum(): lax.ppermute(x, axis, [(i, i ^ k << shift) for i in range(size)])]
    unnamed x1 -> x0, blocking collectives: 34.5 us -> none
    unnamed x63 -> x20, local copies, waits for them, and re-layouts: 38.1 us -> 3.86 us
    unnamed x3 -> x0, waiting for transfers between devices: 26.8 us -> none
    all_to_all x4 -> x2, starting transfers between devices: 51.2 us -> 28.9 us  [the longest x1 17.3 us: local(): lax.all_to_all(packed, 'grp', split_axis=0, concat_axis=0, tiled=True)]
  transfers between devices with their start and end apart: 6 -> 33, of which waited for: 2 -> 16; matrix products, arithmetic and copies ran while one was open for 8% -> 2% of each run, Pallas kernels for 0% -> 0%
where the time goes in v1:
time: 278 us; the launch traced here: 276 us
  starting transfers between devices  145 us (52%)
  waiting for transfers between devices  105 us (38%)
  Pallas kernels  16.4 us (6%)
  local copies, waits for them, and re-layouts  6.93 us (2%)
    ppermute x22, waiting for transfers between devices, swap_sum(): lax.ppermute(x, axis, [(i, i ^ k << shift) for i in range(size)])  97.4 us
    ppermute x22, starting transfers between devices, swap_sum(): lax.ppermute(x, axis, [(i, i ^ k << shift) for i in range(size)])  86.8 us
    all_to_all x1, starting transfers between devices, local(): lax.all_to_all(packed, 'grp', split_axis=0, concat_axis=0, tiled=True)  17.3 us
    all_to_all x1, starting transfers between devices, local(): lax.all_to_all(grad_table.reshape(group_count, slots_dev * span, 2 * HEAD...  11.6 us
    ppermute x3, starting transfers between devices, gather_tp(): lax.ppermute(x, 'tp', [(i, (i + k) % size) for i in range(size)])  9.93 us
    ppermute x3, starting transfers between devices, local(): lax.ppermute(stats, 'tp', [(i, i ^ k) for i in range(size)])  9.58 us
    ppermute x3, starting transfers between devices, scatter_sum_tp(): lax.ppermute(sent, 'tp', [(i, (i + k) % size) for i in range(size)])  9.29 us
    pallas_call x1, Pallas kernels, attend_grads(): pl.pallas_call(functools.partial(grad_kernel, per_question), grid_spec=pl...  8.17 us
  transfers between devices with their start and end apart: 33, of which 16 were waited for; matrix products, arithmetic and copies ran while one was open for 2% of the time, Pallas kernels for 0%

profile of v1, /device:TPU:1, one launch (start us, length us, event | category | flops | bytes accessed | tf_op | source)
XLA Modules:
  0.0 276.4 jit_solution(14174456650062169864)
XLA Ops:
  5.5 17.3 %all-to-all-start = ((bf16[64,128,128]{2,1,0:T(8,128)(2,1)}), bf16[64,128,128]{2,1,0:T(8,128)(2,1)S(1)}, u32[]{:S(2)}, u32[]{:S(2)}) async-start(bf16[64,128,128]{2,1,0:T(8,128)(2,1)} %pack.1), calls=%async_computation | async-start | bytes 4194304 | tf_op jit(solution)/shard_map/all_to_all | solution.py:272
  24.2 3.0 %collective-permute-start = (f32[72,256]{1,0:T(8,128)S(1)}, f32[72,256]{1,0:T(8,128)S(1)}, u32[]{:S(2)}, u32[]{:S(2)}) collective-permute-start(f32[72,256]{1,0:T(8,128)S(1)} %select_maximum_fusion), channel_id=1, source_target_pairs={{0,4},{4,0},{8,12},{12,8},{16,20},{20,16},{24,28},{28,24},{32,36},... | collective-permute-start | bytes 221192 | tf_op jit(solution)/shard_map/ppermute | solution.py:218
  27.2 4.0 %collective-permute-start.1 = (f32[72,256]{1,0:T(8,128)S(1)}, f32[72,256]{1,0:T(8,128)S(1)}, u32[]{:S(2)}, u32[]{:S(2)}) collective-permute-start(f32[72,256]{1,0:T(8,128)S(1)} %select_maximum_fusion), channel_id=1, source_target_pairs={{0,8},{4,12},{8,0},{12,4},{16,24},{20,28},{24,16},{28,20},{32,40},... | collective-permute-start | bytes 221192 | tf_op jit(solution)/shard_map/ppermute | solution.py:218
  33.6 37.4 %collective-permute-done = f32[72,256]{1,0:T(8,128)S(1)} collective-permute-done((f32[72,256]{1,0:T(8,128)S(1)}, f32[72,256]{1,0:T(8,128)S(1)}, u32[]{:S(2)}, u32[]{:S(2)}) %collective-permute-start) | collective-permute-done | bytes 73760 | tf_op jit(solution)/shard_map/ppermute | solution.py:218
  76.0 5.8 %collective-permute-start.3 = (f32[72,256]{1,0:T(8,128)S(1)}, f32[72,256]{1,0:T(8,128)S(1)}, u32[]{:S(2)}, u32[]{:S(2)}) collective-permute-start(f32[72,256]{1,0:T(8,128)S(1)} %add_add_fusion.2), channel_id=1, source_target_pairs={{0,16},{4,20},{8,24},{12,28},{16,0},{20,4},{24,8},{28,12},{32,48},... | collective-permute-start | bytes 221192 | tf_op jit(solution)/shard_map/ppermute | solution.py:218
  81.8 3.7 %collective-permute-start.4 = (f32[72,256]{1,0:T(8,128)S(1)}, f32[72,256]{1,0:T(8,128)S(1)}, u32[]{:S(2)}, u32[]{:S(2)}) collective-permute-start(f32[72,256]{1,0:T(8,128)S(1)} %add_add_fusion.2), channel_id=1, source_target_pairs={{0,32},{4,36},{8,40},{12,44},{16,48},{20,52},{24,56},{28,60},{32,0... | collective-permute-start | bytes 221192 | tf_op jit(solution)/shard_map/ppermute | solution.py:218
  85.6 4.3 %collective-permute-start.5 = (f32[72,256]{1,0:T(8,128)S(1)}, f32[72,256]{1,0:T(8,128)S(1)}, u32[]{:S(2)}, u32[]{:S(2)}) collective-permute-start(f32[72,256]{1,0:T(8,128)S(1)} %add_add_fusion.2), channel_id=1, source_target_pairs={{0,48},{4,52},{8,56},{12,60},{16,32},{20,36},{24,40},{28,44},{32,1... | collective-permute-start | bytes 221192 | tf_op jit(solution)/shard_map/ppermute | solution.py:218
  89.9 5.7 %collective-permute-done.5 = f32[72,256]{1,0:T(8,128)S(1)} collective-permute-done((f32[72,256]{1,0:T(8,128)S(1)}, f32[72,256]{1,0:T(8,128)S(1)}, u32[]{:S(2)}, u32[]{:S(2)}) %collective-permute-start.5) | collective-permute-done | bytes 73760 | tf_op jit(solution)/shard_map/ppermute | solution.py:218
  95.6 5.7 %collective-permute-start.6 = (f32[72,256]{1,0:T(8,128)S(1)}, f32[72,256]{1,0:T(8,128)S(1)}, u32[]{:S(2)}, u32[]{:S(2)}) collective-permute-start(f32[72,256]{1,0:T(8,128)S(1)} %add_add_fusion.1), channel_id=1, source_target_pairs={{0,64},{4,68},{8,72},{12,76},{16,80},{20,84},{24,88},{28,92},{32,9... | collective-permute-start | bytes 221192 | tf_op jit(solution)/shard_map/ppermute | solution.py:218
  101.4 3.2 %collective-permute-start.7 = (f32[72,256]{1,0:T(8,128)S(1)}, f32[72,256]{1,0:T(8,128)S(1)}, u32[]{:S(2)}, u32[]{:S(2)}) collective-permute-start(f32[72,256]{1,0:T(8,128)S(1)} %add_add_fusion.1), channel_id=1, source_target_pairs={{0,128},{4,132},{8,136},{12,140},{16,144},{20,148},{24,152},{28,15... | collective-permute-start | bytes 221192 | tf_op jit(solution)/shard_map/ppermute | solution.py:218
  104.5 4.0 %collective-permute-start.8 = (f32[72,256]{1,0:T(8,128)S(1)}, f32[72,256]{1,0:T(8,128)S(1)}, u32[]{:S(2)}, u32[]{:S(2)}) collective-permute-start(f32[72,256]{1,0:T(8,128)S(1)} %add_add_fusion.1), channel_id=1, source_target_pairs={{0,192},{4,196},{8,200},{12,204},{16,208},{20,212},{24,216},{28,22... | collective-permute-start | bytes 221192 | tf_op jit(solution)/shard_map/ppermute | solution.py:218
  112.5 4.7 %collective-permute-start.10 = (bf16[64,256]{1,0:T(8,128)(2,1)S(1)}, bf16[64,256]{1,0:T(8,128)(2,1)S(1)}, u32[]{:S(2)}, u32[]{:S(2)}) collective-permute-start(bf16[64,256]{1,0:T(8,128)(2,1)S(1)} %slice.157), channel_id=1, source_target_pairs={{0,2},{1,3},{2,0},{3,1},{4,6},{5,7},{6,4},{7,5},{8,10},{9,11},{10,... | collective-permute-start | bytes 98312 | tf_op jit(solution)/shard_map/ppermute | solution.py:237
  122.8 3.0 %collective-permute-done.9 = bf16[64,256]{1,0:T(8,128)(2,1)S(1)} collective-permute-done((bf16[64,256]{1,0:T(8,128)(2,1)S(1)}, bf16[64,256]{1,0:T(8,128)(2,1)S(1)}, u32[]{:S(2)}, u32[]{:S(2)}) %collective-permute-start.9) | collective-permute-done | bytes 32800 | tf_op jit(solution)/shard_map/ppermute | solution.py:237
  127.2 3.6 %stats.1 = f32[4,8,256]{2,1,0:T(8,128)S(1)} custom-call(s32[112]{0:T(128)S(1)} %select_reduce_fusion.chosen_ref, bf16[4,64,256]{2,1,0:T(8,128)(2,1)S(1)} %fusion.1.q_ref, bf16[4,64,256]{2,1,0:T(8,128)(2,1)S(1)} %select_bitcast_fusion.u_ref, bf16[128,64,128]{2,1,0:T(8,128)(2,1)S(1)} %bitcast.62), custom_call_target="tpu_custom_call" | custom-call | flops 939524096 | bytes 2097152 | tf_op jit(solution)/shard_map/stats/pallas_call | solution.py:164
  135.6 4.9 %collective-permute-start.14 = (f32[4,8,256]{2,1,0:T(8,128)S(1)}, f32[4,8,256]{2,1,0:T(8,128)S(1)}, u32[]{:S(2)}, u32[]{:S(2)}) collective-permute-start(f32[4,8,256]{2,1,0:T(8,128)S(1)} %stats.1), channel_id=1, source_target_pairs={{0,3},{1,2},{2,1},{3,0},{4,7},{5,6},{6,5},{7,4},{8,11},{9,10},{10,... | collective-permute-start | bytes 98312 | tf_op jit(solution)/shard_map/ppermute | solution.py:313
  141.9 8.2 %grads.1 = (f32[4,64,256]{2,1,0:T(8,128)S(1)}, bf16[128,64,128]{2,1,0:T(8,128)(2,1)S(1)}) custom-call(s32[112]{0:T(128)S(1)} %select_reduce_fusion.chosen_ref, bf16[4,64,256]{2,1,0:T(8,128)(2,1)S(1)} %fusion.1.q_ref, bf16[4,64,256]{2,1,0:T(8,128)(2,1)S(1)} %select_bitcast_fusion.u_ref, f32[4,8,256]{2,1,0:T(8,128)S(1)} %stack.30.s_ref, ...), custom_call_target="tpu_custom_call" | custom-call | flops 2818572288 | bytes 4194304 | tf_op jit(solution)/shard_map/grads/pallas_call | solution.py:190
  151.4 11.6 %all-to-all-start.1 = ((bf16[64,128,128]{2,1,0:T(8,128)(2,1)}), bf16[64,128,128]{2,1,0:T(8,128)(2,1)S(1)}, u32[]{:S(2)}, u32[]{:S(2)}) async-start(bf16[64,128,128]{2,1,0:T(8,128)(2,1)} %bitcast.61), calls=%async_computation.1 | async-start | bytes 4194304 | tf_op jit(solution)/shard_map/all_to_all | solution.py:327
  165.0 5.4 %collective-permute-start.16 = (f32[64,256]{1,0:T(8,128)S(1)}, f32[64,256]{1,0:T(8,128)S(1)}, u32[]{:S(2)}, u32[]{:S(2)}) collective-permute-start(f32[64,256]{1,0:T(8,128)S(1)} %get-tuple-element.18), channel_id=1, source_target_pairs={{0,2},{1,3},{2,0},{3,1},{4,6},{5,7},{6,4},{7,5},{8,10},{9,11},{10,... | collective-permute-start | bytes 196616 | tf_op jit(solution)/shard_map/ppermute | solution.py:248
  172.4 3.4 %collective-permute-done.17 = f32[64,256]{1,0:T(8,128)S(1)} collective-permute-done((f32[64,256]{1,0:T(8,128)S(1)}, f32[64,256]{1,0:T(8,128)S(1)}, u32[]{:S(2)}, u32[]{:S(2)}) %collective-permute-start.17) | collective-permute-done | bytes 65568 | tf_op jit(solution)/shard_map/ppermute | solution.py:248
  175.9 2.9 %collective-permute-start.18 = (f32[64,256]{1,0:T(8,128)S(1)}, f32[64,256]{1,0:T(8,128)S(1)}, u32[]{:S(2)}, u32[]{:S(2)}) collective-permute-start(f32[64,256]{1,0:T(8,128)S(1)} %convolution_bitcast_fusion), channel_id=1, source_target_pairs={{0,4},{4,0},{8,12},{12,8},{16,20},{20,16},{24,28},{28,24},{32,36},... | collective-permute-start | bytes 196616 | tf_op jit(solution)/shard_map/ppermute | solution.py:218
  178.8 4.0 %collective-permute-start.19 = (f32[64,256]{1,0:T(8,128)S(1)}, f32[64,256]{1,0:T(8,128)S(1)}, u32[]{:S(2)}, u32[]{:S(2)}) collective-permute-start(f32[64,256]{1,0:T(8,128)S(1)} %convolution_bitcast_fusion), channel_id=1, source_target_pairs={{0,8},{4,12},{8,0},{12,4},{16,24},{20,28},{24,16},{28,20},{32,40},... | collective-permute-start | bytes 196616 | tf_op jit(solution)/shard_map/ppermute | solution.py:218
  185.2 25.7 %collective-permute-done.18 = f32[64,256]{1,0:T(8,128)S(1)} collective-permute-done((f32[64,256]{1,0:T(8,128)S(1)}, f32[64,256]{1,0:T(8,128)S(1)}, u32[]{:S(2)}, u32[]{:S(2)}) %collective-permute-start.18) | collective-permute-done | bytes 65568 | tf_op jit(solution)/shard_map/ppermute | solution.py:218
  210.9 7.3 %collective-permute-done.20 = f32[64,256]{1,0:T(8,128)S(1)} collective-permute-done((f32[64,256]{1,0:T(8,128)S(1)}, f32[64,256]{1,0:T(8,128)S(1)}, u32[]{:S(2)}, u32[]{:S(2)}) %collective-permute-start.20) | collective-permute-done | bytes 65568 | tf_op jit(solution)/shard_map/ppermute | solution.py:218
  218.2 3.5 %collective-permute-start.21 = (f32[64,256]{1,0:T(8,128)S(1)}, f32[64,256]{1,0:T(8,128)S(1)}, u32[]{:S(2)}, u32[]{:S(2)}) collective-permute-start(f32[64,256]{1,0:T(8,128)S(1)} %add_add_fusion.4), channel_id=1, source_target_pairs={{0,16},{4,20},{8,24},{12,28},{16,0},{20,4},{24,8},{28,12},{32,48},... | collective-permute-start | bytes 196616 | tf_op jit(solution)/shard_map/ppermute | solution.py:218
  223.7 6.8 %collective-permute-start.23 = (f32[64,256]{1,0:T(8,128)S(1)}, f32[64,256]{1,0:T(8,128)S(1)}, u32[]{:S(2)}, u32[]{:S(2)}) collective-permute-start(f32[64,256]{1,0:T(8,128)S(1)} %add_add_fusion.4), channel_id=1, source_target_pairs={{0,48},{4,52},{8,56},{12,60},{16,32},{20,36},{24,40},{28,44},{32,1... | collective-permute-start | bytes 196616 | tf_op jit(solution)/shard_map/ppermute | solution.py:218
  230.6 3.0 %collective-permute-done.23 = f32[64,256]{1,0:T(8,128)S(1)} collective-permute-done((f32[64,256]{1,0:T(8,128)S(1)}, f32[64,256]{1,0:T(8,128)S(1)}, u32[]{:S(2)}, u32[]{:S(2)}) %collective-permute-start.23) | collective-permute-done | bytes 65568 | tf_op jit(solution)/shard_map/ppermute | solution.py:218
  233.6 4.7 %collective-permute-start.24 = (f32[64,256]{1,0:T(8,128)S(1)}, f32[64,256]{1,0:T(8,128)S(1)}, u32[]{:S(2)}, u32[]{:S(2)}) collective-permute-start(f32[64,256]{1,0:T(8,128)S(1)} %add_add_fusion.3), channel_id=1, source_target_pairs={{0,64},{4,68},{8,72},{12,76},{16,80},{20,84},{24,88},{28,92},{32,9... | collective-permute-start | bytes 196616 | tf_op jit(solution)/shard_map/ppermute | solution.py:218
  238.3 5.7 %collective-permute-start.25 = (f32[64,256]{1,0:T(8,128)S(1)}, f32[64,256]{1,0:T(8,128)S(1)}, u32[]{:S(2)}, u32[]{:S(2)}) collective-permute-start(f32[64,256]{1,0:T(8,128)S(1)} %add_add_fusion.3), channel_id=1, source_target_pairs={{0,128},{4,132},{8,136},{12,140},{16,144},{20,148},{24,152},{28,15... | collective-permute-start | bytes 196616 | tf_op jit(solution)/shard_map/ppermute | solution.py:218
  247.5 4.2 %collective-permute-done.26 = f32[64,256]{1,0:T(8,128)S(1)} collective-permute-done((f32[64,256]{1,0:T(8,128)S(1)}, f32[64,256]{1,0:T(8,128)S(1)}, u32[]{:S(2)}, u32[]{:S(2)}) %collective-permute-start.26) | collective-permute-done | bytes 65568 | tf_op jit(solution)/shard_map/ppermute | solution.py:218
  253.9 5.2 %collective-permute-start.28 = (f32[64,128]{1,0:T(8,128)S(1)}, f32[64,128]{1,0:T(8,128)S(1)}, u32[]{:S(2)}, u32[]{:S(2)}) collective-permute-start(f32[64,128]{1,0:T(8,128)S(1)} %pad_maximum_fusion.1), channel_id=1, source_target_pairs={{0,2},{1,3},{2,0},{3,1},{4,6},{5,7},{6,4},{7,5},{8,10},{9,11},{10,... | collective-permute-start | bytes 98312 | tf_op jit(solution)/shard_map/ppermute | solution.py:218
  261.6 3.6 %collective-permute-done.29 = f32[64,128]{1,0:T(8,128)S(1)} collective-permute-done((f32[64,128]{1,0:T(8,128)S(1)}, f32[64,128]{1,0:T(8,128)S(1)}, u32[]{:S(2)}, u32[]{:S(2)}) %collective-permute-start.29) | collective-permute-done | bytes 32800 | tf_op jit(solution)/shard_map/ppermute | solution.py:218
  265.2 7.4 %collective-permute-start.30 = (f32[64,128]{1,0:T(8,128)S(1)}, f32[64,128]{1,0:T(8,128)S(1)}, u32[]{:S(2)}, u32[]{:S(2)}) collective-permute-start(f32[64,128]{1,0:T(8,128)S(1)} %add_add_fusion.5), channel_id=1, source_target_pairs={{0,256},{256,0},{1,257},{257,1},{2,258},{258,2},{3,259},{259,3},{4... | collective-permute-start | bytes 98312 | tf_op jit(solution)/shard_map/ppermute | solution.py:218
  (102 shorter events, 51.6 us)
Async XLA Ops:
  5.5 121.7 %all-to-all-start = ((bf16[64,128,128]{2,1,0:T(8,128)(2,1)}), bf16[64,128,128]{2,1,0:T(8,128)(2,1)S(1)}, u32[]{:S(2)}, u32[]{:S(2)}) async-start(bf16[64,128,128]{2,1,0:T(8,128)(2,1)} %pack.1), calls=%async_computation | async-start | bytes 4194304 | tf_op jit(solution)/shard_map/all_to_all | solution.py:272
  24.2 46.8 %collective-permute-start = (f32[72,256]{1,0:T(8,128)S(1)}, f32[72,256]{1,0:T(8,128)S(1)}, u32[]{:S(2)}, u32[]{:S(2)}) collective-permute-start(f32[72,256]{1,0:T(8,128)S(1)} %select_maximum_fusion), channel_id=1, source_target_pairs={{0,4},{4,0},{8,12},{12,8},{16,20},{20,16},{24,28},{28,24},{32,36},... | collective-permute-start | bytes 221192 | tf_op jit(solution)/shard_map/ppermute | solution.py:218
  27.2 45.9 %collective-permute-start.1 = (f32[72,256]{1,0:T(8,128)S(1)}, f32[72,256]{1,0:T(8,128)S(1)}, u32[]{:S(2)}, u32[]{:S(2)}) collective-permute-start(f32[72,256]{1,0:T(8,128)S(1)} %select_maximum_fusion), channel_id=1, source_target_pairs={{0,8},{4,12},{8,0},{12,4},{16,24},{20,28},{24,16},{28,20},{32,40},... | collective-permute-start | bytes 221192 | tf_op jit(solution)/shard_map/ppermute | solution.py:218
  31.2 44.8 %collective-permute-start.2 = (f32[72,256]{1,0:T(8,128)S(1)}, f32[72,256]{1,0:T(8,128)S(1)}, u32[]{:S(2)}, u32[]{:S(2)}) collective-permute-start(f32[72,256]{1,0:T(8,128)S(1)} %select_maximum_fusion), channel_id=1, source_target_pairs={{0,12},{4,8},{8,4},{12,0},{16,28},{20,24},{24,20},{28,16},{32,44},... | collective-permute-start | bytes 221192 | tf_op jit(solution)/shard_map/ppermute | solution.py:218
  76.0 13.9 %collective-permute-start.3 = (f32[72,256]{1,0:T(8,128)S(1)}, f32[72,256]{1,0:T(8,128)S(1)}, u32[]{:S(2)}, u32[]{:S(2)}) collective-permute-start(f32[72,256]{1,0:T(8,128)S(1)} %add_add_fusion.2), channel_id=1, source_target_pairs={{0,16},{4,20},{8,24},{12,28},{16,0},{20,4},{24,8},{28,12},{32,48},... | collective-permute-start | bytes 221192 | tf_op jit(solution)/shard_map/ppermute | solution.py:218
  81.8 8.1 %collective-permute-start.4 = (f32[72,256]{1,0:T(8,128)S(1)}, f32[72,256]{1,0:T(8,128)S(1)}, u32[]{:S(2)}, u32[]{:S(2)}) collective-permute-start(f32[72,256]{1,0:T(8,128)S(1)} %add_add_fusion.2), channel_id=1, source_target_pairs={{0,32},{4,36},{8,40},{12,44},{16,48},{20,52},{24,56},{28,60},{32,0... | collective-permute-start | bytes 221192 | tf_op jit(solution)/shard_map/ppermute | solution.py:218
  85.6 10.0 %collective-permute-start.5 = (f32[72,256]{1,0:T(8,128)S(1)}, f32[72,256]{1,0:T(8,128)S(1)}, u32[]{:S(2)}, u32[]{:S(2)}) collective-permute-start(f32[72,256]{1,0:T(8,128)S(1)} %add_add_fusion.2), channel_id=1, source_target_pairs={{0,48},{4,52},{8,56},{12,60},{16,32},{20,36},{24,40},{28,44},{32,1... | collective-permute-start | bytes 221192 | tf_op jit(solution)/shard_map/ppermute | solution.py:218
  95.6 12.9 %collective-permute-start.6 = (f32[72,256]{1,0:T(8,128)S(1)}, f32[72,256]{1,0:T(8,128)S(1)}, u32[]{:S(2)}, u32[]{:S(2)}) collective-permute-start(f32[72,256]{1,0:T(8,128)S(1)} %add_add_fusion.1), channel_id=1, source_target_pairs={{0,64},{4,68},{8,72},{12,76},{16,80},{20,84},{24,88},{28,92},{32,9... | collective-permute-start | bytes 221192 | tf_op jit(solution)/shard_map/ppermute | solution.py:218
  101.4 9.0 %collective-permute-start.7 = (f32[72,256]{1,0:T(8,128)S(1)}, f32[72,256]{1,0:T(8,128)S(1)}, u32[]{:S(2)}, u32[]{:S(2)}) collective-permute-start(f32[72,256]{1,0:T(8,128)S(1)} %add_add_fusion.1), channel_id=1, source_target_pairs={{0,128},{4,132},{8,136},{12,140},{16,144},{20,148},{24,152},{28,15... | collective-permute-start | bytes 221192 | tf_op jit(solution)/shard_map/ppermute | solution.py:218
  104.5 7.9 %collective-permute-start.8 = (f32[72,256]{1,0:T(8,128)S(1)}, f32[72,256]{1,0:T(8,128)S(1)}, u32[]{:S(2)}, u32[]{:S(2)}) collective-permute-start(f32[72,256]{1,0:T(8,128)S(1)} %add_add_fusion.1), channel_id=1, source_target_pairs={{0,192},{4,196},{8,200},{12,204},{16,208},{20,212},{24,216},{28,22... | collective-permute-start | bytes 221192 | tf_op jit(solution)/shard_map/ppermute | solution.py:218
  112.5 10.3 %collective-permute-start.10 = (bf16[64,256]{1,0:T(8,128)(2,1)S(1)}, bf16[64,256]{1,0:T(8,128)(2,1)S(1)}, u32[]{:S(2)}, u32[]{:S(2)}) collective-permute-start(bf16[64,256]{1,0:T(8,128)(2,1)S(1)} %slice.157), channel_id=1, source_target_pairs={{0,2},{1,3},{2,0},{3,1},{4,6},{5,7},{6,4},{7,5},{8,10},{9,11},{10,... | collective-permute-start | bytes 98312 | tf_op jit(solution)/shard_map/ppermute | solution.py:237
  117.1 5.6 %collective-permute-start.11 = (bf16[64,256]{1,0:T(8,128)(2,1)S(1)}, bf16[64,256]{1,0:T(8,128)(2,1)S(1)}, u32[]{:S(2)}, u32[]{:S(2)}) collective-permute-start(bf16[64,256]{1,0:T(8,128)(2,1)S(1)} %slice.157), channel_id=1, source_target_pairs={{0,3},{1,0},{2,1},{3,2},{4,7},{5,4},{6,5},{7,6},{8,11},{9,8},{10,9... | collective-permute-start | bytes 98312 | tf_op jit(solution)/shard_map/ppermute | solution.py:237
  119.9 5.9 %collective-permute-start.9 = (bf16[64,256]{1,0:T(8,128)(2,1)S(1)}, bf16[64,256]{1,0:T(8,128)(2,1)S(1)}, u32[]{:S(2)}, u32[]{:S(2)}) collective-permute-start(bf16[64,256]{1,0:T(8,128)(2,1)S(1)} %slice.157), channel_id=1, source_target_pairs={{0,1},{1,2},{2,3},{3,0},{4,5},{5,6},{6,7},{7,4},{8,9},{9,10},{10,1... | collective-permute-start | bytes 98312 | tf_op jit(solution)/shard_map/ppermute | solution.py:237
  130.9 9.6 %collective-permute-start.12 = (f32[4,8,256]{2,1,0:T(8,128)S(1)}, f32[4,8,256]{2,1,0:T(8,128)S(1)}, u32[]{:S(2)}, u32[]{:S(2)}) collective-permute-start(f32[4,8,256]{2,1,0:T(8,128)S(1)} %stats.1), channel_id=1, source_target_pairs={{0,1},{1,0},{2,3},{3,2},{4,5},{5,4},{6,7},{7,6},{8,9},{9,8},{10,11... | collective-permute-start | bytes 98312 | tf_op jit(solution)/shard_map/ppermute | solution.py:313
  132.8 7.7 %collective-permute-start.13 = (f32[4,8,256]{2,1,0:T(8,128)S(1)}, f32[4,8,256]{2,1,0:T(8,128)S(1)}, u32[]{:S(2)}, u32[]{:S(2)}) collective-permute-start(f32[4,8,256]{2,1,0:T(8,128)S(1)} %stats.1), channel_id=1, source_target_pairs={{0,2},{1,3},{2,0},{3,1},{4,6},{5,7},{6,4},{7,5},{8,10},{9,11},{10,... | collective-permute-start | bytes 98312 | tf_op jit(solution)/shard_map/ppermute | solution.py:313
  135.6 6.2 %collective-permute-start.14 = (f32[4,8,256]{2,1,0:T(8,128)S(1)}, f32[4,8,256]{2,1,0:T(8,128)S(1)}, u32[]{:S(2)}, u32[]{:S(2)}) collective-permute-start(f32[4,8,256]{2,1,0:T(8,128)S(1)} %stats.1), channel_id=1, source_target_pairs={{0,3},{1,2},{2,1},{3,0},{4,7},{5,6},{6,5},{7,4},{8,11},{9,10},{10,... | collective-permute-start | bytes 98312 | tf_op jit(solution)/shard_map/ppermute | solution.py:313
  151.4 122.7 %all-to-all-start.1 = ((bf16[64,128,128]{2,1,0:T(8,128)(2,1)}), bf16[64,128,128]{2,1,0:T(8,128)(2,1)S(1)}, u32[]{:S(2)}, u32[]{:S(2)}) async-start(bf16[64,128,128]{2,1,0:T(8,128)(2,1)} %bitcast.61), calls=%async_computation.1 | async-start | bytes 4194304 | tf_op jit(solution)/shard_map/all_to_all | solution.py:327
  163.1 9.3 %collective-permute-start.15 = (f32[64,256]{1,0:T(8,128)S(1)}, f32[64,256]{1,0:T(8,128)S(1)}, u32[]{:S(2)}, u32[]{:S(2)}) collective-permute-start(f32[64,256]{1,0:T(8,128)S(1)} %get-tuple-element.16), channel_id=1, source_target_pairs={{0,1},{1,2},{2,3},{3,0},{4,5},{5,6},{6,7},{7,4},{8,9},{9,10},{10,1... | collective-permute-start | bytes 196616 | tf_op jit(solution)/shard_map/ppermute | solution.py:248
  165.0 7.4 %collective-permute-start.16 = (f32[64,256]{1,0:T(8,128)S(1)}, f32[64,256]{1,0:T(8,128)S(1)}, u32[]{:S(2)}, u32[]{:S(2)}) collective-permute-start(f32[64,256]{1,0:T(8,128)S(1)} %get-tuple-element.18), channel_id=1, source_target_pairs={{0,2},{1,3},{2,0},{3,1},{4,6},{5,7},{6,4},{7,5},{8,10},{9,11},{10,... | collective-permute-start | bytes 196616 | tf_op jit(solution)/shard_map/ppermute | solution.py:248
  175.9 35.0 %collective-permute-start.18 = (f32[64,256]{1,0:T(8,128)S(1)}, f32[64,256]{1,0:T(8,128)S(1)}, u32[]{:S(2)}, u32[]{:S(2)}) collective-permute-start(f32[64,256]{1,0:T(8,128)S(1)} %convolution_bitcast_fusion), channel_id=1, source_target_pairs={{0,4},{4,0},{8,12},{12,8},{16,20},{20,16},{24,28},{28,24},{32,36},... | collective-permute-start | bytes 196616 | tf_op jit(solution)/shard_map/ppermute | solution.py:218
  178.8 32.1 %collective-permute-start.19 = (f32[64,256]{1,0:T(8,128)S(1)}, f32[64,256]{1,0:T(8,128)S(1)}, u32[]{:S(2)}, u32[]{:S(2)}) collective-permute-start(f32[64,256]{1,0:T(8,128)S(1)} %convolution_bitcast_fusion), channel_id=1, source_target_pairs={{0,8},{4,12},{8,0},{12,4},{16,24},{20,28},{24,16},{28,20},{32,40},... | collective-permute-start | bytes 196616 | tf_op jit(solution)/shard_map/ppermute | solution.py:218
  182.8 35.4 %collective-permute-start.20 = (f32[64,256]{1,0:T(8,128)S(1)}, f32[64,256]{1,0:T(8,128)S(1)}, u32[]{:S(2)}, u32[]{:S(2)}) collective-permute-start(f32[64,256]{1,0:T(8,128)S(1)} %convolution_bitcast_fusion), channel_id=1, source_target_pairs={{0,12},{4,8},{8,4},{12,0},{16,28},{20,24},{24,20},{28,16},{32,44},... | collective-permute-start | bytes 196616 | tf_op jit(solution)/shard_map/ppermute | solution.py:218
  218.2 12.3 %collective-permute-start.21 = (f32[64,256]{1,0:T(8,128)S(1)}, f32[64,256]{1,0:T(8,128)S(1)}, u32[]{:S(2)}, u32[]{:S(2)}) collective-permute-start(f32[64,256]{1,0:T(8,128)S(1)} %add_add_fusion.4), channel_id=1, source_target_pairs={{0,16},{4,20},{8,24},{12,28},{16,0},{20,4},{24,8},{28,12},{32,48},... | collective-permute-start | bytes 196616 | tf_op jit(solution)/shard_map/ppermute | solution.py:218
  221.8 8.8 %collective-permute-start.22 = (f32[64,256]{1,0:T(8,128)S(1)}, f32[64,256]{1,0:T(8,128)S(1)}, u32[]{:S(2)}, u32[]{:S(2)}) collective-permute-start(f32[64,256]{1,0:T(8,128)S(1)} %add_add_fusion.4), channel_id=1, source_target_pairs={{0,32},{4,36},{8,40},{12,44},{16,48},{20,52},{24,56},{28,60},{32,0... | collective-permute-start | bytes 196616 | tf_op jit(solution)/shard_map/ppermute | solution.py:218
  223.7 9.8 %collective-permute-start.23 = (f32[64,256]{1,0:T(8,128)S(1)}, f32[64,256]{1,0:T(8,128)S(1)}, u32[]{:S(2)}, u32[]{:S(2)}) collective-permute-start(f32[64,256]{1,0:T(8,128)S(1)} %add_add_fusion.4), channel_id=1, source_target_pairs={{0,48},{4,52},{8,56},{12,60},{16,32},{20,36},{24,40},{28,44},{32,1... | collective-permute-start | bytes 196616 | tf_op jit(solution)/shard_map/ppermute | solution.py:218
  233.6 12.5 %collective-permute-start.24 = (f32[64,256]{1,0:T(8,128)S(1)}, f32[64,256]{1,0:T(8,128)S(1)}, u32[]{:S(2)}, u32[]{:S(2)}) collective-permute-start(f32[64,256]{1,0:T(8,128)S(1)} %add_add_fusion.3), channel_id=1, source_target_pairs={{0,64},{4,68},{8,72},{12,76},{16,80},{20,84},{24,88},{28,92},{32,9... | collective-permute-start | bytes 196616 | tf_op jit(solution)/shard_map/ppermute | solution.py:218
  238.3 9.3 %collective-permute-start.25 = (f32[64,256]{1,0:T(8,128)S(1)}, f32[64,256]{1,0:T(8,128)S(1)}, u32[]{:S(2)}, u32[]{:S(2)}) collective-permute-start(f32[64,256]{1,0:T(8,128)S(1)} %add_add_fusion.3), channel_id=1, source_target_pairs={{0,128},{4,132},{8,136},{12,140},{16,144},{20,148},{24,152},{28,15... | collective-permute-start | bytes 196616 | tf_op jit(solution)/shard_map/ppermute | solution.py:218
  244.0 7.8 %collective-permute-start.26 = (f32[64,256]{1,0:T(8,128)S(1)}, f32[64,256]{1,0:T(8,128)S(1)}, u32[]{:S(2)}, u32[]{:S(2)}) collective-permute-start(f32[64,256]{1,0:T(8,128)S(1)} %add_add_fusion.3), channel_id=1, source_target_pairs={{0,192},{4,196},{8,200},{12,204},{16,208},{20,212},{24,216},{28,22... | collective-permute-start | bytes 196616 | tf_op jit(solution)/shard_map/ppermute | solution.py:218
  252.0 9.6 %collective-permute-start.27 = (f32[64,128]{1,0:T(8,128)S(1)}, f32[64,128]{1,0:T(8,128)S(1)}, u32[]{:S(2)}, u32[]{:S(2)}) collective-permute-start(f32[64,128]{1,0:T(8,128)S(1)} %pad_maximum_fusion.1), channel_id=1, source_target_pairs={{0,1},{1,0},{2,3},{3,2},{4,5},{5,4},{6,7},{7,6},{8,9},{9,8},{10,11... | collective-permute-start | bytes 98312 | tf_op jit(solution)/shard_map/ppermute | solution.py:218
  253.9 7.7 %collective-permute-start.28 = (f32[64,128]{1,0:T(8,128)S(1)}, f32[64,128]{1,0:T(8,128)S(1)}, u32[]{:S(2)}, u32[]{:S(2)}) collective-permute-start(f32[64,128]{1,0:T(8,128)S(1)} %pad_maximum_fusion.1), channel_id=1, source_target_pairs={{0,2},{1,3},{2,0},{3,1},{4,6},{5,7},{6,4},{7,5},{8,10},{9,11},{10,... | collective-permute-start | bytes 98312 | tf_op jit(solution)/shard_map/ppermute | solution.py:218
  259.1 6.1 %collective-permute-start.29 = (f32[64,128]{1,0:T(8,128)S(1)}, f32[64,128]{1,0:T(8,128)S(1)}, u32[]{:S(2)}, u32[]{:S(2)}) collective-permute-start(f32[64,128]{1,0:T(8,128)S(1)} %pad_maximum_fusion.1), channel_id=1, source_target_pairs={{0,3},{1,2},{2,1},{3,0},{4,7},{5,6},{6,5},{7,4},{8,11},{9,10},{10,... | collective-permute-start | bytes 98312 | tf_op jit(solution)/shard_map/ppermute | solution.py:218
  265.2 8.2 %collective-permute-start.30 = (f32[64,128]{1,0:T(8,128)S(1)}, f32[64,128]{1,0:T(8,128)S(1)}, u32[]{:S(2)}, u32[]{:S(2)}) collective-permute-start(f32[64,128]{1,0:T(8,128)S(1)} %add_add_fusion.5), channel_id=1, source_target_pairs={{0,256},{256,0},{1,257},{257,1},{2,258},{258,2},{3,259},{259,3},{4... | collective-permute-start | bytes 98312 | tf_op jit(solution)/shard_map/ppermute | solution.py:218
  (11 other events, 332.4 us)

commit v2 on v1

v2 whole, which is shorter than its diff:
```python
import functools

import jax
import jax.numpy as jnp
from jax import lax
from jax.experimental import pallas as pl
from jax.experimental.pallas import tpu as pltpu
from jax.sharding import PartitionSpec as P

HEAD = 64
BF16 = jnp.bfloat16
F32 = jnp.float32
VMEM_LIMIT = 32 * 1024 * 1024


def pack_kernel(k_ref, v_ref, o_ref):
    slots, span, width = k_ref.shape
    for pair in range(width // (2 * HEAD)):
        low = pair * 2 * HEAD
        for slot in range(slots):
            rows = pl.ds(slot * span, span)
            k = k_ref[slot, :, low : low + 2 * HEAD]
            v = v_ref[slot, :, low : low + 2 * HEAD]
            o_ref[2 * pair, rows, :] = jnp.concatenate([k[:, :HEAD], v[:, :HEAD]], axis=1)
            o_ref[2 * pair + 1, rows, :] = jnp.concatenate([k[:, HEAD:], v[:, HEAD:]], axis=1)


def unpack_kernel(i_ref, k_ref, v_ref):
    slots, span, width = k_ref.shape
    for pair in range(width // (2 * HEAD)):
        low = pair * 2 * HEAD
        for slot in range(slots):
            rows = pl.ds(slot * span, span)
            even = i_ref[2 * pair, rows, :]
            odd = i_ref[2 * pair + 1, rows, :]
            k_ref[slot, :, low : low + 2 * HEAD] = jnp.concatenate([even[:, :HEAD], odd[:, :HEAD]], axis=1)
            v_ref[slot, :, low : low + 2 * HEAD] = jnp.concatenate([even[:, HEAD:], odd[:, HEAD:]], axis=1)


PACK_HEADS = 16


def pack(keys, values, spare):
    slots, span, width = keys.shape
    heads, rows = width // HEAD, slots * span + spare
    part = pl.BlockSpec((slots, span, PACK_HEADS * HEAD), lambda i: (0, 0, i))
    return pl.pallas_call(
        pack_kernel,
        grid=(heads // PACK_HEADS,),
        in_specs=[part, part],
        out_specs=pl.BlockSpec((PACK_HEADS, rows, 2 * HEAD), lambda i: (i, 0, 0)),
        out_shape=jax.ShapeDtypeStruct((heads, rows, 2 * HEAD), keys.dtype),
        compiler_params=pltpu.CompilerParams(vmem_limit_bytes=VMEM_LIMIT),
        cost_estimate=pl.CostEstimate(flops=0, bytes_accessed=8 * slots * span * width, transcendentals=0),
        name="pack",
    )(keys, values)


def unpack(table, slots, span):
    heads, rows, _ = table.shape
    part = pl.BlockSpec((slots, span, PACK_HEADS * HEAD), lambda i: (0, 0, i))
    shape = jax.ShapeDtypeStruct((slots, span, heads * HEAD), table.dtype)
    return pl.pallas_call(
        unpack_kernel,
        grid=(heads // PACK_HEADS,),
        in_specs=[pl.BlockSpec((PACK_HEADS, rows, 2 * HEAD), lambda i: (i, 0, 0))],
        out_specs=[part, part],
        out_shape=[shape, shape],
        compiler_params=pltpu.CompilerParams(vmem_limit_bytes=VMEM_LIMIT),
        cost_estimate=pl.CostEstimate(flops=0, bytes_accessed=8 * slots * span * heads * HEAD, transcendentals=0),
        name="unpack",
    )(table)


CHUNK_SLOTS = 4


def two_sided(q_ref, u_ref):
    q, u = q_ref[0], u_ref[0]
    zero = jnp.zeros_like(q)
    return jnp.concatenate(
        [jnp.concatenate([q, zero], axis=1), jnp.concatenate([zero, u], axis=1)], axis=0
    )


def slot_rows(chosen_ref, slots, span, entry):
    slot = chosen_ref[entry]
    return slot // slots, pl.ds(pl.multiple_of(lax.rem(slot, slots) * span, span), span)


def gathered(chosen_ref, t_ref, slots, span, first):
    blocks = []
    for i in range(CHUNK_SLOTS):
        device, rows = slot_rows(chosen_ref, slots, span, first + i)
        blocks.append(t_ref[device, rows, :])
    return jnp.concatenate(blocks, axis=0)


def stats_kernel(per_question, slots, span, chosen_ref, q_ref, u_ref, t_ref, o_ref):
    question = pl.program_id(0)
    targets = q_ref.shape[2]
    both = two_sided(q_ref, u_ref)
    top = jnp.full((1, targets), -jnp.inf, F32)
    mass = jnp.zeros((1, targets), F32)
    dot = jnp.zeros((1, targets), F32)
    for chunk in range(per_question // CHUNK_SLOTS):
        first = question * per_question + chunk * CHUNK_SLOTS
        rows = gathered(chosen_ref, t_ref, slots, span, first)
        prod = jnp.dot(rows, both, preferred_element_type=F32)
        scores, prob_grad = prod[:, :targets], prod[:, targets:]
        new_top = jnp.maximum(top, jnp.max(scores, axis=0, keepdims=True))
        scale = jnp.exp(top - new_top)
        exp_scores = jnp.exp(scores - new_top)
        mass = mass * scale + jnp.sum(exp_scores, axis=0, keepdims=True)
        dot = dot * scale + jnp.sum(exp_scores * prob_grad, axis=0, keepdims=True)
        top = new_top
    o_ref[0] = jnp.concatenate([top, mass, dot, jnp.zeros((5, targets), F32)], axis=0)


def row_stats(s_ref):
    members = s_ref.shape[0]
    tops = [s_ref[i, 0, 0:1, :] for i in range(members)]
    top = functools.reduce(jnp.maximum, tops)
    scales = [jnp.exp(t - top) for t in tops]
    inverse = 1.0 / sum(s_ref[i, 0, 1:2, :] * scales[i] for i in range(members))
    delta = sum(s_ref[i, 0, 2:3, :] * scales[i] for i in range(members)) * inverse
    return top, inverse, delta


def grad_kernel(
    per_question, slots, span, chosen_ref, q_ref, u_ref, w_ref, s_ref, t_ref, dq_ref, l_ref, o_ref
):
    question = pl.program_id(0)
    targets = q_ref.shape[2]
    peers, _, pair_width = dq_ref.shape
    piece = targets // peers

    @pl.when(question == 0)
    def _():
        o_ref[...] = jnp.zeros_like(o_ref)

    both = two_sided(q_ref, u_ref)
    top, inverse, delta = row_stats(s_ref)
    dq = jnp.zeros((2 * HEAD, targets), F32)
    for chunk in range(per_question // CHUNK_SLOTS):
        first = question * per_question + chunk * CHUNK_SLOTS
        rows = gathered(chosen_ref, t_ref, slots, span, first)
        prod = jnp.dot(rows, both, preferred_element_type=F32)
        scores, prob_grad = prod[:, :targets], prod[:, targets:]
        weights = jnp.exp(scores - top) * inverse
        score_grad = (weights * (prob_grad - delta)).astype(BF16)
        pair = jnp.concatenate([score_grad, weights.astype(BF16)], axis=1)
        out = lax.dot_general(
            pair, both, (((1,), (1,)), ((), ())), preferred_element_type=F32
        ).astype(BF16)
        for i in range(CHUNK_SLOTS):
            device, place = slot_rows(chosen_ref, slots, span, first + i)
            o_ref[device, place, :] = out[i * span : (i + 1) * span]
        dq = dq + lax.dot_general(
            rows, score_grad, (((0,), (0,)), ((), ())), preferred_element_type=F32
        )
    dq = dq[:HEAD]

    for side in range(pair_width // piece):

        @pl.when(question % (pair_width // piece) == side)
        def _():
            for peer in range(peers):
                dq_ref[peer, :, side * piece : (side + 1) * piece] = dq[
                    :, peer * piece : (peer + 1) * piece
                ]

    high = dq.astype(BF16)
    low = (dq - high.astype(F32)).astype(BF16)
    latent = jnp.dot(w_ref[...], high, preferred_element_type=F32) + jnp.dot(
        w_ref[...], low, preferred_element_type=F32
    )
    lanes = l_ref.shape[2]
    for part in range(targets // lanes):
        row = question * (targets // lanes) + part
        l_ref[:, pl.ds(row, 1), :] = latent[:, None, part * lanes : (part + 1) * lanes]


def attend_stats(chosen, query_t, upstream_t, table, per_question, slots, span):
    questions, size, targets = query_t.shape
    one = pl.BlockSpec((1, size, targets), lambda q, c: (q, 0, 0))
    whole = pl.BlockSpec(table.shape, lambda q, c: (0, 0, 0))
    keys = per_question * span
    return pl.pallas_call(
        functools.partial(stats_kernel, per_question, slots, span),
        grid_spec=pltpu.PrefetchScalarGridSpec(
            num_scalar_prefetch=1,
            grid=(questions,),
            in_specs=[one, one, whole],
            out_specs=pl.BlockSpec((1, 8, targets), lambda q, c: (q, 0, 0)),
        ),
        out_shape=jax.ShapeDtypeStruct((questions, 8, targets), F32),
        compiler_params=pltpu.CompilerParams(vmem_limit_bytes=VMEM_LIMIT),
        cost_estimate=pl.CostEstimate(
            flops=8 * questions * targets * keys * HEAD,
            bytes_accessed=2 * table.size,
            transcendentals=questions * targets * keys,
        ),
        name="stats",
    )(chosen, query_t, upstream_t, table)


def attend_grads(chosen, query_t, upstream_t, up_weight, stats, table, per_question, slots, span):
    questions, size, targets = query_t.shape
    peers = stats.shape[0]
    one = pl.BlockSpec((1, size, targets), lambda q, c: (q, 0, 0))
    whole = pl.BlockSpec(table.shape, lambda q, c: (0, 0, 0))
    keys = per_question * span
    piece = targets // peers
    in_block = 128 // piece
    latent_shape = (up_weight.shape[0], questions * targets // 128, 128)
    return pl.pallas_call(
        functools.partial(grad_kernel, per_question, slots, span),
        grid_spec=pltpu.PrefetchScalarGridSpec(
            num_scalar_prefetch=1,
            grid=(questions,),
            in_specs=[
                one,
                one,
                pl.BlockSpec(up_weight.shape, lambda q, c: (0, 0)),
                pl.BlockSpec((peers, 1, 8, targets), lambda q, c: (0, q, 0, 0)),
                whole,
            ],
            out_specs=[
                pl.BlockSpec((peers, HEAD, 128), lambda q, c: (0, 0, q // in_block)),
                pl.BlockSpec(latent_shape, lambda q, c: (0, 0, 0)),
                whole,
            ],
        ),
        out_shape=[
            jax.ShapeDtypeStruct((peers, HEAD, questions * piece), F32),
            jax.ShapeDtypeStruct(latent_shape, F32),
            jax.ShapeDtypeStruct(table.shape, BF16),
        ],
        compiler_params=pltpu.CompilerParams(vmem_limit_bytes=VMEM_LIMIT),
        cost_estimate=pl.CostEstimate(
            flops=24 * questions * targets * keys * HEAD,
            bytes_accessed=4 * table.size,
            transcendentals=questions * targets * keys,
        ),
        name="grads",
    )(chosen, query_t, upstream_t, up_weight, stats, table)


def swap_sum(x, axis, shift, radix):
    size = lax.axis_size(axis)
    got = [x] + [
        lax.ppermute(x, axis, [(i, i ^ (k << shift)) for i in range(size)]) for k in range(1, radix)
    ]
    while len(got) > 1:
        got = [a + b for a, b in zip(got[0::2], got[1::2])]
    return got[0]


def to_all(x, axis):
    size = lax.axis_size(axis)
    return lax.all_to_all(
        jnp.broadcast_to(x[None], (size,) + x.shape), axis, split_axis=0, concat_axis=0, tiled=True
    )


def scatter_sum_tp(x):
    size, here = lax.axis_size("tp"), lax.axis_index("tp")
    own = lax.dynamic_index_in_dim(x, here, 0, keepdims=False)
    for k in range(1, size):
        sent = lax.dynamic_index_in_dim(x, (here + k) % size, 0, keepdims=False)
        own = own + lax.ppermute(sent, "tp", [(i, (i + k) % size) for i in range(size)])
    return own


def exchange(x, axis):
    return lax.all_to_all(x, axis, split_axis=0, concat_axis=0, tiled=True)


def local(
    keys,
    values,
    frozen_query_projection,
    context_gradient,
    hidden,
    adapter_down_weight,
    adapter_up_weight,
    owner,
    counts,
    target_length,
):
    group_count, token_split = lax.axis_size("grp"), lax.axis_size("tp")
    questions, targets, _ = frozen_query_projection.shape
    slots_dev, span, _ = keys.shape
    total_slots = group_count * slots_dev
    per_question = (total_slots - group_count // 4) // questions
    piece = targets // token_split
    table_rows = slots_dev * span
    positions = questions * targets
    row_shape = (positions // 128, 128)

    hidden_t = jnp.swapaxes(hidden, 1, 2)
    latent_part = jnp.einsum("dr,qdt->rqt", adapter_down_weight, hidden_t, preferred_element_type=F32)
    live = jnp.arange(slots_dev, dtype=jnp.int32) < counts[0]
    tag = jnp.where(live, owner, questions).astype(F32)
    tags = jnp.broadcast_to(jnp.pad(tag, (0, 128 - slots_dev))[None, None], (group_count, 1, 128))
    sent = jnp.concatenate([latent_part.reshape(group_count, 1, positions), tags], axis=2)
    got = exchange(sent, "grp")
    latent_row = jnp.sum(got[:, 0, :positions], axis=0).astype(BF16).reshape(row_shape)
    slot_key = got[:, 0, positions : positions + slots_dev].astype(jnp.int32).reshape(total_slots)

    packed = pack(keys, values, row_shape[0])
    packed = lax.dynamic_update_slice(
        packed, jnp.broadcast_to(latent_row[None], (group_count,) + row_shape), (0, table_rows, 0)
    )
    table = exchange(packed, "grp")

    slot_ids = jnp.arange(total_slots, dtype=jnp.int32)
    same = (slot_key[:, None] == slot_key[None, :]) & (slot_ids[None, :] < slot_ids[:, None])
    rank = jnp.sum(same.astype(jnp.int32), axis=1)
    place = slot_key * per_question + rank
    wanted = jnp.arange(questions * per_question, dtype=jnp.int32)
    hit = (place[None, :] == wanted[:, None]) & (slot_key < questions)[None, :]
    chosen = jnp.sum(jnp.where(hit, slot_ids[None, :], 0), axis=1)

    step_ids = lax.broadcasted_iota(jnp.int32, (questions, 1, targets), 2)
    keep = step_ids < target_length[:, None, None]
    upstream_t = jnp.swapaxes(context_gradient, 1, 2)
    upstream_t = jnp.where(keep, upstream_t, jnp.zeros_like(upstream_t))
    latent_t = table[:, table_rows:, :].reshape(group_count, questions, targets)
    raised = jnp.einsum("rd,rqt->qdt", adapter_up_weight, latent_t, preferred_element_type=F32)
    frozen_t = jnp.swapaxes(frozen_query_projection, 1, 2)
    query_t = (frozen_t.astype(F32) + raised).astype(BF16)

    stats = attend_stats(chosen, query_t, upstream_t, table, per_question, slots_dev, span)
    dq_parts, latent_grad_part, grad_table = attend_grads(
        chosen,
        query_t,
        upstream_t,
        adapter_up_weight,
        to_all(stats, "tp"),
        table,
        per_question,
        slots_dev,
        span,
    )
    latent_grad_row = jnp.sum(exchange(latent_grad_part, "grp"), axis=0)
    latent_grad_row = jnp.sum(to_all(latent_grad_row, "tp"), axis=0).astype(BF16)
    grad_table = lax.dynamic_update_slice(
        grad_table,
        jnp.broadcast_to(latent_grad_row[None], (group_count,) + row_shape),
        (0, table_rows, 0),
    )
    back = exchange(grad_table, "grp")
    grad_keys, grad_values = unpack(back, slots_dev, span)
    latent_grad = back[:, table_rows:, :].reshape(group_count, questions, targets)
    grad_a = jnp.einsum("qdt,rqt->dr", hidden_t, latent_grad, preferred_element_type=F32)
    grad_a = swap_sum(grad_a, "sect", 0, lax.axis_size("sect"))

    dq_t = scatter_sum_tp(dq_parts).astype(BF16).reshape(HEAD, questions, piece)
    adapted = jnp.transpose(dq_t, (1, 2, 0))
    start = lax.axis_index("tp") * piece
    latent_cut = lax.dynamic_slice_in_dim(latent_t, start, piece, 2)
    grad_b = jnp.einsum("rqt,dqt->rd", latent_cut, dq_t, preferred_element_type=F32)
    grad_b = swap_sum(swap_sum(grad_b, "tp", 0, token_split), "sect", 0, lax.axis_size("sect"))
    return (adapted, grad_keys, grad_values, grad_a, grad_b)


def solution(mesh):
    return jax.shard_map(
        local,
        mesh=mesh,
        in_specs=(
            P(("sect", "grp"), "tp", None),
            P(("sect", "grp"), "tp", None),
            P("sect", None, "grp"),
            P("sect", None, "grp"),
            P("sect", None, "grp"),
            P("grp", None),
            P(None, "grp"),
            P(("sect", "grp")),
            P(("sect", "grp")),
            P("sect"),
        ),
        out_specs=(
            P("sect", "tp", "grp"),
            P(("sect", "grp"), "tp", None),
            P(("sect", "grp"), "tp", None),
            P("grp", None),
            P(None, "grp"),
        ),
        check_vma=False,
    )
```

time: 278 us -> 222 us (0.80)
  starting transfers between devices: 145 us -> 62.9 us
  blocking collectives: 0 us -> 42.4 us
  waiting for transfers between devices: 105 us -> 81.4 us
  other arithmetic: 0.71 us -> 3.76 us
    ppermute x22 -> x5, waiting for transfers between devices: 97.4 us -> 1.58 us  [swap_sum(): lax.ppermute(x, axis, [(i, i ^ k << shift) for i in range(size)])]
    all_to_all x2 -> x3, waiting for transfers between devices: 0.01 us -> 75.2 us  [exchange(): return lax.all_to_all(x, axis, split_axis=0, concat_axis=0, tiled=True)]
    ppermute x22 -> x5, starting transfers between devices: 86.8 us -> 26.8 us  [swap_sum(): lax.ppermute(x, axis, [(i, i ^ k << shift) for i in range(size)])]
    all_to_all x0 -> x3, blocking collectives: none -> 42.4 us  [the longest x1 27.2 us: exchange(): return lax.all_to_all(x, axis, split_axis=0, concat_axis=0, tiled=True)]
    ppermute x6 -> x0, starting transfers between devices: 19.5 us -> none  [the longest x3 9.93 us: gather_tp(): lax.ppermute(x, 'tp', [(i, (i + k) % size) for i in range(size)])]
    ppermute x6 -> x0, waiting for transfers between devices: 4.27 us -> none  [the longest x3 2.99 us: gather_tp(): lax.ppermute(x, 'tp', [(i, (i + k) % size) for i in range(size)])]
    all_to_all x2 -> x3, starting transfers between devices: 28.9 us -> 28.3 us  [exchange(): return lax.all_to_all(x, axis, split_axis=0, concat_axis=0, tiled=True)]
  transfers between devices with their start and end apart: 33 -> 11, of which waited for: 16 -> 7; matrix products, arithmetic and copies ran while one was open for 2% -> 1% of each run, Pallas kernels for 0% -> 2%
where the time goes in v2:
time: 222 us; the launch traced here: 219 us
  waiting for transfers between devices  81.4 us (37%)
  starting transfers between devices  62.9 us (28%)
  blocking collectives  42.4 us (19%)
  Pallas kernels  17.4 us (8%)
  local copies, waits for them, and re-layouts  7.51 us (3%)
  other arithmetic  3.76 us (2%)
    all_to_all x3, waiting for transfers between devices, exchange(): return lax.all_to_all(x, axis, split_axis=0, concat_axis=0, tiled=True)  75.2 us
    all_to_all x3, starting transfers between devices, exchange(): return lax.all_to_all(x, axis, split_axis=0, concat_axis=0, tiled=True)  28.3 us
    all_to_all x1, blocking collectives, exchange(): return lax.all_to_all(x, axis, split_axis=0, concat_axis=0, tiled=True)  27.2 us
    ppermute x5, starting transfers between devices, swap_sum(): lax.ppermute(x, axis, [(i, i ^ k << shift) for i in range(size)])  26.8 us
    all_to_all x2, blocking collectives, to_all(): lax.all_to_all(jnp.broadcast_to(x[None], (size,) + x.shape), axis, split_...  15.2 us
    pallas_call x1, Pallas kernels, attend_grads(): pl.pallas_call(functools.partial(grad_kernel, per_question, slots, span),...  9.1 us
    ppermute x3, starting transfers between devices, scatter_sum_tp(): lax.ppermute(sent, 'tp', [(i, (i + k) % size) for i in range(size)])  7.81 us
    ppermute x3, waiting for transfers between devices, scatter_sum_tp(): lax.ppermute(sent, 'tp', [(i, (i + k) % size) for i in range(size)])  4.55 us
  transfers between devices with their start and end apart: 11, of which 7 were waited for; matrix products, arithmetic and copies ran while one was open for 1% of the time, Pallas kernels for 2%

profile of v2, /device:TPU:1, one launch (start us, length us, event | category | flops | bytes accessed | tf_op | source)
XLA Modules:
  0.0 218.6 jit_solution(3885600726973409200)
XLA Ops:
  0.7 0.9 copy-done
  1.5 0.9 fusion.3
  4.1 1.0 copy.41
  5.1 17.4 %all-to-all-start = ((f32[64,1,1152]{2,1,0:T(1,128)}), f32[64,1,1152]{2,1,0:T(1,128)}, u32[]{:S(2)}, u32[]{:S(2)}) async-start(f32[64,1,1152]{2,1,0:T(1,128)} %copy.41), calls=%async_computation | async-start | bytes 589824 | tf_op jit(solution)/shard_map/all_to_all | solution.py:277
  22.5 1.2 copy-done.3
  23.8 2.4 %pack.1 = bf16[64,136,128]{2,1,0:T(8,128)(2,1)} custom-call(bf16[2,64,4096]{2,1,0:T(8,128)(2,1)S(1)} %copy-done.2, bf16[2,64,4096]{2,1,0:T(8,128)(2,1)S(1)} %copy-done.3), custom_call_target="tpu_custom_call" | custom-call | bytes 4194304 | tf_op jit(solution)/shard_map/pack/pallas_call | solution.py:47
  26.2 9.4 %all-to-all-done = f32[64,1,1152]{2,1,0:T(1,128)} async-done(((f32[64,1,1152]{2,1,0:T(1,128)}), f32[64,1,1152]{2,1,0:T(1,128)}, u32[]{:S(2)}, u32[]{:S(2)}) %all-to-all-start) | async-done | bytes 294944 | tf_op jit(solution)/shard_map/all_to_all | solution.py:277
  35.6 1.1 slice_reduce_fusion
  37.4 6.2 %all-to-all-start.1 = ((bf16[64,136,128]{2,1,0:T(8,128)(2,1)}), bf16[64,136,128]{2,1,0:T(8,128)(2,1)S(1)}, u32[]{:S(2)}, u32[]{:S(2)}) async-start(bf16[64,136,128]{2,1,0:T(8,128)(2,1)} %broadcast_dynamic-update-slice_fusion.1), calls=%async_computation.1 | async-start | bytes 4456448 | tf_op jit(solution)/shard_map/all_to_all | solution.py:277
  43.7 0.9 fusion.12
  45.0 50.5 %all-to-all-done.1.t_ref = bf16[64,136,128]{2,1,0:T(8,128)(2,1)S(1)} async-done(((bf16[64,136,128]{2,1,0:T(8,128)(2,1)}), bf16[64,136,128]{2,1,0:T(8,128)(2,1)S(1)}, u32[]{:S(2)}, u32[]{:S(2)}) %all-to-all-start.1) | async-done | bytes 2228256 | tf_op jit(solution)/shard_map/all_to_all | solution.py:277
  95.9 3.7 %stats.1 = f32[4,8,256]{2,1,0:T(8,128)S(1)} custom-call(s32[112]{0:T(128)S(1)} %select_reduce_fusion.chosen_ref, bf16[4,64,256]{2,1,0:T(8,128)(2,1)S(1)} %fusion.1.q_ref, bf16[4,64,256]{2,1,0:T(8,128)(2,1)S(1)} %select_bitcast_fusion.u_ref, bf16[64,136,128]{2,1,0:T(8,128)(2,1)S(1)} %all-to-all-done.1.t_ref), custom_call_target="tpu_custom_call" | custom-call | flops 939524096 | bytes 2228224 | tf_op jit(solution)/shard_map/stats/pallas_call | solution.py:189
  99.6 8.6 %all_to_all.30.s_ref = f32[4,4,8,256]{3,2,1,0:T(8,128)S(1)} all-to-all(f32[4,4,8,256]{3,2,1,0:T(8,128)S(1)} %broadcast_in_dim.70), channel_id=1, replica_groups=mesh['sect'=2,'grp'=64,'tp'=4] {'tp'}, dimensions={0} | all-to-all | bytes 262144 | tf_op jit(solution)/shard_map/all_to_all | solution.py:262
  108.3 9.1 %grads.1 = (f32[4,64,256]{2,1,0:T(8,128)S(1)}, f32[64,8,128]{2,1,0:T(8,128)S(1)}, bf16[64,136,128]{2,1,0:T(8,128)(2,1)S(1)}) custom-call(s32[112]{0:T(128)S(1)} %select_reduce_fusion.chosen_ref, bf16[4,64,256]{2,1,0:T(8,128)(2,1)S(1)} %fusion.1.q_ref, bf16[4,64,256]{2,1,0:T(8,128)(2,1)S(1)} %select_bitcast_fusion.u_ref, bf16[64,64]{1,0:T(8,128)(2,1)S(1)} %copy-done.4, ...), custom_call_target="tpu_custom_call" | custom-call | flops 2818572288 | bytes 4456448 | tf_op jit(solution)/shard_map/grads/pallas_call | solution.py:217
  117.4 1.4 copy-done.1
  118.7 27.2 %all_to_all.31 = f32[64,8,128]{2,1,0:T(8,128)S(1)} all-to-all(f32[64,8,128]{2,1,0:T(8,128)S(1)} %get-tuple-element.12), channel_id=1, replica_groups=mesh['sect'=2,'grp'=64,'tp'=4] {'grp'}, dimensions={0} | all-to-all | bytes 524288 | tf_op jit(solution)/shard_map/all_to_all | solution.py:277
  146.0 6.6 %all_to_all.32 = f32[4,8,128]{2,1,0:T(8,128)S(1)} all-to-all(f32[4,8,128]{2,1,0:T(8,128)S(1)} %broadcast_in_dim.71), channel_id=1, replica_groups=mesh['sect'=2,'grp'=64,'tp'=4] {'tp'}, dimensions={0} | all-to-all | bytes 32768 | tf_op jit(solution)/shard_map/all_to_all | solution.py:262
  152.6 0.7 broadcast_dynamic-update-slice_fusion
  153.3 4.7 %all-to-all-start.5 = ((bf16[64,136,128]{2,1,0:T(8,128)(2,1)}), bf16[64,136,128]{2,1,0:T(8,128)(2,1)S(1)}, u32[]{:S(2)}, u32[]{:S(2)}) async-start(bf16[64,136,128]{2,1,0:T(8,128)(2,1)} %broadcast_dynamic-update-slice_fusion), calls=%async_computation.5 | async-start | bytes 4456448 | tf_op jit(solution)/shard_map/all_to_all | solution.py:277
  158.1 2.8 %collective-permute-start.2 = (f32[64,256]{1,0:T(8,128)S(1)}, f32[64,256]{1,0:T(8,128)S(1)}, u32[]{:S(2)}, u32[]{:S(2)}) collective-permute-start(f32[64,256]{1,0:T(8,128)S(1)} %get-tuple-element.36), channel_id=1, source_target_pairs={{0,3},{1,0},{2,1},{3,2},{4,7},{5,4},{6,5},{7,6},{8,11},{9,8},{10,9... | collective-permute-start | bytes 196616 | tf_op jit(solution)/shard_map/ppermute | solution.py:272
  160.9 3.1 %collective-permute-start.1 = (f32[64,256]{1,0:T(8,128)S(1)}, f32[64,256]{1,0:T(8,128)S(1)}, u32[]{:S(2)}, u32[]{:S(2)}) collective-permute-start(f32[64,256]{1,0:T(8,128)S(1)} %get-tuple-element.37), channel_id=1, source_target_pairs={{0,2},{1,3},{2,0},{3,1},{4,6},{5,7},{6,4},{7,5},{8,10},{9,11},{10,... | collective-permute-start | bytes 196616 | tf_op jit(solution)/shard_map/ppermute | solution.py:272
  164.0 1.9 collective-permute-start
  166.0 1.4 collective-permute-done.1
  167.4 3.1 %collective-permute-done = f32[64,256]{1,0:T(8,128)S(1)} collective-permute-done((f32[64,256]{1,0:T(8,128)S(1)}, f32[64,256]{1,0:T(8,128)S(1)}, u32[]{:S(2)}, u32[]{:S(2)}) %collective-permute-start) | collective-permute-done | bytes 65568 | tf_op jit(solution)/shard_map/ppermute | solution.py:272
  170.9 2.5 %collective-permute-start.5 = (f32[64,64]{1,0:T(8,128)S(1)}, f32[64,64]{1,0:T(8,128)S(1)}, u32[]{:S(2)}, u32[]{:S(2)}) collective-permute-start(f32[64,64]{1,0:T(8,128)S(1)} %convolution_bitcast_fusion), channel_id=1, source_target_pairs={{0,2},{1,3},{2,0},{3,1},{4,6},{5,7},{6,4},{7,5},{8,10},{9,11},{10,... | collective-permute-start | bytes 49160 | tf_op jit(solution)/shard_map/ppermute | solution.py:253
  173.4 2.5 %collective-permute-start.6 = (f32[64,64]{1,0:T(8,128)S(1)}, f32[64,64]{1,0:T(8,128)S(1)}, u32[]{:S(2)}, u32[]{:S(2)}) collective-permute-start(f32[64,64]{1,0:T(8,128)S(1)} %convolution_bitcast_fusion), channel_id=1, source_target_pairs={{0,3},{1,2},{2,1},{3,0},{4,7},{5,6},{6,5},{7,4},{8,11},{9,10},{10,... | collective-permute-start | bytes 49160 | tf_op jit(solution)/shard_map/ppermute | solution.py:253
  176.0 3.4 %collective-permute-start.4 = (f32[64,64]{1,0:T(8,128)S(1)}, f32[64,64]{1,0:T(8,128)S(1)}, u32[]{:S(2)}, u32[]{:S(2)}) collective-permute-start(f32[64,64]{1,0:T(8,128)S(1)} %convolution_bitcast_fusion), channel_id=1, source_target_pairs={{0,1},{1,0},{2,3},{3,2},{4,5},{5,4},{6,7},{7,6},{8,9},{9,8},{10,11... | collective-permute-start | bytes 49160 | tf_op jit(solution)/shard_map/ppermute | solution.py:253
  179.6 1.3 collective-permute-done.4
  180.9 10.5 %collective-permute-start.7 = (f32[64,64]{1,0:T(8,128)S(1)}, f32[64,64]{1,0:T(8,128)S(1)}, u32[]{:S(2)}, u32[]{:S(2)}) collective-permute-start(f32[64,64]{1,0:T(8,128)S(1)} %add_add_fusion), channel_id=1, source_target_pairs={{0,256},{256,0},{1,257},{257,1},{2,258},{258,2},{3,259},{259,3},{4... | collective-permute-start | bytes 49160 | tf_op jit(solution)/shard_map/ppermute | solution.py:253
  191.4 15.3 %all-to-all-done.5.i_ref = bf16[64,136,128]{2,1,0:T(8,128)(2,1)S(1)} async-done(((bf16[64,136,128]{2,1,0:T(8,128)(2,1)}), bf16[64,136,128]{2,1,0:T(8,128)(2,1)S(1)}, u32[]{:S(2)}, u32[]{:S(2)}) %all-to-all-start.5) | async-done | bytes 2228256 | tf_op jit(solution)/shard_map/all_to_all | solution.py:277
  207.0 7.9 %collective-permute-start.3 = (f32[64,64]{0,1:T(8,128)S(1)}, f32[64,64]{0,1:T(8,128)S(1)}, u32[]{:S(2)}, u32[]{:S(2)}) collective-permute-start(f32[64,64]{0,1:T(8,128)S(1)} %convolution_bitcast_fusion.1), channel_id=1, source_target_pairs={{0,256},{256,0},{1,257},{257,1},{2,258},{258,2},{3,259},{259,3},{4... | collective-permute-start | bytes 49160 | tf_op jit(solution)/shard_map/ppermute | solution.py:253
  215.6 2.2 %unpack.1 = (bf16[2,64,4096]{2,1,0:T(8,128)(2,1)}, bf16[2,64,4096]{2,1,0:T(8,128)(2,1)}) custom-call(bf16[64,136,128]{2,1,0:T(8,128)(2,1)S(1)} %all-to-all-done.5.i_ref), custom_call_target="tpu_custom_call" | custom-call | bytes 4194304 | tf_op jit(solution)/shard_map/unpack/pallas_call | solution.py:63
  (52 shorter events, 5.0 us)
Async XLA Ops:
  0.6 0.9 copy-start
  0.6 21.9 %copy-start.2 = (bf16[2,64,4096]{2,1,0:T(8,128)(2,1)S(1)}, bf16[2,64,4096]{2,1,0:T(8,128)(2,1)}, u32[]{:S(2)}) copy-start(bf16[2,64,4096]{2,1,0:T(8,128)(2,1)} %k_ref.1) | copy-start | bytes 3145732
  5.1 30.4 %all-to-all-start = ((f32[64,1,1152]{2,1,0:T(1,128)}), f32[64,1,1152]{2,1,0:T(1,128)}, u32[]{:S(2)}, u32[]{:S(2)}) async-start(f32[64,1,1152]{2,1,0:T(1,128)} %copy.41), calls=%async_computation | async-start | bytes 589824 | tf_op jit(solution)/shard_map/all_to_all | solution.py:277
  22.5 1.2 copy-start.3
  37.4 6.2 %copy-start.8 = (s32[4]{0:T(128)S(1)}, s32[4]{0:T(128)}, u32[]{:S(2)}) copy-start(s32[4]{0:T(128)} %param.19) | copy-start | bytes 52
  37.4 6.3 %copy-start.7 = (bf16[4,256,64]{1,2,0:T(8,128)(2,1)S(1)}, bf16[4,256,64]{1,2,0:T(8,128)(2,1)}, u32[]{:S(2)}) copy-start(bf16[4,256,64]{1,2,0:T(8,128)(2,1)} %param.13) | copy-start | bytes 393220
  37.4 58.3 %copy-start.4 = (bf16[64,64]{1,0:T(8,128)(2,1)S(1)}, bf16[64,64]{1,0:T(8,128)(2,1)}, u32[]{:S(2)}) copy-start(bf16[64,64]{1,0:T(8,128)(2,1)} %w_ref.1) | copy-start | bytes 24580
  37.4 58.3 %copy-start.6 = (bf16[4,256,64]{1,2,0:T(8,128)(2,1)S(1)}, bf16[4,256,64]{1,2,0:T(8,128)(2,1)}, u32[]{:S(2)}) copy-start(bf16[4,256,64]{1,2,0:T(8,128)(2,1)} %param.12) | copy-start | bytes 393220
  37.4 58.2 %all-to-all-start.1 = ((bf16[64,136,128]{2,1,0:T(8,128)(2,1)}), bf16[64,136,128]{2,1,0:T(8,128)(2,1)S(1)}, u32[]{:S(2)}, u32[]{:S(2)}) async-start(bf16[64,136,128]{2,1,0:T(8,128)(2,1)} %broadcast_dynamic-update-slice_fusion.1), calls=%async_computation.1 | async-start | bytes 4456448 | tf_op jit(solution)/shard_map/all_to_all | solution.py:277
  117.4 1.4 copy-start.1
  153.3 53.4 %all-to-all-start.5 = ((bf16[64,136,128]{2,1,0:T(8,128)(2,1)}), bf16[64,136,128]{2,1,0:T(8,128)(2,1)S(1)}, u32[]{:S(2)}, u32[]{:S(2)}) async-start(bf16[64,136,128]{2,1,0:T(8,128)(2,1)} %broadcast_dynamic-update-slice_fusion), calls=%async_computation.5 | async-start | bytes 4456448 | tf_op jit(solution)/shard_map/all_to_all | solution.py:277
  158.1 7.9 %collective-permute-start.2 = (f32[64,256]{1,0:T(8,128)S(1)}, f32[64,256]{1,0:T(8,128)S(1)}, u32[]{:S(2)}, u32[]{:S(2)}) collective-permute-start(f32[64,256]{1,0:T(8,128)S(1)} %get-tuple-element.36), channel_id=1, source_target_pairs={{0,3},{1,0},{2,1},{3,2},{4,7},{5,4},{6,5},{7,6},{8,11},{9,8},{10,9... | collective-permute-start | bytes 196616 | tf_op jit(solution)/shard_map/ppermute | solution.py:272
  160.9 6.5 %collective-permute-start.1 = (f32[64,256]{1,0:T(8,128)S(1)}, f32[64,256]{1,0:T(8,128)S(1)}, u32[]{:S(2)}, u32[]{:S(2)}) collective-permute-start(f32[64,256]{1,0:T(8,128)S(1)} %get-tuple-element.37), channel_id=1, source_target_pairs={{0,2},{1,3},{2,0},{3,1},{4,6},{5,7},{6,4},{7,5},{8,10},{9,11},{10,... | collective-permute-start | bytes 196616 | tf_op jit(solution)/shard_map/ppermute | solution.py:272
  164.0 6.5 %collective-permute-start = (f32[64,256]{1,0:T(8,128)S(1)}, f32[64,256]{1,0:T(8,128)S(1)}, u32[]{:S(2)}, u32[]{:S(2)}) collective-permute-start(f32[64,256]{1,0:T(8,128)S(1)} %get-tuple-element.35), channel_id=1, source_target_pairs={{0,1},{1,2},{2,3},{3,0},{4,5},{5,6},{6,7},{7,4},{8,9},{9,10},{10,1... | collective-permute-start | bytes 196616 | tf_op jit(solution)/shard_map/ppermute | solution.py:272
  170.7 47.9 %copy-start.5 = (bf16[64,256]{0,1:T(8,128)(2,1)}, bf16[64,256]{0,1:T(8,128)(2,1)S(1)}, u32[]{:S(2)}) copy-start(bf16[64,256]{0,1:T(8,128)(2,1)S(1)} %copy.50) | copy-start | bytes 98308
  170.9 8.4 %collective-permute-start.5 = (f32[64,64]{1,0:T(8,128)S(1)}, f32[64,64]{1,0:T(8,128)S(1)}, u32[]{:S(2)}, u32[]{:S(2)}) collective-permute-start(f32[64,64]{1,0:T(8,128)S(1)} %convolution_bitcast_fusion), channel_id=1, source_target_pairs={{0,2},{1,3},{2,0},{3,1},{4,6},{5,7},{6,4},{7,5},{8,10},{9,11},{10,... | collective-permute-start | bytes 49160 | tf_op jit(solution)/shard_map/ppermute | solution.py:253
  173.4 6.2 %collective-permute-start.6 = (f32[64,64]{1,0:T(8,128)S(1)}, f32[64,64]{1,0:T(8,128)S(1)}, u32[]{:S(2)}, u32[]{:S(2)}) collective-permute-start(f32[64,64]{1,0:T(8,128)S(1)} %convolution_bitcast_fusion), channel_id=1, source_target_pairs={{0,3},{1,2},{2,1},{3,0},{4,7},{5,6},{6,5},{7,4},{8,11},{9,10},{10,... | collective-permute-start | bytes 49160 | tf_op jit(solution)/shard_map/ppermute | solution.py:253
  176.0 5.0 %collective-permute-start.4 = (f32[64,64]{1,0:T(8,128)S(1)}, f32[64,64]{1,0:T(8,128)S(1)}, u32[]{:S(2)}, u32[]{:S(2)}) collective-permute-start(f32[64,64]{1,0:T(8,128)S(1)} %convolution_bitcast_fusion), channel_id=1, source_target_pairs={{0,1},{1,0},{2,3},{3,2},{4,5},{5,4},{6,7},{7,6},{8,9},{9,8},{10,11... | collective-permute-start | bytes 49160 | tf_op jit(solution)/shard_map/ppermute | solution.py:253
  180.9 34.0 %collective-permute-start.7 = (f32[64,64]{1,0:T(8,128)S(1)}, f32[64,64]{1,0:T(8,128)S(1)}, u32[]{:S(2)}, u32[]{:S(2)}) collective-permute-start(f32[64,64]{1,0:T(8,128)S(1)} %add_add_fusion), channel_id=1, source_target_pairs={{0,256},{256,0},{1,257},{257,1},{2,258},{258,2},{3,259},{259,3},{4... | collective-permute-start | bytes 49160 | tf_op jit(solution)/shard_map/ppermute | solution.py:253
  207.0 10.8 %collective-permute-start.3 = (f32[64,64]{0,1:T(8,128)S(1)}, f32[64,64]{0,1:T(8,128)S(1)}, u32[]{:S(2)}, u32[]{:S(2)}) collective-permute-start(f32[64,64]{0,1:T(8,128)S(1)} %convolution_bitcast_fusion.1), channel_id=1, source_target_pairs={{0,256},{256,0},{1,257},{257,1},{2,258},{258,2},{3,259},{259,3},{4... | collective-permute-start | bytes 49160 | tf_op jit(solution)/shard_map/ppermute | solution.py:253

commit v3 on v2

--- a/solution.py
+++ b/solution.py
@@ -25,19 +25,52 @@
             o_ref[2 * pair + 1, rows, :] = jnp.concatenate([k[:, HEAD:], v[:, HEAD:]], axis=1)
 
 
-def unpack_kernel(i_ref, k_ref, v_ref):
-    slots, span, width = k_ref.shape
+def unpack_kernel(i_ref, o_ref):
+    slots, span, width = o_ref.shape
     for pair in range(width // (2 * HEAD)):
         low = pair * 2 * HEAD
+        even = i_ref[2 * pair, :span, :]
+        odd = i_ref[2 * pair + 1, :span, :]
         for slot in range(slots):
-            rows = pl.ds(slot * span, span)
-            even = i_ref[2 * pair, rows, :]
-            odd = i_ref[2 * pair + 1, rows, :]
-            k_ref[slot, :, low : low + 2 * HEAD] = jnp.concatenate([even[:, :HEAD], odd[:, :HEAD]], axis=1)
-            v_ref[slot, :, low : low + 2 * HEAD] = jnp.concatenate([even[:, HEAD:], odd[:, HEAD:]], axis=1)
+            side = slice(slot * HEAD, (slot + 1) * HEAD)
+            o_ref[slot, :, low : low + 2 * HEAD] = jnp.concatenate([even[:, side], odd[:, side]], axis=1)
 
 
 PACK_HEADS = 16
+
+
+def latent_kernel(questions, owner_ref, counts_ref, down_ref, hidden_ref, o_ref):
+    down = down_ref[...]
+    targets = hidden_ref.shape[2]
+    for question in range(questions):
+        o_ref[:, 0, question * targets : (question + 1) * targets] = lax.dot_general(
+            down, hidden_ref[question], (((0,), (0,)), ((), ())), preferred_element_type=F32
+        )
+    lanes = lax.broadcasted_iota(jnp.int32, (o_ref.shape[0], 128), 1)
+    tags = jnp.zeros(lanes.shape, jnp.int32)
+    for slot in range(owner_ref.shape[0]):
+        tag = jnp.where(slot < counts_ref[0], owner_ref[slot], questions)
+        tags = jnp.where(lanes == slot, tag, tags)
+    o_ref[:, 0, questions * targets :] = tags.astype(F32)
+
+
+def latent_parts(owner, counts, down_weight, hidden_t):
+    questions, size, targets = hidden_t.shape
+    ranks = down_weight.shape[1]
+    smem, vmem = pl.BlockSpec(memory_space=pltpu.SMEM), pl.BlockSpec(memory_space=pltpu.VMEM)
+    return pl.pallas_call(
+        functools.partial(latent_kernel, questions),
+        in_specs=[smem, smem, vmem, vmem],
+        out_specs=vmem,
+        out_shape=jax.ShapeDtypeStruct((ranks, 1, questions * targets + 128), F32),
+        compiler_params=pltpu.CompilerParams(vmem_limit_bytes=VMEM_LIMIT),
+        cost_estimate=pl.CostEstimate(
+            flops=2 * questions * size * targets * ranks,
+            bytes_accessed=6 * questions * size * targets,
+            transcendentals=0,
+        ),
+        name="latent_parts",
+    )(owner, counts, down_weight, hidden_t)
 
 
 def pack(keys, values, spare):
@@ -58,21 +91,20 @@
 
 def unpack(table, slots, span):
     heads, rows, _ = table.shape
-    part = pl.BlockSpec((slots, span, PACK_HEADS * HEAD), lambda i: (0, 0, i))
-    shape = jax.ShapeDtypeStruct((slots, span, heads * HEAD), table.dtype)
     return pl.pallas_call(
         unpack_kernel,
         grid=(heads // PACK_HEADS,),
         in_specs=[pl.BlockSpec((PACK_HEADS, rows, 2 * HEAD), lambda i: (i, 0, 0))],
-        out_specs=[part, part],
-        out_shape=[shape, shape],
-        compiler_params=pltpu.CompilerParams(vmem_limit_bytes=VMEM_LIMIT),
-        cost_estimate=pl.CostEstimate(flops=0, bytes_accessed=8 * slots * span * heads * HEAD, transcendentals=0),
+        out_specs=pl.BlockSpec((slots, span, PACK_HEADS * HEAD), lambda i: (0, 0, i)),
+        out_shape=jax.ShapeDtypeStruct((slots, span, heads * HEAD), table.dtype),
+        compiler_params=pltpu.CompilerParams(vmem_limit_bytes=VMEM_LIMIT),
+        cost_estimate=pl.CostEstimate(flops=0, bytes_accessed=4 * slots * span * heads * HEAD, transcendentals=0),
         name="unpack",
     )(table)
 
 
-CHUNK_SLOTS = 4
+STATS_CHUNK = 4
+GRAD_CHUNK = 14
 
 
 def two_sided(q_ref, u_ref):
@@ -88,9 +120,9 @@
     return slot // slots, pl.ds(pl.multiple_of(lax.rem(slot, slots) * span, span), span)
 
 
-def gathered(chosen_ref, t_ref, slots, span, first):
+def gathered(chosen_ref, t_ref, slots, span, first, count):
     blocks = []
-    for i in range(CHUNK_SLOTS):
+    for i in range(count):
         device, rows = slot_rows(chosen_ref, slots, span, first + i)
         blocks.append(t_ref[device, rows, :])
     return jnp.concatenate(blocks, axis=0)
@@ -103,9 +135,9 @@
     top = jnp.full((1, targets), -jnp.inf, F32)
     mass = jnp.zeros((1, targets), F32)
     dot = jnp.zeros((1, targets), F32)
-    for chunk in range(per_question // CHUNK_SLOTS):
-        first = question * per_question + chunk * CHUNK_SLOTS
-        rows = gathered(chosen_ref, t_ref, slots, span, first)
+    for chunk in range(per_question // STATS_CHUNK):
+        first = question * per_question + chunk * STATS_CHUNK
+        rows = gathered(chosen_ref, t_ref, slots, span, first, STATS_CHUNK)
         prod = jnp.dot(rows, both, preferred_element_type=F32)
         scores, prob_grad = prod[:, :targets], prod[:, targets:]
         new_top = jnp.maximum(top, jnp.max(scores, axis=0, keepdims=True))
@@ -127,8 +159,38 @@
     return top, inverse, delta
 
 
-def grad_kernel(
-    per_question, slots, span, chosen_ref, q_ref, u_ref, w_ref, s_ref, t_ref, dq_ref, l_ref, o_ref
+def chunk_products(chosen_ref, t_ref, slots, span, first, both, stats):
+    top, inverse, delta = stats
+    targets = top.shape[1]
+    rows = gathered(chosen_ref, t_ref, slots, span, first, GRAD_CHUNK)
+    prod = jnp.dot(rows, both, preferred_element_type=F32)
+    scores, prob_grad = prod[:, :targets], prod[:, targets:]
+    weights = jnp.exp(scores - top) * inverse
+    score_grad = (weights * (prob_grad - delta)).astype(BF16)
+    return rows, weights, score_grad
+
+
+def store_half(o_ref, slot, slots, value):
+    device, span = slot // slots, value.shape[0]
+    lanes = lax.broadcasted_iota(jnp.int32, value.shape, 1)
+    old = o_ref[device, :span, :]
+    o_ref[device, :span, :] = jnp.where(lanes // HEAD == lax.rem(slot, slots), value, old)
+
+
+def query_value_kernel(
+    per_question,
+    slots,
+    span,
+    chosen_ref,
+    q_ref,
+    u_ref,
+    w_ref,
+    s_ref,
+    t_ref,
+    dq_ref,
+    o_ref,
+    rows_ref,
+    grad_ref,
 ):
     question = pl.program_id(0)
     targets = q_ref.shape[2]
@@ -140,26 +202,25 @@
         o_ref[...] = jnp.zeros_like(o_ref)
 
     both = two_sided(q_ref, u_ref)
-    top, inverse, delta = row_stats(s_ref)
-    dq = jnp.zeros((2 * HEAD, targets), F32)
-    for chunk in range(per_question // CHUNK_SLOTS):
-        first = question * per_question + chunk * CHUNK_SLOTS
-        rows = gathered(chosen_ref, t_ref, slots, span, first)
-        prod = jnp.dot(rows, both, preferred_element_type=F32)
-        scores, prob_grad = prod[:, :targets], prod[:, targets:]
-        weights = jnp.exp(scores - top) * inverse
-        score_grad = (weights * (prob_grad - delta)).astype(BF16)
-        pair = jnp.concatenate([score_grad, weights.astype(BF16)], axis=1)
+    upstream = jnp.concatenate([u_ref[0]] * slots, axis=0)
+    stats = row_stats(s_ref)
+    size = GRAD_CHUNK * span
+    last = (((1,), (1,)), ((), ()))
+    for chunk in range(per_question // GRAD_CHUNK):
+        first = question * per_question + chunk * GRAD_CHUNK
+        rows, weights, score_grad = chunk_products(
+            chosen_ref, t_ref, slots, span, first, both, stats
+        )
+        rows_ref[chunk * size : (chunk + 1) * size, :] = rows
+        grad_ref[chunk * size : (chunk + 1) * size, :] = score_grad
         out = lax.dot_general(
-            pair, both, (((1,), (1,)), ((), ())), preferred_element_type=F32
+            weights.astype(BF16), upstream, last, preferred_element_type=F32
         ).astype(BF16)
-        for i in range(CHUNK_SLOTS):
-            device, place = slot_rows(chosen_ref, slots, span, first + i)
-            o_ref[device, place, :] = out[i * span : (i + 1) * span]
-        dq = dq + lax.dot_general(
-            rows, score_grad, (((0,), (0,)), ((), ())), preferred_element_type=F32
-        )
-    dq = dq[:HEAD]
+        for i in range(GRAD_CHUNK):
+            store_half(o_ref, chosen_ref[first + i], slots, out[i * span : (i + 1) * span])
+    dq = lax.dot_general(
+        rows_ref[...], grad_ref[...], (((0,), (0,)), ((), ())), preferred_element_type=F32
+    )[:HEAD]
 
     for side in range(pair_width // piece):
 
@@ -175,10 +236,35 @@
     latent = jnp.dot(w_ref[...], high, preferred_element_type=F32) + jnp.dot(
         w_ref[...], low, preferred_element_type=F32
     )
-    lanes = l_ref.shape[2]
-    for part in range(targets // lanes):
-        row = question * (targets // lanes) + part
-        l_ref[:, pl.ds(row, 1), :] = latent[:, None, part * lanes : (part + 1) * lanes]
+    high = latent.astype(BF16)
+    low = (latent - high.astype(F32)).astype(BF16)
+    bands = latent.shape[0] // 8
+    tiles = o_ref.shape[0] // bands
+    for band in range(bands):
+        for part in range(targets // 128):
+            tile = band * tiles + question * (targets // 128) + part
+            cut = (slice(band * 8, (band + 1) * 8), slice(part * 128, (part + 1) * 128))
+            o_ref[tile, span : span + 16, :] = jnp.concatenate([high[cut], low[cut]], axis=0)
+
+
+def key_kernel(per_question, slots, span, chosen_ref, q_ref, u_ref, s_ref, t_ref, o_ref):
+    question = pl.program_id(0)
+
+    @pl.when(question == 0)
+    def _():
+        o_ref[...] = jnp.zeros_like(o_ref)
+
+    both = two_sided(q_ref, u_ref)
+    query = jnp.concatenate([q_ref[0]] * slots, axis=0)
+    stats = row_stats(s_ref)
+    for chunk in range(per_question // GRAD_CHUNK):
+        first = question * per_question + chunk * GRAD_CHUNK
+        _, _, score_grad = chunk_products(chosen_ref, t_ref, slots, span, first, both, stats)
+        out = lax.dot_general(
+            score_grad, query, (((1,), (1,)), ((), ())), preferred_element_type=F32
+        ).astype(BF16)
+        for i in range(GRAD_CHUNK):
+            store_half(o_ref, chosen_ref[first + i], slots, out[i * span : (i + 1) * span])
 
 
 def attend_stats(chosen, query_t, upstream_t, table, per_question, slots, span):
@@ -205,17 +291,17 @@
     )(chosen, query_t, upstream_t, table)
 
 
-def attend_grads(chosen, query_t, upstream_t, up_weight, stats, table, per_question, slots, span):
+def query_value_grads(chosen, query_t, upstream_t, up_weight, stats, table, per_question, slots, span):
     questions, size, targets = query_t.shape
     peers = stats.shape[0]
     one = pl.BlockSpec((1, size, targets), lambda q, c: (q, 0, 0))
     whole = pl.BlockSpec(table.shape, lambda q, c: (0, 0, 0))
+    out = (table.shape[0], span + 16, table.shape[2])
     keys = per_question * span
     piece = targets // peers
     in_block = 128 // piece
-    latent_shape = (up_weight.shape[0], questions * targets // 128, 128)
-    return pl.pallas_call(
-        functools.partial(grad_kernel, per_question, slots, span),
+    return pl.pallas_call(
+        functools.partial(query_value_kernel, per_question, slots, span),
         grid_spec=pltpu.PrefetchScalarGridSpec(
             num_scalar_prefetch=1,
             grid=(questions,),
@@ -227,15 +313,14 @@
                 whole,
             ],
             out_specs=[
-                pl.BlockSpec((peers, HEAD, 128), lambda q, c: (0, 0, q // in_block)),
-                pl.BlockSpec(latent_shape, lambda q, c: (0, 0, 0)),
-                whole,
+                pl.BlockSpec((peers, size, 128), lambda q, c: (0, 0, q // in_block)),
+                pl.BlockSpec(out, lambda q, c: (0, 0, 0)),
             ],
+            scratch_shapes=[pltpu.VMEM((keys, 2 * HEAD), BF16), pltpu.VMEM((keys, targets), BF16)],
         ),
         out_shape=[
-            jax.ShapeDtypeStruct((peers, HEAD, questions * piece), F32),
-            jax.ShapeDtypeStruct(latent_shape, F32),
-            jax.ShapeDtypeStruct(table.shape, BF16),
+            jax.ShapeDtypeStruct((peers, size, questions * piece), F32),
+            jax.ShapeDtypeStruct(out, BF16),
         ],
         compiler_params=pltpu.CompilerParams(vmem_limit_bytes=VMEM_LIMIT),
         cost_estimate=pl.CostEstimate(
@@ -243,24 +328,45 @@
             bytes_accessed=4 * table.size,
             transcendentals=questions * targets * keys,
         ),
-        name="grads",
+        name="query_value_grads",
     )(chosen, query_t, upstream_t, up_weight, stats, table)
 
 
-def swap_sum(x, axis, shift, radix):
-    size = lax.axis_size(axis)
-    got = [x] + [
-        lax.ppermute(x, axis, [(i, i ^ (k << shift)) for i in range(size)]) for k in range(1, radix)
-    ]
-    while len(got) > 1:
-        got = [a + b for a, b in zip(got[0::2], got[1::2])]
-    return got[0]
+def key_grads(chosen, query_t, upstream_t, stats, table, per_question, slots, span):
+    questions, size, targets = query_t.shape
+    peers = stats.shape[0]
+    one = pl.BlockSpec((1, size, targets), lambda q, c: (q, 0, 0))
+    whole = pl.BlockSpec(table.shape, lambda q, c: (0, 0, 0))
+    out = (table.shape[0], span + 8, table.shape[2])
+    keys = per_question * span
+    return pl.pallas_call(
+        functools.partial(key_kernel, per_question, slots, span),
+        grid_spec=pltpu.PrefetchScalarGridSpec(
+            num_scalar_prefetch=1,
+            grid=(questions,),
+            in_specs=[
+                one,
+                one,
+                pl.BlockSpec((peers, 1, 8, targets), lambda q, c: (0, q, 0, 0)),
+                whole,
+            ],
+            out_specs=pl.BlockSpec(out, lambda q, c: (0, 0, 0)),
+        ),
+        out_shape=jax.ShapeDtypeStruct(out, BF16),
+        compiler_params=pltpu.CompilerParams(vmem_limit_bytes=VMEM_LIMIT),
+        cost_estimate=pl.CostEstimate(
+            flops=16 * questions * targets * keys * HEAD,
+            bytes_accessed=4 * table.size,
+            transcendentals=questions * targets * keys,
+        ),
+        name="key_grads",
+    )(chosen, query_t, upstream_t, stats, table)
 
 
 def to_all(x, axis):
     size = lax.axis_size(axis)
-    return lax.all_to_all(
-        jnp.broadcast_to(x[None], (size,) + x.shape), axis, split_axis=0, concat_axis=0, tiled=True
+    return exchange(
+        jnp.broadcast_to(x[None], (size,) + x.shape), axis
     )
 
 
@@ -300,11 +406,7 @@
     row_shape = (positions // 128, 128)
 
     hidden_t = jnp.swapaxes(hidden, 1, 2)
-    latent_part = jnp.einsum("dr,qdt->rqt", adapter_down_weight, hidden_t, preferred_element_type=F32)
-    live = jnp.arange(slots_dev, dtype=jnp.int32) < counts[0]
-    tag = jnp.where(live, owner, questions).astype(F32)
-    tags = jnp.broadcast_to(jnp.pad(tag, (0, 128 - slots_dev))[None, None], (group_count, 1, 128))
-    sent = jnp.concatenate([latent_part.reshape(group_count, 1, positions), tags], axis=2)
+    sent = latent_parts(owner, counts, adapter_down_weight, hidden_t)
     got = exchange(sent, "grp")
     latent_row = jnp.sum(got[:, 0, :positions], axis=0).astype(BF16).reshape(row_shape)
     slot_key = got[:, 0, positions : positions + slots_dev].astype(jnp.int32).reshape(total_slots)
@@ -333,37 +435,36 @@
     query_t = (frozen_t.astype(F32) + raised).astype(BF16)
 
     stats = attend_stats(chosen, query_t, upstream_t, table, per_question, slots_dev, span)
-    dq_parts, latent_grad_part, grad_table = attend_grads(
-        chosen,
-        query_t,
-        upstream_t,
-        adapter_up_weight,
-        to_all(stats, "tp"),
-        table,
-        per_question,
-        slots_dev,
-        span,
-    )
-    latent_grad_row = jnp.sum(exchange(latent_grad_part, "grp"), axis=0)
-    latent_grad_row = jnp.sum(to_all(latent_grad_row, "tp"), axis=0).astype(BF16)
-    grad_table = lax.dynamic_update_slice(
-        grad_table,
-        jnp.broadcast_to(latent_grad_row[None], (group_count,) + row_shape),
-        (0, table_rows, 0),
-    )
-    back = exchange(grad_table, "grp")
-    grad_keys, grad_values = unpack(back, slots_dev, span)
-    latent_grad = back[:, table_rows:, :].reshape(group_count, questions, targets)
+    all_stats = to_all(stats, "tp")
+    shared = (table, per_question, slots_dev, span)
+    dq_parts, value_table = query_value_grads(
+        chosen, query_t, upstream_t, adapter_up_weight, all_stats, *shared
+    )
+    key_table = key_grads(chosen, query_t, upstream_t, all_stats, *shared)
+    value_back = exchange(value_table, "grp")
+    latent_grad_tile = jnp.sum(value_back[:, span:, :].astype(F32), axis=0)
+    latent_grad_tile = (latent_grad_tile[:8] + latent_grad_tile[8:]).astype(BF16)
+    key_table = lax.dynamic_update_slice(
+        key_table,
+        jnp.broadcast_to(latent_grad_tile[None], (group_count,) + latent_grad_tile.shape),
+        (0, span, 0),
+    )
+    grad_values = unpack(value_back, slots_dev, span)
+    key_back = exchange(key_table, "grp")
+    grad_keys = unpack(key_back, slots_dev, span)
+    latent_grad = key_back[:, span:, :].reshape(HEAD // 8, positions // 128, 8, 128)
+    latent_grad = jnp.transpose(latent_grad, (0, 2, 1, 3)).reshape(HEAD, questions, targets)
     grad_a = jnp.einsum("qdt,rqt->dr", hidden_t, latent_grad, preferred_element_type=F32)
-    grad_a = swap_sum(grad_a, "sect", 0, lax.axis_size("sect"))
 
     dq_t = scatter_sum_tp(dq_parts).astype(BF16).reshape(HEAD, questions, piece)
     adapted = jnp.transpose(dq_t, (1, 2, 0))
     start = lax.axis_index("tp") * piece
     latent_cut = lax.dynamic_slice_in_dim(latent_t, start, piece, 2)
     grad_b = jnp.einsum("rqt,dqt->rd", latent_cut, dq_t, preferred_element_type=F32)
-    grad_b = swap_sum(swap_sum(grad_b, "tp", 0, token_split), "sect", 0, lax.axis_size("sect"))
-    return (adapted, grad_keys, grad_values, grad_a, grad_b)
+    got = to_all(jnp.concatenate([grad_a, grad_b], axis=1), ("sect", "tp"))
+    got, grad_keys = lax.optimization_barrier((got, grad_keys))
+    grads = jnp.sum(got, axis=0)
+    return (adapted, grad_keys, grad_values, grads[:, :HEAD], grads[:, HEAD:])
 
 
 def solution(mesh):

time: 222 us -> 216 us (0.973); the launches traced: 219 us -> 215 us
  blocking collectives: 42.4 us -> 8.65 us
  waiting for transfers between devices: 81.4 us -> 103 us
  local copies, waits for them, and re-layouts: 7.51 us -> 13.6 us
  Pallas kernels: 17.4 us -> 22 us
  other arithmetic: 3.76 us -> 0.82 us
    all_to_all x3 -> x5, starting transfers between devices: 28.3 us -> 56.4 us  [exchange(): return lax.all_to_all(x, axis, split_axis=0, concat_axis=0, tiled=True)]
    ppermute x5 -> x0, starting transfers between devices: 26.8 us -> none  [swap_sum(): lax.ppermute(x, axis, [(i, i ^ k << shift) for i in range(size)])]
    all_to_all x3 -> x5, waiting for transfers between devices: 75.2 us -> 98.3 us  [exchange(): return lax.all_to_all(x, axis, split_axis=0, concat_axis=0, tiled=True)]
    all_to_all x1, blocking collectives: 27.2 us -> 8.65 us  [exchange(): return lax.all_to_all(x, axis, split_axis=0, concat_axis=0, tiled=True)]
    all_to_all x2 -> x0, blocking collectives: 15.2 us -> none  [to_all(): lax.all_to_all(jnp.broadcast_to(x[None], (size,) + x.shape), axis, split_...]
    unnamed x19 -> x46, local copies, waits for them, and re-layouts: 4.2 us -> 10.3 us
    pallas_call x1 -> x3, Pallas kernels: 9.1 us -> 12.3 us  [the longest x1 6.05 us: query_value_grads(): pl.pallas_call(functools.partial(query_value_kernel, per_question, slots,...]
  transfers between devices with their start and end apart: 11 -> 8, of which waited for: 7 -> 7; matrix products, arithmetic and copies ran while one was open for 1% -> 0% of each run, Pallas kernels for 2% -> 5%
where the time goes in v3:
time: 216 us; the launch traced here: 215 us
  waiting for transfers between devices  103 us (48%)
  starting transfers between devices  64.4 us (30%)
  Pallas kernels  22 us (10%)
  local copies, waits for them, and re-layouts  13.6 us (6%)
  blocking collectives  8.65 us (4%)
    all_to_all x5, waiting for transfers between devices, exchange(): return lax.all_to_all(x, axis, split_axis=0, concat_axis=0, tiled=True)  98.3 us
    all_to_all x5, starting transfers between devices, exchange(): return lax.all_to_all(x, axis, split_axis=0, concat_axis=0, tiled=True)  56.4 us
    unnamed x46, local copies, waits for them, and re-layouts  10.3 us
    all_to_all x1, blocking collectives, exchange(): return lax.all_to_all(x, axis, split_axis=0, concat_axis=0, tiled=True)  8.65 us
    ppermute x3, starting transfers between devices, scatter_sum_tp(): lax.ppermute(sent, 'tp', [(i, (i + k) % size) for i in range(size)])  7.95 us
    pallas_call x1, Pallas kernels, query_value_grads(): pl.pallas_call(functools.partial(query_value_kernel, per_question, slots,...  6.05 us
    ppermute x3, waiting for transfers between devices, scatter_sum_tp(): lax.ppermute(sent, 'tp', [(i, (i + k) % size) for i in range(size)])  5.09 us
    pallas_call x1, Pallas kernels, key_grads(): pl.pallas_call(functools.partial(key_kernel, per_question, slots, span),...  4.74 us
  transfers between devices with their start and end apart: 8, of which 7 were waited for; matrix products, arithmetic and copies ran while one was open for 0% of the time, Pallas kernels for 5%

profile of v3, /device:TPU:1, one launch (start us, length us, event | category | flops | bytes accessed | tf_op | source)
XLA Modules:
  0.0 215.2 jit_solution(18350342316851383967)
XLA Ops:
  1.3 0.9 copy-done.4
  3.6 1.5 latent_parts.1
  5.1 17.1 %all-to-all-start = ((f32[64,1,1152]{2,1,0:T(1,128)}), f32[64,1,1152]{2,1,0:T(1,128)S(1)}, u32[]{:S(2)}, u32[]{:S(2)}) async-start(f32[64,1,1152]{2,1,0:T(1,128)} %latent_parts.1), calls=%async_computation | async-start | bytes 589824 | tf_op jit(solution)/shard_map/all_to_all | solution.py:383
  22.2 1.2 copy-done.2
  23.4 1.2 copy-done.3
  24.7 2.4 %pack.1 = bf16[64,136,128]{2,1,0:T(8,128)(2,1)} custom-call(bf16[2,64,4096]{2,1,0:T(8,128)(2,1)S(1)} %copy-done.2, bf16[2,64,4096]{2,1,0:T(8,128)(2,1)S(1)} %copy-done.3), custom_call_target="tpu_custom_call" | custom-call | bytes 4194304 | tf_op jit(solution)/shard_map/pack/pallas_call | solution.py:80
  27.0 8.3 %all-to-all-done = f32[64,1,1152]{2,1,0:T(1,128)S(1)} async-done(((f32[64,1,1152]{2,1,0:T(1,128)}), f32[64,1,1152]{2,1,0:T(1,128)S(1)}, u32[]{:S(2)}, u32[]{:S(2)}) %all-to-all-start) | async-done | bytes 294944 | tf_op jit(solution)/shard_map/all_to_all | solution.py:383
  36.2 6.1 %all-to-all-start.1 = ((bf16[64,136,128]{2,1,0:T(8,128)(2,1)}), bf16[64,136,128]{2,1,0:T(8,128)(2,1)S(1)}, u32[]{:S(2)}, u32[]{:S(2)}) async-start(bf16[64,136,128]{2,1,0:T(8,128)(2,1)} %broadcast_dynamic-update-slice_fusion.1), calls=%async_computation.1 | async-start | bytes 4456448 | tf_op jit(solution)/shard_map/all_to_all | solution.py:383
  43.0 50.2 %all-to-all-done.1.t_ref = bf16[64,136,128]{2,1,0:T(8,128)(2,1)S(1)} async-done(((bf16[64,136,128]{2,1,0:T(8,128)(2,1)}), bf16[64,136,128]{2,1,0:T(8,128)(2,1)S(1)}, u32[]{:S(2)}, u32[]{:S(2)}) %all-to-all-start.1) | async-done | bytes 2228256 | tf_op jit(solution)/shard_map/all_to_all | solution.py:383
  93.7 3.7 %stats.1 = f32[4,8,256]{2,1,0:T(8,128)S(1)} custom-call(s32[112]{0:T(128)S(1)} %select_reduce_fusion.chosen_ref, bf16[4,64,256]{2,1,0:T(8,128)(2,1)S(1)} %fusion.1.q_ref, bf16[4,64,256]{2,1,0:T(8,128)(2,1)S(1)} %select_bitcast_fusion.u_ref, bf16[64,136,128]{2,1,0:T(8,128)(2,1)S(1)} %all-to-all-done.1.t_ref), custom_call_target="tpu_custom_call" | custom-call | flops 939524096 | bytes 2228224 | tf_op jit(solution)/shard_map/stats/pallas_call | solution.py:275
  97.4 8.6 %all_to_all.30.s_ref = f32[4,4,8,256]{3,2,1,0:T(8,128)S(1)} all-to-all(f32[4,4,8,256]{3,2,1,0:T(8,128)S(1)} %broadcast_in_dim.35), channel_id=1, replica_groups=mesh['sect'=2,'grp'=64,'tp'=4] {'tp'}, dimensions={0} | all-to-all | bytes 262144 | tf_op jit(solution)/shard_map/all_to_all | solution.py:383
  106.0 6.0 %query_value_grads.1 = (f32[4,64,256]{2,1,0:T(8,128)S(1)}, bf16[64,80,128]{2,1,0:T(8,128)(2,1)S(1)}) custom-call(s32[112]{0:T(128)S(1)} %select_reduce_fusion.chosen_ref, bf16[4,64,256]{2,1,0:T(8,128)(2,1)S(1)} %fusion.1.q_ref, bf16[4,64,256]{2,1,0:T(8,128)(2,1)S(1)} %select_bitcast_fusion.u_ref, bf16[64,64]{1,0:T(8,128)(2,1)S(1)} %copy-done.15, ...), custom_call_target="tpu_custom_call" | custom-call | flops 2818572288 | bytes 4456448 | tf_op jit(solution)/shard_map/query_value_grads/pallas_call | solution.py:303
  112.1 1.1 copy-done
  113.9 15.0 %all-to-all-start.3 = ((bf16[64,80,128]{2,1,0:T(8,128)(2,1)}), bf16[64,80,128]{2,1,0:T(8,128)(2,1)S(1)}, u32[]{:S(2)}, u32[]{:S(2)}) async-start(bf16[64,80,128]{2,1,0:T(8,128)(2,1)} %copy-done), calls=%async_computation.3 | async-start | bytes 2621440 | tf_op jit(solution)/shard_map/all_to_all | solution.py:383
  128.9 0.9 copy-done.9
  129.8 0.9 copy-done.11
  130.7 0.9 copy-done.13
  131.6 4.7 %key_grads.1 = bf16[64,72,128]{2,1,0:T(8,128)(2,1)S(1)} custom-call(s32[112]{0:T(128)S(1)} %select_reduce_fusion.chosen_ref, bf16[4,64,256]{2,1,0:T(8,128)(2,1)S(1)} %copy-done.9, bf16[4,64,256]{2,1,0:T(8,128)(2,1)S(1)} %copy-done.11, f32[4,4,8,256]{3,2,1,0:T(8,128)S(1)} %copy-done.13, bf16[64,136,128]{2,1,0:T(8,128)(2,1)S(1)} %all-to-all-done.1.t_ref), custom_call_target="tpu_custom_call" | custom-call | flops 1879048192 | bytes 4456448 | tf_op jit(solution)/shard_map/key_grads/pallas_call | solution.py:342
  136.4 1.0 copy-done.1
  137.4 21.8 %all-to-all-done.3.i_ref = bf16[64,80,128]{2,1,0:T(8,128)(2,1)S(1)} async-done(((bf16[64,80,128]{2,1,0:T(8,128)(2,1)}), bf16[64,80,128]{2,1,0:T(8,128)(2,1)S(1)}, u32[]{:S(2)}, u32[]{:S(2)}) %all-to-all-start.3) | async-done | bytes 1310752 | tf_op jit(solution)/shard_map/all_to_all | solution.py:383
  160.0 10.2 %all-to-all-start.4 = ((bf16[64,72,128]{2,1,0:T(8,128)(2,1)}), bf16[64,72,128]{2,1,0:T(8,128)(2,1)S(1)}, u32[]{:S(2)}, u32[]{:S(2)}) async-start(bf16[64,72,128]{2,1,0:T(8,128)(2,1)} %broadcast_dynamic-update-slice_fusion), calls=%async_computation.4 | async-start | bytes 2359296 | tf_op jit(solution)/shard_map/all_to_all | solution.py:383
  170.3 2.8 %collective-permute-start.2 = (f32[64,256]{1,0:T(8,128)S(1)}, f32[64,256]{1,0:T(8,128)S(1)}, u32[]{:S(2)}, u32[]{:S(2)}) collective-permute-start(f32[64,256]{1,0:T(8,128)S(1)} %get-tuple-element.14), channel_id=1, source_target_pairs={{0,3},{1,0},{2,1},{3,2},{4,7},{5,4},{6,5},{7,6},{8,11},{9,8},{10,9... | collective-permute-start | bytes 196616 | tf_op jit(solution)/shard_map/ppermute | solution.py:378
  173.1 3.2 %collective-permute-start.1 = (f32[64,256]{1,0:T(8,128)S(1)}, f32[64,256]{1,0:T(8,128)S(1)}, u32[]{:S(2)}, u32[]{:S(2)}) collective-permute-start(f32[64,256]{1,0:T(8,128)S(1)} %get-tuple-element.15), channel_id=1, source_target_pairs={{0,2},{1,3},{2,0},{3,1},{4,6},{5,7},{6,4},{7,5},{8,10},{9,11},{10,... | collective-permute-start | bytes 196616 | tf_op jit(solution)/shard_map/ppermute | solution.py:378
  176.2 2.0 collective-permute-start
  178.3 1.6 collective-permute-done.1
  179.9 3.5 %collective-permute-done = f32[64,256]{1,0:T(8,128)S(1)} collective-permute-done((f32[64,256]{1,0:T(8,128)S(1)}, f32[64,256]{1,0:T(8,128)S(1)}, u32[]{:S(2)}, u32[]{:S(2)}) %collective-permute-start) | collective-permute-done | bytes 65568 | tf_op jit(solution)/shard_map/ppermute | solution.py:378
  183.8 15.0 %all-to-all-done.4.i_ref = bf16[64,72,128]{2,1,0:T(8,128)(2,1)S(1)} async-done(((bf16[64,72,128]{2,1,0:T(8,128)(2,1)}), bf16[64,72,128]{2,1,0:T(8,128)(2,1)S(1)}, u32[]{:S(2)}, u32[]{:S(2)}) %all-to-all-start.4) | async-done | bytes 1179680 | tf_op jit(solution)/shard_map/all_to_all | solution.py:383
  199.2 0.7 broadcast_in_dim.60
  199.9 8.0 %all-to-all-start.5 = ((f32[8,64,128]{2,1,0:T(8,128)}), f32[8,64,128]{2,1,0:T(8,128)S(1)}, u32[]{:S(2)}, u32[]{:S(2)}) async-start(f32[8,64,128]{2,1,0:T(8,128)} %broadcast_in_dim.60), calls=%async_computation.5 | async-start | bytes 524288 | tf_op jit(solution)/shard_map/all_to_all | solution.py:383
  207.9 1.8 unpack.3
  209.8 1.8 unpack.2
  211.6 2.9 %all-to-all-done.5 = f32[8,64,128]{2,1,0:T(8,128)S(1)} async-done(((f32[8,64,128]{2,1,0:T(8,128)}), f32[8,64,128]{2,1,0:T(8,128)S(1)}, u32[]{:S(2)}, u32[]{:S(2)}) %all-to-all-start.5) | async-done | bytes 262176 | tf_op jit(solution)/shard_map/all_to_all | solution.py:383
  (68 shorter events, 6.2 us)
Async XLA Ops:
  1.3 0.9 copy-start.4
  2.2 0.7 copy-start.14
  2.9 0.7 copy-start.16
  5.1 30.3 %all-to-all-start = ((f32[64,1,1152]{2,1,0:T(1,128)}), f32[64,1,1152]{2,1,0:T(1,128)S(1)}, u32[]{:S(2)}, u32[]{:S(2)}) async-start(f32[64,1,1152]{2,1,0:T(1,128)} %latent_parts.1), calls=%async_computation | async-start | bytes 589824 | tf_op jit(solution)/shard_map/all_to_all | solution.py:383
  22.2 1.2 copy-start.2
  23.4 1.2 copy-start.3
  36.2 6.2 %copy-start.22 = (s32[4]{0:T(128)S(1)}, s32[4]{0:T(128)}, u32[]{:S(2)}) copy-start(s32[4]{0:T(128)} %param.19) | copy-start | bytes 52
  36.2 6.2 %copy-start.21 = (bf16[4,256,64]{1,2,0:T(8,128)(2,1)S(1)}, bf16[4,256,64]{1,2,0:T(8,128)(2,1)}, u32[]{:S(2)}) copy-start(bf16[4,256,64]{1,2,0:T(8,128)(2,1)} %param.13) | copy-start | bytes 393220
  36.2 57.2 %copy-start.15 = (bf16[64,64]{1,0:T(8,128)(2,1)S(1)}, bf16[64,64]{1,0:T(8,128)(2,1)}, u32[]{:S(2)}) copy-start(bf16[64,64]{1,0:T(8,128)(2,1)} %w_ref.1) | copy-start | bytes 24580
  36.2 57.2 %copy-start.20 = (bf16[4,256,64]{1,2,0:T(8,128)(2,1)S(1)}, bf16[4,256,64]{1,2,0:T(8,128)(2,1)}, u32[]{:S(2)}) copy-start(bf16[4,256,64]{1,2,0:T(8,128)(2,1)} %param.12) | copy-start | bytes 393220
  36.2 57.1 %all-to-all-start.1 = ((bf16[64,136,128]{2,1,0:T(8,128)(2,1)}), bf16[64,136,128]{2,1,0:T(8,128)(2,1)S(1)}, u32[]{:S(2)}, u32[]{:S(2)}) async-start(bf16[64,136,128]{2,1,0:T(8,128)(2,1)} %broadcast_dynamic-update-slice_fusion.1), calls=%async_computation.1 | async-start | bytes 4456448 | tf_op jit(solution)/shard_map/all_to_all | solution.py:383
  42.5 63.5 %copy-start.10 = (bf16[4,64,256]{2,1,0:T(8,128)(2,1)}, bf16[4,64,256]{2,1,0:T(8,128)(2,1)S(1)}, u32[]{:S(2)}) copy-start(bf16[4,64,256]{2,1,0:T(8,128)(2,1)S(1)} %select_bitcast_fusion.u_ref) | copy-start | bytes 393220
  93.4 3.9 %copy-start.17 = (bf16[64,4,256]{2,1,0:T(4,128)(2,1)}, bf16[64,4,256]{2,1,0:T(4,128)(2,1)S(1)}, u32[]{:S(2)}) copy-start(bf16[64,4,256]{2,1,0:T(4,128)(2,1)S(1)} %reshape.73) | copy-start | bytes 393220
  93.6 12.4 %copy-start.8 = (bf16[4,64,256]{2,1,0:T(8,128)(2,1)}, bf16[4,64,256]{2,1,0:T(8,128)(2,1)S(1)}, u32[]{:S(2)}) copy-start(bf16[4,64,256]{2,1,0:T(8,128)(2,1)S(1)} %fusion.1.q_ref) | copy-start | bytes 393220
  106.0 6.1 %copy-start.12 = (f32[4,4,8,256]{3,2,1,0:T(8,128)}, f32[4,4,8,256]{3,2,1,0:T(8,128)S(1)}, u32[]{:S(2)}) copy-start(f32[4,4,8,256]{3,2,1,0:T(8,128)S(1)} %all_to_all.30.s_ref) | copy-start | bytes 393220
  112.1 1.1 copy-start
  113.2 0.7 copy-start.6
  113.9 45.4 %all-to-all-start.3 = ((bf16[64,80,128]{2,1,0:T(8,128)(2,1)}), bf16[64,80,128]{2,1,0:T(8,128)(2,1)S(1)}, u32[]{:S(2)}, u32[]{:S(2)}) async-start(bf16[64,80,128]{2,1,0:T(8,128)(2,1)} %copy-done), calls=%async_computation.3 | async-start | bytes 2621440 | tf_op jit(solution)/shard_map/all_to_all | solution.py:383
  128.9 0.9 copy-start.9
  129.8 0.9 copy-start.11
  130.7 0.9 copy-start.13
  136.4 1.0 copy-start.1
  159.3 10.9 %copy-start.7 = (f32[4,64,256]{2,1,0:T(8,128)S(1)}, f32[4,64,256]{2,1,0:T(8,128)}, u32[]{:S(2)}) copy-start(f32[4,64,256]{2,1,0:T(8,128)} %copy-done.6) | copy-start | bytes 786436
  160.0 18.2 %copy-start.18 = (bf16[64,4,256]{2,1,0:T(4,128)(2,1)S(1)}, bf16[64,4,256]{2,1,0:T(4,128)(2,1)}, u32[]{:S(2)}) copy-start(bf16[64,4,256]{2,1,0:T(4,128)(2,1)} %copy-done.17) | copy-start | bytes 393220
  160.0 38.8 %all-to-all-start.4 = ((bf16[64,72,128]{2,1,0:T(8,128)(2,1)}), bf16[64,72,128]{2,1,0:T(8,128)(2,1)S(1)}, u32[]{:S(2)}, u32[]{:S(2)}) async-start(bf16[64,72,128]{2,1,0:T(8,128)(2,1)} %broadcast_dynamic-update-slice_fusion), calls=%async_computation.4 | async-start | bytes 2359296 | tf_op jit(solution)/shard_map/all_to_all | solution.py:383
  170.2 28.8 %copy-start.5 = (bf16[4,256,64]{1,2,0:T(8,128)(2,1)S(1)}, bf16[4,256,64]{1,2,0:T(8,128)(2,1)}, u32[]{:S(2)}) copy-start(bf16[4,256,64]{1,2,0:T(8,128)(2,1)} %param.14) | copy-start | bytes 393220
  170.3 8.0 %collective-permute-start.2 = (f32[64,256]{1,0:T(8,128)S(1)}, f32[64,256]{1,0:T(8,128)S(1)}, u32[]{:S(2)}, u32[]{:S(2)}) collective-permute-start(f32[64,256]{1,0:T(8,128)S(1)} %get-tuple-element.14), channel_id=1, source_target_pairs={{0,3},{1,0},{2,1},{3,2},{4,7},{5,4},{6,5},{7,6},{8,11},{9,8},{10,9... | collective-permute-start | bytes 196616 | tf_op jit(solution)/shard_map/ppermute | solution.py:378
  173.1 6.8 %collective-permute-start.1 = (f32[64,256]{1,0:T(8,128)S(1)}, f32[64,256]{1,0:T(8,128)S(1)}, u32[]{:S(2)}, u32[]{:S(2)}) collective-permute-start(f32[64,256]{1,0:T(8,128)S(1)} %get-tuple-element.15), channel_id=1, source_target_pairs={{0,2},{1,3},{2,0},{3,1},{4,6},{5,7},{6,4},{7,5},{8,10},{9,11},{10,... | collective-permute-start | bytes 196616 | tf_op jit(solution)/shard_map/ppermute | solution.py:378
  176.2 7.1 %collective-permute-start = (f32[64,256]{1,0:T(8,128)S(1)}, f32[64,256]{1,0:T(8,128)S(1)}, u32[]{:S(2)}, u32[]{:S(2)}) collective-permute-start(f32[64,256]{1,0:T(8,128)S(1)} %get-tuple-element.13), channel_id=1, source_target_pairs={{0,1},{1,2},{2,3},{3,0},{4,5},{5,6},{6,7},{7,4},{8,9},{9,10},{10,1... | collective-permute-start | bytes 196616 | tf_op jit(solution)/shard_map/ppermute | solution.py:378
  183.5 26.2 %copy-start.19 = (bf16[64,256]{0,1:T(8,128)(2,1)}, bf16[64,256]{0,1:T(8,128)(2,1)S(1)}, u32[]{:S(2)}) copy-start(bf16[64,256]{0,1:T(8,128)(2,1)S(1)} %copy.31) | copy-start | bytes 98308
  199.9 14.5 %all-to-all-start.5 = ((f32[8,64,128]{2,1,0:T(8,128)}), f32[8,64,128]{2,1,0:T(8,128)S(1)}, u32[]{:S(2)}, u32[]{:S(2)}) async-start(f32[8,64,128]{2,1,0:T(8,128)} %broadcast_in_dim.60), calls=%async_computation.5 | async-start | bytes 524288 | tf_op jit(solution)/shard_map/all_to_all | solution.py:383

commit v4 on v3

--- a/solution.py
+++ b/solution.py
@@ -11,26 +11,34 @@
 BF16 = jnp.bfloat16
 F32 = jnp.float32
 VMEM_LIMIT = 32 * 1024 * 1024
+ALL_VMEM = 62 * 1024 * 1024
+
+
+def reverse(index, size):
+    bits = size.bit_length() - 1
+    return sum(((index >> bit) & 1) << (bits - 1 - bit) for bit in range(bits))
 
 
 def pack_kernel(k_ref, v_ref, o_ref):
     slots, span, width = k_ref.shape
+    heads = width // HEAD
     for pair in range(width // (2 * HEAD)):
         low = pair * 2 * HEAD
         for slot in range(slots):
             rows = pl.ds(slot * span, span)
             k = k_ref[slot, :, low : low + 2 * HEAD]
             v = v_ref[slot, :, low : low + 2 * HEAD]
-            o_ref[2 * pair, rows, :] = jnp.concatenate([k[:, :HEAD], v[:, :HEAD]], axis=1)
-            o_ref[2 * pair + 1, rows, :] = jnp.concatenate([k[:, HEAD:], v[:, HEAD:]], axis=1)
+            o_ref[reverse(2 * pair, heads), 0, rows, :] = jnp.concatenate([k[:, :HEAD], v[:, :HEAD]], axis=1)
+            o_ref[reverse(2 * pair + 1, heads), 0, rows, :] = jnp.concatenate([k[:, HEAD:], v[:, HEAD:]], axis=1)
 
 
 def unpack_kernel(i_ref, o_ref):
     slots, span, width = o_ref.shape
+    heads = width // HEAD
     for pair in range(width // (2 * HEAD)):
         low = pair * 2 * HEAD
-        even = i_ref[2 * pair, :span, :]
-        odd = i_ref[2 * pair + 1, :span, :]
+        even = i_ref[reverse(2 * pair, heads), 0, :span, :]
+        odd = i_ref[reverse(2 * pair + 1, heads), 0, :span, :]
         for slot in range(slots):
             side = slice(slot * HEAD, (slot + 1) * HEAD)
             o_ref[slot, :, low : low + 2 * HEAD] = jnp.concatenate([even[:, side], odd[:, side]], axis=1)
@@ -63,7 +71,7 @@
         in_specs=[smem, smem, vmem, vmem],
         out_specs=vmem,
         out_shape=jax.ShapeDtypeStruct((ranks, 1, questions * targets + 128), F32),
-        compiler_params=pltpu.CompilerParams(vmem_limit_bytes=VMEM_LIMIT),
+        compiler_params=pltpu.CompilerParams(vmem_limit_bytes=ALL_VMEM),
         cost_estimate=pl.CostEstimate(
             flops=2 * questions * size * targets * ranks,
             bytes_accessed=6 * questions * size * targets,
@@ -76,31 +84,37 @@
 def pack(keys, values, spare):
     slots, span, width = keys.shape
     heads, rows = width // HEAD, slots * span + spare
+    steps = heads // PACK_HEADS
     part = pl.BlockSpec((slots, span, PACK_HEADS * HEAD), lambda i: (0, 0, i))
     return pl.pallas_call(
         pack_kernel,
-        grid=(heads // PACK_HEADS,),
+        grid=(steps,),
         in_specs=[part, part],
-        out_specs=pl.BlockSpec((PACK_HEADS, rows, 2 * HEAD), lambda i: (i, 0, 0)),
-        out_shape=jax.ShapeDtypeStruct((heads, rows, 2 * HEAD), keys.dtype),
+        out_specs=pl.BlockSpec(
+            (PACK_HEADS, 1, rows, 2 * HEAD), lambda i: (0, reverse(i, steps), 0, 0)
+        ),
+        out_shape=jax.ShapeDtypeStruct((PACK_HEADS, steps, rows, 2 * HEAD), keys.dtype),
         compiler_params=pltpu.CompilerParams(vmem_limit_bytes=VMEM_LIMIT),
         cost_estimate=pl.CostEstimate(flops=0, bytes_accessed=8 * slots * span * width, transcendentals=0),
         name="pack",
-    )(keys, values)
+    )(keys, values).reshape(heads, rows, 2 * HEAD)
 
 
 def unpack(table, slots, span):
     heads, rows, _ = table.shape
+    steps = heads // PACK_HEADS
     return pl.pallas_call(
         unpack_kernel,
-        grid=(heads // PACK_HEADS,),
-        in_specs=[pl.BlockSpec((PACK_HEADS, rows, 2 * HEAD), lambda i: (i, 0, 0))],
+        grid=(steps,),
+        in_specs=[
+            pl.BlockSpec((PACK_HEADS, 1, rows, 2 * HEAD), lambda i: (0, reverse(i, steps), 0, 0))
+        ],
         out_specs=pl.BlockSpec((slots, span, PACK_HEADS * HEAD), lambda i: (0, 0, i)),
         out_shape=jax.ShapeDtypeStruct((slots, span, heads * HEAD), table.dtype),
         compiler_params=pltpu.CompilerParams(vmem_limit_bytes=VMEM_LIMIT),
         cost_estimate=pl.CostEstimate(flops=0, bytes_accessed=4 * slots * span * heads * HEAD, transcendentals=0),
         name="unpack",
-    )(table)
+    )(table.reshape(PACK_HEADS, steps, rows, 2 * HEAD))
 
 
 STATS_CHUNK = 4
@@ -319,8 +333,8 @@
             scratch_shapes=[pltpu.VMEM((keys, 2 * HEAD), BF16), pltpu.VMEM((keys, targets), BF16)],
         ),
         out_shape=[
-            jax.ShapeDtypeStruct((peers, size, questions * piece), F32),
-            jax.ShapeDtypeStruct(out, BF16),
+            pltpu.HBM((peers, size, questions * piece), F32),
+            pltpu.HBM(out, BF16),
         ],
         compiler_params=pltpu.CompilerParams(vmem_limit_bytes=VMEM_LIMIT),
         cost_estimate=pl.CostEstimate(
@@ -352,7 +366,7 @@
             ],
             out_specs=pl.BlockSpec(out, lambda q, c: (0, 0, 0)),
         ),
-        out_shape=jax.ShapeDtypeStruct(out, BF16),
+        out_shape=pltpu.HBM(out, BF16),
         compiler_params=pltpu.CompilerParams(vmem_limit_bytes=VMEM_LIMIT),
         cost_estimate=pl.CostEstimate(
             flops=16 * questions * targets * keys * HEAD,
@@ -380,7 +394,13 @@
 
 
 def exchange(x, axis):
-    return lax.all_to_all(x, axis, split_axis=0, concat_axis=0, tiled=True)
+    order = None
+    if axis == "grp":
+        size = lax.axis_size(axis)
+        order = [[reverse(i, size) for i in range(size)]]
+    return lax.all_to_all(
+        x, axis, split_axis=0, concat_axis=0, tiled=True, axis_index_groups=order
+    )
 
 
 def local(

time: 216 us -> 211 us (0.977)
  starting transfers between devices: 64.4 us -> 56.5 us
  waiting for transfers between devices: 103 us -> 109 us
  local copies, waits for them, and re-layouts: 13.6 us -> 8.56 us
  Pallas kernels: 22 us -> 24.8 us
    all_to_all x5, starting transfers between devices: 56.4 us -> 48.7 us  [exchange(): lax.all_to_all(x, axis, split_axis=0, concat_axis=0, tiled=True, axis_ind...]
    all_to_all x5, waiting for transfers between devices: 98.3 us -> 104 us  [exchange(): lax.all_to_all(x, axis, split_axis=0, concat_axis=0, tiled=True, axis_ind...]
    unnamed x46 -> x34, local copies, waits for them, and re-layouts: 10.3 us -> 5.21 us
  transfers between devices with their start and end apart: 8 -> 8, of which waited for: 7 -> 7; matrix products, arithmetic and copies ran while one was open for 0% -> 1% of each run, Pallas kernels for 5% -> 6%
where the time goes in v4:
time: 211 us
  waiting for transfers between devices  109 us (52%)
  starting transfers between devices  56.5 us (27%)
  Pallas kernels  24.8 us (12%)
  blocking collectives  8.6 us (4%)
  local copies, waits for them, and re-layouts  8.56 us (4%)
    all_to_all x5, waiting for transfers between devices, exchange(): lax.all_to_all(x, axis, split_axis=0, concat_axis=0, tiled=True, axis_ind...  104 us
    all_to_all x5, starting transfers between devices, exchange(): lax.all_to_all(x, axis, split_axis=0, concat_axis=0, tiled=True, axis_ind...  48.7 us
    all_to_all x1, blocking collectives, exchange(): lax.all_to_all(x, axis, split_axis=0, concat_axis=0, tiled=True, axis_ind...  8.6 us
    ppermute x3, starting transfers between devices, scatter_sum_tp(): lax.ppermute(sent, 'tp', [(i, (i + k) % size) for i in range(size)])  7.84 us
    pallas_call x1, Pallas kernels, query_value_grads(): pl.pallas_call(functools.partial(query_value_kernel, per_question, slots,...  7.13 us
    pallas_call x1, Pallas kernels, key_grads(): pl.pallas_call(functools.partial(key_kernel, per_question, slots, span),...  5.75 us
    unnamed x34, local copies, waits for them, and re-layouts  5.21 us
    ppermute x3, waiting for transfers between devices, scatter_sum_tp(): lax.ppermute(sent, 'tp', [(i, (i + k) % size) for i in range(size)])  4.54 us
  transfers between devices with their start and end apart: 8, of which 7 were waited for; matrix products, arithmetic and copies ran while one was open for 1% of the time, Pallas kernels for 6%

profile of v4, /device:TPU:1, one launch (start us, length us, event | category | flops | bytes accessed | tf_op | source)
XLA Modules:
  0.0 210.5 jit_solution(13432044482775898703)
XLA Ops:
  1.3 1.9 latent_parts.1
  3.2 17.1 %all-to-all-start = ((f32[64,1,1152]{2,1,0:T(1,128)}), f32[64,1,1152]{2,1,0:T(1,128)S(1)}, u32[]{:S(2)}, u32[]{:S(2)}) async-start(f32[64,1,1152]{2,1,0:T(1,128)} %latent_parts.1), calls=%async_computation | async-start | bytes 589824 | tf_op jit(solution)/shard_map/all_to_all | solution.py:401
  20.3 1.2 copy-done
  21.6 1.2 copy-done.1
  22.8 2.5 %pack.1 = bf16[16,4,136,128]{3,2,1,0:T(8,128)(2,1)} custom-call(bf16[2,64,4096]{2,1,0:T(8,128)(2,1)S(1)} %copy-done, bf16[2,64,4096]{2,1,0:T(8,128)(2,1)S(1)} %copy-done.1), custom_call_target="tpu_custom_call" | custom-call | bytes 4194304 | tf_op jit(solution)/shard_map/pack/pallas_call | solution.py:89
  25.2 9.2 %all-to-all-done = f32[64,1,1152]{2,1,0:T(1,128)S(1)} async-done(((f32[64,1,1152]{2,1,0:T(1,128)}), f32[64,1,1152]{2,1,0:T(1,128)S(1)}, u32[]{:S(2)}, u32[]{:S(2)}) %all-to-all-start) | async-done | bytes 294944 | tf_op jit(solution)/shard_map/all_to_all | solution.py:401
  34.5 0.7 broadcast_dynamic-update-slice_fusion.1
  35.3 5.4 %all-to-all-start.1 = ((bf16[64,136,128]{2,1,0:T(8,128)(2,1)}), bf16[64,136,128]{2,1,0:T(8,128)(2,1)S(1)}, u32[]{:S(2)}, u32[]{:S(2)}) async-start(bf16[64,136,128]{2,1,0:T(8,128)(2,1)} %broadcast_dynamic-update-slice_fusion.1), calls=%async_computation.1 | async-start | bytes 4456448 | tf_op jit(solution)/shard_map/all_to_all | solution.py:401
  41.4 54.5 %all-to-all-done.1.t_ref = bf16[64,136,128]{2,1,0:T(8,128)(2,1)S(1)} async-done(((bf16[64,136,128]{2,1,0:T(8,128)(2,1)}), bf16[64,136,128]{2,1,0:T(8,128)(2,1)S(1)}, u32[]{:S(2)}, u32[]{:S(2)}) %all-to-all-start.1) | async-done | bytes 2228256 | tf_op jit(solution)/shard_map/all_to_all | solution.py:401
  96.3 3.7 %stats.1 = f32[4,8,256]{2,1,0:T(8,128)S(1)} custom-call(s32[112]{0:T(128)S(1)} %select_reduce_fusion.chosen_ref, bf16[4,64,256]{2,1,0:T(8,128)(2,1)S(1)} %fusion.1.q_ref, bf16[4,64,256]{2,1,0:T(8,128)(2,1)S(1)} %select_bitcast_fusion.u_ref, bf16[64,136,128]{2,1,0:T(8,128)(2,1)S(1)} %all-to-all-done.1.t_ref), custom_call_target="tpu_custom_call" | custom-call | flops 939524096 | bytes 2228224 | tf_op jit(solution)/shard_map/stats/pallas_call | solution.py:289
  100.0 8.6 %all_to_all.30.s_ref = f32[4,4,8,256]{3,2,1,0:T(8,128)S(1)} all-to-all(f32[4,4,8,256]{3,2,1,0:T(8,128)S(1)} %broadcast_in_dim.35), channel_id=1, replica_groups=mesh['sect'=2,'grp'=64,'tp'=4] {'tp'}, dimensions={0} | all-to-all | bytes 262144 | tf_op jit(solution)/shard_map/all_to_all | solution.py:401
  108.6 7.1 %query_value_grads.1 = (f32[4,64,256]{2,1,0:T(8,128)}, bf16[64,80,128]{2,1,0:T(8,128)(2,1)}) custom-call(s32[112]{0:T(128)S(1)} %select_reduce_fusion.chosen_ref, bf16[4,64,256]{2,1,0:T(8,128)(2,1)S(1)} %fusion.1.q_ref, bf16[4,64,256]{2,1,0:T(8,128)(2,1)S(1)} %select_bitcast_fusion.u_ref, bf16[64,64]{1,0:T(8,128)(2,1)S(1)} %copy-done.8, ...), custom_call_target="tpu_custom_call" | custom-call | flops 2818572288 | bytes 4456448 | tf_op jit(solution)/shard_map/query_value_grads/pallas_call | solution.py:317
  115.8 8.2 %all-to-all-start.3 = ((bf16[64,80,128]{2,1,0:T(8,128)(2,1)}), bf16[64,80,128]{2,1,0:T(8,128)(2,1)S(1)}, u32[]{:S(2)}, u32[]{:S(2)}) async-start(bf16[64,80,128]{2,1,0:T(8,128)(2,1)} %get-tuple-element.10), calls=%async_computation.3 | async-start | bytes 2621440 | tf_op jit(solution)/shard_map/all_to_all | solution.py:401
  123.9 0.9 copy-done.3
  124.8 0.9 copy-done.5
  125.7 0.9 copy-done.7
  126.6 5.8 %key_grads.1 = bf16[64,72,128]{2,1,0:T(8,128)(2,1)} custom-call(s32[112]{0:T(128)S(1)} %select_reduce_fusion.chosen_ref, bf16[4,64,256]{2,1,0:T(8,128)(2,1)S(1)} %copy-done.3, bf16[4,64,256]{2,1,0:T(8,128)(2,1)S(1)} %copy-done.5, f32[4,4,8,256]{3,2,1,0:T(8,128)S(1)} %copy-done.7, bf16[64,136,128]{2,1,0:T(8,128)(2,1)S(1)} %all-to-all-done.1.t_ref), custom_call_target="tpu_custom_call" | custom-call | flops 1879048192 | bytes 4456448 | tf_op jit(solution)/shard_map/key_grads/pallas_call | solution.py:356
  132.4 23.2 %all-to-all-done.3 = bf16[64,80,128]{2,1,0:T(8,128)(2,1)S(1)} async-done(((bf16[64,80,128]{2,1,0:T(8,128)(2,1)}), bf16[64,80,128]{2,1,0:T(8,128)(2,1)S(1)}, u32[]{:S(2)}, u32[]{:S(2)}) %all-to-all-start.3) | async-done | bytes 1310752 | tf_op jit(solution)/shard_map/all_to_all | solution.py:401
  155.7 0.7 broadcast_dynamic-update-slice_fusion
  156.4 7.6 %all-to-all-start.4 = ((bf16[64,72,128]{2,1,0:T(8,128)(2,1)}), bf16[64,72,128]{2,1,0:T(8,128)(2,1)S(1)}, u32[]{:S(2)}, u32[]{:S(2)}) async-start(bf16[64,72,128]{2,1,0:T(8,128)(2,1)} %broadcast_dynamic-update-slice_fusion), calls=%async_computation.4 | async-start | bytes 2359296 | tf_op jit(solution)/shard_map/all_to_all | solution.py:401
  164.2 2.8 %collective-permute-start.2 = (f32[64,256]{1,0:T(8,128)S(1)}, f32[64,256]{1,0:T(8,128)S(1)}, u32[]{:S(2)}, u32[]{:S(2)}) collective-permute-start(f32[64,256]{1,0:T(8,128)S(1)} %get-tuple-element.14), channel_id=1, source_target_pairs={{0,3},{1,0},{2,1},{3,2},{4,7},{5,4},{6,5},{7,6},{8,11},{9,8},{10,9... | collective-permute-start | bytes 196616 | tf_op jit(solution)/shard_map/ppermute | solution.py:392
  167.0 3.1 %collective-permute-start.1 = (f32[64,256]{1,0:T(8,128)S(1)}, f32[64,256]{1,0:T(8,128)S(1)}, u32[]{:S(2)}, u32[]{:S(2)}) collective-permute-start(f32[64,256]{1,0:T(8,128)S(1)} %get-tuple-element.15), channel_id=1, source_target_pairs={{0,2},{1,3},{2,0},{3,1},{4,6},{5,7},{6,4},{7,5},{8,10},{9,11},{10,... | collective-permute-start | bytes 196616 | tf_op jit(solution)/shard_map/ppermute | solution.py:392
  170.1 1.9 collective-permute-start
  172.1 1.7 collective-permute-done.1
  173.8 2.8 %collective-permute-done = f32[64,256]{1,0:T(8,128)S(1)} collective-permute-done((f32[64,256]{1,0:T(8,128)S(1)}, f32[64,256]{1,0:T(8,128)S(1)}, u32[]{:S(2)}, u32[]{:S(2)}) %collective-permute-start) | collective-permute-done | bytes 65568 | tf_op jit(solution)/shard_map/ppermute | solution.py:392
  177.0 14.7 %all-to-all-done.4 = bf16[64,72,128]{2,1,0:T(8,128)(2,1)S(1)} async-done(((bf16[64,72,128]{2,1,0:T(8,128)(2,1)}), bf16[64,72,128]{2,1,0:T(8,128)(2,1)S(1)}, u32[]{:S(2)}, u32[]{:S(2)}) %all-to-all-start.4) | async-done | bytes 1179680 | tf_op jit(solution)/shard_map/all_to_all | solution.py:401
  192.2 0.7 broadcast_in_dim.60
  192.9 10.3 %all-to-all-start.5 = ((f32[8,64,128]{2,1,0:T(8,128)}), f32[8,64,128]{2,1,0:T(8,128)S(1)}, u32[]{:S(2)}, u32[]{:S(2)}) async-start(f32[8,64,128]{2,1,0:T(8,128)} %broadcast_in_dim.60), calls=%async_computation.5 | async-start | bytes 524288 | tf_op jit(solution)/shard_map/all_to_all | solution.py:401
  203.2 1.9 unpack.3
  205.2 1.9 unpack.2
  207.1 2.7 %all-to-all-done.5 = f32[8,64,128]{2,1,0:T(8,128)S(1)} async-done(((f32[8,64,128]{2,1,0:T(8,128)}), f32[8,64,128]{2,1,0:T(8,128)S(1)}, u32[]{:S(2)}, u32[]{:S(2)}) %all-to-all-start.5) | async-done | bytes 262176 | tf_op jit(solution)/shard_map/all_to_all | solution.py:401
  209.8 0.7 fusion.15
  (56 shorter events, 2.1 us)
Async XLA Ops:
  3.2 31.2 %all-to-all-start = ((f32[64,1,1152]{2,1,0:T(1,128)}), f32[64,1,1152]{2,1,0:T(1,128)S(1)}, u32[]{:S(2)}, u32[]{:S(2)}) async-start(f32[64,1,1152]{2,1,0:T(1,128)} %latent_parts.1), calls=%async_computation | async-start | bytes 589824 | tf_op jit(solution)/shard_map/all_to_all | solution.py:401
  20.3 1.2 copy-start
  21.6 1.2 copy-start.1
  35.3 5.4 %copy-start.16 = (s32[4]{0:T(128)S(1)}, s32[4]{0:T(128)}, u32[]{:S(2)}) copy-start(s32[4]{0:T(128)} %param.19) | copy-start | bytes 52
  35.3 5.5 %copy-start.15 = (bf16[4,256,64]{1,2,0:T(8,128)(2,1)S(1)}, bf16[4,256,64]{1,2,0:T(8,128)(2,1)}, u32[]{:S(2)}) copy-start(bf16[4,256,64]{1,2,0:T(8,128)(2,1)} %param.13) | copy-start | bytes 393220
  35.3 60.7 %copy-start.8 = (bf16[64,64]{1,0:T(8,128)(2,1)S(1)}, bf16[64,64]{1,0:T(8,128)(2,1)}, u32[]{:S(2)}) copy-start(bf16[64,64]{1,0:T(8,128)(2,1)} %w_ref.1) | copy-start | bytes 24580
  35.3 60.7 %copy-start.14 = (bf16[4,256,64]{1,2,0:T(8,128)(2,1)S(1)}, bf16[4,256,64]{1,2,0:T(8,128)(2,1)}, u32[]{:S(2)}) copy-start(bf16[4,256,64]{1,2,0:T(8,128)(2,1)} %param.12) | copy-start | bytes 393220
  35.3 60.6 %all-to-all-start.1 = ((bf16[64,136,128]{2,1,0:T(8,128)(2,1)}), bf16[64,136,128]{2,1,0:T(8,128)(2,1)S(1)}, u32[]{:S(2)}, u32[]{:S(2)}) async-start(bf16[64,136,128]{2,1,0:T(8,128)(2,1)} %broadcast_dynamic-update-slice_fusion.1), calls=%async_computation.1 | async-start | bytes 4456448 | tf_op jit(solution)/shard_map/all_to_all | solution.py:401
  40.8 67.8 %copy-start.4 = (bf16[4,64,256]{2,1,0:T(8,128)(2,1)}, bf16[4,64,256]{2,1,0:T(8,128)(2,1)S(1)}, u32[]{:S(2)}) copy-start(bf16[4,64,256]{2,1,0:T(8,128)(2,1)S(1)} %select_bitcast_fusion.u_ref) | copy-start | bytes 393220
  96.0 4.0 %copy-start.9 = (bf16[64,4,256]{2,1,0:T(4,128)(2,1)}, bf16[64,4,256]{2,1,0:T(4,128)(2,1)S(1)}, u32[]{:S(2)}) copy-start(bf16[64,4,256]{2,1,0:T(4,128)(2,1)S(1)} %reshape.83) | copy-start | bytes 393220
  96.3 12.3 %copy-start.2 = (bf16[4,64,256]{2,1,0:T(8,128)(2,1)}, bf16[4,64,256]{2,1,0:T(8,128)(2,1)S(1)}, u32[]{:S(2)}) copy-start(bf16[4,64,256]{2,1,0:T(8,128)(2,1)S(1)} %fusion.1.q_ref) | copy-start | bytes 393220
  108.6 7.1 %copy-start.6 = (f32[4,4,8,256]{3,2,1,0:T(8,128)}, f32[4,4,8,256]{3,2,1,0:T(8,128)S(1)}, u32[]{:S(2)}) copy-start(f32[4,4,8,256]{3,2,1,0:T(8,128)S(1)} %all_to_all.30.s_ref) | copy-start | bytes 393220
  115.8 39.9 %all-to-all-start.3 = ((bf16[64,80,128]{2,1,0:T(8,128)(2,1)}), bf16[64,80,128]{2,1,0:T(8,128)(2,1)S(1)}, u32[]{:S(2)}, u32[]{:S(2)}) async-start(bf16[64,80,128]{2,1,0:T(8,128)(2,1)} %get-tuple-element.10), calls=%async_computation.3 | async-start | bytes 2621440 | tf_op jit(solution)/shard_map/all_to_all | solution.py:401
  123.9 0.9 copy-start.3
  124.8 0.9 copy-start.5
  125.7 0.9 copy-start.7
  155.7 8.4 %copy-start.12 = (f32[4,64,256]{2,1,0:T(8,128)S(1)}, f32[4,64,256]{2,1,0:T(8,128)}, u32[]{:S(2)}) copy-start(f32[4,64,256]{2,1,0:T(8,128)} %get-tuple-element.9) | copy-start | bytes 786436
  156.4 15.6 %copy-start.10 = (bf16[64,4,256]{2,1,0:T(4,128)(2,1)S(1)}, bf16[64,4,256]{2,1,0:T(4,128)(2,1)}, u32[]{:S(2)}) copy-start(bf16[64,4,256]{2,1,0:T(4,128)(2,1)} %copy-done.9) | copy-start | bytes 393220
  156.4 35.4 %all-to-all-start.4 = ((bf16[64,72,128]{2,1,0:T(8,128)(2,1)}), bf16[64,72,128]{2,1,0:T(8,128)(2,1)S(1)}, u32[]{:S(2)}, u32[]{:S(2)}) async-start(bf16[64,72,128]{2,1,0:T(8,128)(2,1)} %broadcast_dynamic-update-slice_fusion), calls=%async_computation.4 | async-start | bytes 2359296 | tf_op jit(solution)/shard_map/all_to_all | solution.py:401
  164.1 27.8 %copy-start.11 = (bf16[4,256,64]{1,2,0:T(8,128)(2,1)S(1)}, bf16[4,256,64]{1,2,0:T(8,128)(2,1)}, u32[]{:S(2)}) copy-start(bf16[4,256,64]{1,2,0:T(8,128)(2,1)} %param.14) | copy-start | bytes 393220
  164.2 7.9 %collective-permute-start.2 = (f32[64,256]{1,0:T(8,128)S(1)}, f32[64,256]{1,0:T(8,128)S(1)}, u32[]{:S(2)}, u32[]{:S(2)}) collective-permute-start(f32[64,256]{1,0:T(8,128)S(1)} %get-tuple-element.14), channel_id=1, source_target_pairs={{0,3},{1,0},{2,1},{3,2},{4,7},{5,4},{6,5},{7,6},{8,11},{9,8},{10,9... | collective-permute-start | bytes 196616 | tf_op jit(solution)/shard_map/ppermute | solution.py:392
  167.0 6.8 %collective-permute-start.1 = (f32[64,256]{1,0:T(8,128)S(1)}, f32[64,256]{1,0:T(8,128)S(1)}, u32[]{:S(2)}, u32[]{:S(2)}) collective-permute-start(f32[64,256]{1,0:T(8,128)S(1)} %get-tuple-element.15), channel_id=1, source_target_pairs={{0,2},{1,3},{2,0},{3,1},{4,6},{5,7},{6,4},{7,5},{8,10},{9,11},{10,... | collective-permute-start | bytes 196616 | tf_op jit(solution)/shard_map/ppermute | solution.py:392
  170.1 6.5 %collective-permute-start = (f32[64,256]{1,0:T(8,128)S(1)}, f32[64,256]{1,0:T(8,128)S(1)}, u32[]{:S(2)}, u32[]{:S(2)}) collective-permute-start(f32[64,256]{1,0:T(8,128)S(1)} %get-tuple-element.13), channel_id=1, source_target_pairs={{0,1},{1,2},{2,3},{3,0},{4,5},{5,6},{6,7},{7,4},{8,9},{9,10},{10,1... | collective-permute-start | bytes 196616 | tf_op jit(solution)/shard_map/ppermute | solution.py:392
  176.7 28.4 %copy-start.13 = (bf16[64,256]{0,1:T(8,128)(2,1)}, bf16[64,256]{0,1:T(8,128)(2,1)S(1)}, u32[]{:S(2)}) copy-start(bf16[64,256]{0,1:T(8,128)(2,1)S(1)} %copy.31) | copy-start | bytes 98308
  192.9 16.9 %all-to-all-start.5 = ((f32[8,64,128]{2,1,0:T(8,128)}), f32[8,64,128]{2,1,0:T(8,128)S(1)}, u32[]{:S(2)}, u32[]{:S(2)}) async-start(f32[8,64,128]{2,1,0:T(8,128)} %broadcast_in_dim.60), calls=%async_computation.5 | async-start | bytes 524288 | tf_op jit(solution)/shard_map/all_to_all | solution.py:401

commit v5 on v4

v5 whole, which is shorter than its diff:
```python
import functools

import jax
import jax.numpy as jnp
from jax import lax
from jax.experimental import pallas as pl
from jax.experimental.pallas import tpu as pltpu
from jax.sharding import PartitionSpec as P

HEAD = 64
BF16 = jnp.bfloat16
F32 = jnp.float32
VMEM_LIMIT = 32 * 1024 * 1024
ALL_VMEM = 62 * 1024 * 1024


def reverse(index, size):
    bits = size.bit_length() - 1
    return sum(((index >> bit) & 1) << (bits - 1 - bit) for bit in range(bits))


def pack_rows(x_ref, o_ref):
    slots, span, width = x_ref.shape
    heads = width // HEAD
    for pair in range(width // (2 * HEAD)):
        low = pair * 2 * HEAD
        parts = [x_ref[slot, :, low : low + 2 * HEAD] for slot in range(slots)]
        for side in range(2):
            cut = slice(side * HEAD, (side + 1) * HEAD)
            o_ref[reverse(2 * pair + side, heads), 0, :span, :] = jnp.concatenate(
                [part[:, cut] for part in parts], axis=1
            )


def pack_key_kernel(k_ref, o_ref):
    pack_rows(k_ref, o_ref)


def pack_value_kernel(owner_ref, counts_ref, down_ref, hidden_ref, v_ref, o_ref):
    pack_rows(v_ref, o_ref)
    span = v_ref.shape[1]
    questions, _, targets = hidden_ref.shape
    blocks, steps = o_ref.shape[0], pl.num_programs(0)
    halves = targets // 128
    lanes = lax.broadcasted_iota(jnp.int32, (8, 128), 1)
    tags = jnp.zeros(lanes.shape, jnp.int32)
    for slot in range(owner_ref.shape[0]):
        tag = jnp.where(slot < counts_ref[0], owner_ref[slot], questions)
        tags = jnp.where(lanes == slot, tag, tags)
    tags = tags.astype(F32)
    down = down_ref[...]
    bands = down.shape[1] // 8
    per_band = blocks // bands
    step = reverse(pl.program_id(0), PACK_STEPS)
    for turn in range(per_band):
        part = turn * steps + step
        start = pl.multiple_of(lax.rem(part, halves) * 128, 128)
        latent = lax.dot_general(
            down,
            hidden_ref[part // halves, :, pl.ds(start, 128)],
            (((0,), (0,)), ((), ())),
            preferred_element_type=F32,
        )
        for band in range(bands):
            tile = latent[band * 8 : (band + 1) * 8]
            o_ref[band * per_band + turn, 0, span : span + 16, :] = jnp.concatenate(
                [tile, tags], axis=0
            ).astype(o_ref.dtype)


def unpack_kernel(i_ref, o_ref):
    slots, span, width = o_ref.shape
    heads = width // HEAD
    for pair in range(width // (2 * HEAD)):
        low = pair * 2 * HEAD
        even = i_ref[reverse(2 * pair, heads), 0, :span, :]
        odd = i_ref[reverse(2 * pair + 1, heads), 0, :span, :]
        for slot in range(slots):
            side = slice(slot * HEAD, (slot + 1) * HEAD)
            o_ref[slot, :, low : low + 2 * HEAD] = jnp.concatenate([even[:, side], odd[:, side]], axis=1)


PACK_STEPS = 4


def pack_specs(slots, span, width, rows):
    heads = width // HEAD
    blocks = heads // PACK_STEPS
    part = pl.BlockSpec((slots, span, blocks * HEAD), lambda i: (0, 0, i))
    table = pl.BlockSpec(
        (blocks, 1, rows, slots * HEAD), lambda i: (0, reverse(i, PACK_STEPS), 0, 0)
    )
    return part, table, (blocks, PACK_STEPS, rows, slots * HEAD)


def pack_keys(keys, spare):
    slots, span, width = keys.shape
    part, table, shape = pack_specs(slots, span, width, span + spare)
    packed = pl.pallas_call(
        pack_key_kernel,
        grid=(PACK_STEPS,),
        in_specs=[part],
        out_specs=table,
        out_shape=jax.ShapeDtypeStruct(shape, keys.dtype),
        compiler_params=pltpu.CompilerParams(vmem_limit_bytes=VMEM_LIMIT),
        cost_estimate=pl.CostEstimate(flops=0, bytes_accessed=4 * keys.size, transcendentals=0),
        name="pack_keys",
    )(keys)
    return packed.reshape(width // HEAD, span + spare, slots * HEAD)


def pack_values(owner, counts, down_weight, hidden_t, values):
    slots, span, width = values.shape
    part, table, shape = pack_specs(slots, span, width, span + 16)
    smem = pl.BlockSpec(memory_space=pltpu.SMEM)
    packed = pl.pallas_call(
        pack_value_kernel,
        grid=(PACK_STEPS,),
        in_specs=[
            smem,
            smem,
            pl.BlockSpec(down_weight.shape, lambda i: (0, 0)),
            pl.BlockSpec(hidden_t.shape, lambda i: (0, 0, 0)),
            part,
        ],
        out_specs=table,
        out_shape=jax.ShapeDtypeStruct(shape, values.dtype),
        compiler_params=pltpu.CompilerParams(vmem_limit_bytes=ALL_VMEM),
        cost_estimate=pl.CostEstimate(
            flops=2 * hidden_t.size * down_weight.shape[1],
            bytes_accessed=4 * values.size,
            transcendentals=0,
        ),
        name="pack_values",
    )(owner, counts, down_weight, hidden_t, values)
    return packed.reshape(width // HEAD, span + 16, slots * HEAD)


def unpack(table, slots, span):
    heads, rows, _ = table.shape
    part, blocks, shape = pack_specs(slots, span, heads * HEAD, rows)
    return pl.pallas_call(
        unpack_kernel,
        grid=(PACK_STEPS,),
        in_specs=[blocks],
        out_specs=part,
        out_shape=jax.ShapeDtypeStruct((slots, span, heads * HEAD), table.dtype),
        compiler_params=pltpu.CompilerParams(vmem_limit_bytes=VMEM_LIMIT),
        cost_estimate=pl.CostEstimate(flops=0, bytes_accessed=4 * slots * span * heads * HEAD, transcendentals=0),
        name="unpack",
    )(table.reshape(shape))


STATS_CHUNK = 4
GRAD_CHUNK = 14


def two_sided(q_ref, u_ref):
    q, u = q_ref[0], u_ref[0]
    zero = jnp.zeros_like(q)
    return jnp.concatenate(
        [jnp.concatenate([q, zero], axis=1), jnp.concatenate([zero, u], axis=1)], axis=0
    )


def gathered(chosen_ref, k_ref, v_ref, slots, span, first):
    blocks = []
    for i in range(STATS_CHUNK):
        slot = chosen_ref[first + i]
        device, second = slot // slots, lax.rem(slot, slots) == 1
        k, v = k_ref[device, :span, :], v_ref[device, :span, :]
        left = jnp.concatenate([k[:, :HEAD], v[:, :HEAD]], axis=1)
        right = jnp.concatenate([k[:, HEAD:], v[:, HEAD:]], axis=1)
        blocks.append(jnp.where(second, right, left))
    return jnp.concatenate(blocks, axis=0)


def stats_kernel(
    per_question, slots, span, chosen_ref, q_ref, u_ref, k_ref, v_ref, o_ref, rows_ref
):
    question = pl.program_id(0)
    targets = q_ref.shape[2]
    both = two_sided(q_ref, u_ref)
    top = jnp.full((1, targets), -jnp.inf, F32)
    mass = jnp.zeros((1, targets), F32)
    dot = jnp.zeros((1, targets), F32)
    for chunk in range(per_question // STATS_CHUNK):
        first = question * per_question + chunk * STATS_CHUNK
        rows = gathered(chosen_ref, k_ref, v_ref, slots, span, first)
        rows_ref[0, chunk * STATS_CHUNK * span : (chunk + 1) * STATS_CHUNK * span, :] = rows
        prod = jnp.dot(rows, both, preferred_element_type=F32)
        scores, prob_grad = prod[:, :targets], prod[:, targets:]
        new_top = jnp.maximum(top, jnp.max(scores, axis=0, keepdims=True))
        scale = jnp.exp(top - new_top)
        exp_scores = jnp.exp(scores - new_top)
        mass = mass * scale + jnp.sum(exp_scores, axis=0, keepdims=True)
        dot = dot * scale + jnp.sum(exp_scores * prob_grad, axis=0, keepdims=True)
        top = new_top
    o_ref[0] = jnp.concatenate([top, mass, dot, jnp.zeros((5, targets), F32)], axis=0)


def row_stats(s_ref):
    members = s_ref.shape[0]
    tops = [s_ref[i, 0, 0:1, :] for i in range(members)]
    top = functools.reduce(jnp.maximum, tops)
    scales = [jnp.exp(t - top) for t in tops]
    inverse = 1.0 / sum(s_ref[i, 0, 1:2, :] * scales[i] for i in range(members))
    delta = sum(s_ref[i, 0, 2:3, :] * scales[i] for i in range(members)) * inverse
    return top, inverse, delta


def chunk_products(rows, both, stats):
    top, inverse, delta = stats
    targets = top.shape[1]
    prod = jnp.dot(rows, both, preferred_element_type=F32)
    scores, prob_grad = prod[:, :targets], prod[:, targets:]
    weights = jnp.exp(scores - top) * inverse
    score_grad = (weights * (prob_grad - delta)).astype(BF16)
    return weights, score_grad


def store_half(o_ref, slot, slots, value):
    device, span = slot // slots, value.shape[0]
    lanes = lax.broadcasted_iota(jnp.int32, value.shape, 1)
    old = o_ref[device, :span, :]
    o_ref[device, :span, :] = jnp.where(lanes // HEAD == lax.rem(slot, slots), value, old)


def query_value_kernel(
    per_question,
    slots,
    span,
    chosen_ref,
    q_ref,
    u_ref,
    w_ref,
    s_ref,
    rows_ref,
    dq_ref,
    o_ref,
    grad_ref,
):
    question = pl.program_id(0)
    targets = q_ref.shape[2]
    peers, _, pair_width = dq_ref.shape
    piece = targets // peers

    @pl.when(question == 0)
    def _():
        o_ref[...] = jnp.zeros_like(o_ref)

    both = two_sided(q_ref, u_ref)
    upstream = jnp.concatenate([u_ref[0]] * slots, axis=0)
    stats = row_stats(s_ref)
    size = GRAD_CHUNK * span
    last = (((1,), (1,)), ((), ()))
    for chunk in range(per_question // GRAD_CHUNK):
        first = question * per_question + chunk * GRAD_CHUNK
        rows = rows_ref[0, chunk * size : (chunk + 1) * size, :]
        weights, score_grad = chunk_products(rows, both, stats)
        grad_ref[chunk * size : (chunk + 1) * size, :] = score_grad
        out = lax.dot_general(
            weights.astype(BF16), upstream, last, preferred_element_type=F32
        ).astype(BF16)
        for i in range(GRAD_CHUNK):
            store_half(o_ref, chosen_ref[first + i], slots, out[i * span : (i + 1) * span])
    dq = lax.dot_general(
        rows_ref[0], grad_ref[...], (((0,), (0,)), ((), ())), preferred_element_type=F32
    )[:HEAD]

    for side in range(pair_width // piece):

        @pl.when(question % (pair_width // piece) == side)
        def _():
            for peer in range(peers):
                dq_ref[peer, :, side * piece : (side + 1) * piece] = dq[
                    :, peer * piece : (peer + 1) * piece
                ]

    high = dq.astype(BF16)
    low = (dq - high.astype(F32)).astype(BF16)
    latent = jnp.dot(w_ref[...], high, preferred_element_type=F32) + jnp.dot(
        w_ref[...], low, preferred_element_type=F32
    )
    latent = latent.astype(BF16)
    bands = latent.shape[0] // 8
    tiles = o_ref.shape[0] // bands
    for band in range(bands):
        for part in range(targets // 128):
            tile = band * tiles + question * (targets // 128) + part
            o_ref[tile, span:, :] = latent[
                band * 8 : (band + 1) * 8, part * 128 : (part + 1) * 128
            ]


def key_kernel(per_question, slots, span, chosen_ref, q_ref, u_ref, s_ref, rows_ref, o_ref):
    question = pl.program_id(0)

    @pl.when(question == 0)
    def _():
        o_ref[...] = jnp.zeros_like(o_ref)

    both = two_sided(q_ref, u_ref)
    query = jnp.concatenate([q_ref[0]] * slots, axis=0)
    stats = row_stats(s_ref)
    for chunk in range(per_question // GRAD_CHUNK):
        first = question * per_question + chunk * GRAD_CHUNK
        rows = rows_ref[0, chunk * GRAD_CHUNK * span : (chunk + 1) * GRAD_CHUNK * span, :]
        _, score_grad = chunk_products(rows, both, stats)
        out = lax.dot_general(
            score_grad, query, (((1,), (1,)), ((), ())), preferred_element_type=F32
        ).astype(BF16)
        for i in range(GRAD_CHUNK):
            store_half(o_ref, chosen_ref[first + i], slots, out[i * span : (i + 1) * span])


def attend_stats(chosen, query_t, upstream_t, key_table, value_table, per_question, slots, span):
    questions, size, targets = query_t.shape
    one = pl.BlockSpec((1, size, targets), lambda q, c: (q, 0, 0))
    tables = [
        pl.BlockSpec(table.shape, lambda q, c: (0, 0, 0)) for table in (key_table, value_table)
    ]
    keys = per_question * span
    return pl.pallas_call(
        functools.partial(stats_kernel, per_question, slots, span),
        grid_spec=pltpu.PrefetchScalarGridSpec(
            num_scalar_prefetch=1,
            grid=(questions,),
            in_specs=[one, one, *tables],
            out_specs=[
                pl.BlockSpec((1, 8, targets), lambda q, c: (q, 0, 0)),
                pl.BlockSpec((1, keys, 2 * size), lambda q, c: (q, 0, 0)),
            ],
        ),
        out_shape=[
            jax.ShapeDtypeStruct((questions, 8, targets), F32),
            jax.ShapeDtypeStruct((questions, keys, 2 * size), BF16),
        ],
        compiler_params=pltpu.CompilerParams(vmem_limit_bytes=VMEM_LIMIT),
        cost_estimate=pl.CostEstimate(
            flops=8 * questions * targets * keys * HEAD,
            bytes_accessed=4 * key_table.size,
            transcendentals=questions * targets * keys,
        ),
        name="stats",
    )(chosen, query_t, upstream_t, key_table, value_table)


def query_value_grads(
    chosen, query_t, upstream_t, up_weight, stats, rows, heads, per_question, slots, span
):
    questions, size, targets = query_t.shape
    peers = stats.shape[0]
    one = pl.BlockSpec((1, size, targets), lambda q, c: (q, 0, 0))
    whole = pl.BlockSpec((1,) + rows.shape[1:], lambda q, c: (q, 0, 0))
    out = (heads, span + 8, rows.shape[2])
    keys = per_question * span
    piece = targets // peers
    in_block = 128 // piece
    return pl.pallas_call(
        functools.partial(query_value_kernel, per_question, slots, span),
        grid_spec=pltpu.PrefetchScalarGridSpec(
            num_scalar_prefetch=1,
            grid=(questions,),
            in_specs=[
                one,
                one,
                pl.BlockSpec(up_weight.shape, lambda q, c: (0, 0)),
                pl.BlockSpec((peers, 1, 8, targets), lambda q, c: (0, q, 0, 0)),
                whole,
            ],
            out_specs=[
                pl.BlockSpec((peers, size, 128), lambda q, c: (0, 0, q // in_block)),
                pl.BlockSpec(out, lambda q, c: (0, 0, 0)),
            ],
            scratch_shapes=[pltpu.VMEM((keys, targets), BF16)],
        ),
        out_shape=[
            pltpu.HBM((peers, size, questions * piece), F32),
            pltpu.HBM(out, BF16),
        ],
        compiler_params=pltpu.CompilerParams(vmem_limit_bytes=VMEM_LIMIT),
        cost_estimate=pl.CostEstimate(
            flops=24 * questions * targets * keys * HEAD,
            bytes_accessed=4 * rows.size,
            transcendentals=questions * targets * keys,
        ),
        name="query_value_grads",
    )(chosen, query_t, upstream_t, up_weight, stats, rows)


def key_grads(chosen, query_t, upstream_t, stats, rows, heads, per_question, slots, span):
    questions, size, targets = query_t.shape
    peers = stats.shape[0]
    one = pl.BlockSpec((1, size, targets), lambda q, c: (q, 0, 0))
    whole = pl.BlockSpec((1,) + rows.shape[1:], lambda q, c: (q, 0, 0))
    out = (heads, span + 8, rows.shape[2])
    keys = per_question * span
    return pl.pallas_call(
        functools.partial(key_kernel, per_question, slots, span),
        grid_spec=pltpu.PrefetchScalarGridSpec(
            num_scalar_prefetch=1,
            grid=(questions,),
            in_specs=[
                one,
                one,
                pl.BlockSpec((peers, 1, 8, targets), lambda q, c: (0, q, 0, 0)),
                whole,
            ],
            out_specs=pl.BlockSpec(out, lambda q, c: (0, 0, 0)),
        ),
        out_shape=pltpu.HBM(out, BF16),
        compiler_params=pltpu.CompilerParams(vmem_limit_bytes=VMEM_LIMIT),
        cost_estimate=pl.CostEstimate(
            flops=16 * questions * targets * keys * HEAD,
            bytes_accessed=4 * rows.size,
            transcendentals=questions * targets * keys,
        ),
        name="key_grads",
    )(chosen, query_t, upstream_t, stats, rows)


def to_all(x, axis):
    size = lax.axis_size(axis)
    return exchange(
        jnp.broadcast_to(x[None], (size,) + x.shape), axis
    )


def scatter_sum_tp(x):
    size, here = lax.axis_size("tp"), lax.axis_index("tp")
    own = lax.dynamic_index_in_dim(x, here, 0, keepdims=False)
    for k in range(1, size):
        sent = lax.dynamic_index_in_dim(x, (here + k) % size, 0, keepdims=False)
        own = own + lax.ppermute(sent, "tp", [(i, (i + k) % size) for i in range(size)])
    return own


def exchange(x, axis):
    order = None
    if axis == "grp":
        size = lax.axis_size(axis)
        order = [[reverse(i, size) for i in range(size)]]
    return lax.all_to_all(
        x, axis, split_axis=0, concat_axis=0, tiled=True, axis_index_groups=order
    )


def with_tile(table, tile, row):
    tile = jnp.broadcast_to(tile[None], (table.shape[0],) + tile.shape)
    return lax.dynamic_update_slice(table, tile, (0, row, 0))


def untiled(x, tiles):
    bands, parts, rows, lanes = tiles
    return jnp.transpose(x.reshape(tiles), (0, 2, 1, 3)).reshape(bands * rows, parts * lanes)


def local(
    keys,
    values,
    frozen_query_projection,
    context_gradient,
    hidden,
    adapter_down_weight,
    adapter_up_weight,
    owner,
    counts,
    target_length,
):
    group_count, token_split = lax.axis_size("grp"), lax.axis_size("tp")
    questions, targets, _ = frozen_query_projection.shape
    slots_dev, span, _ = keys.shape
    total_slots = group_count * slots_dev
    per_question = (total_slots - group_count // 4) // questions
    piece = targets // token_split
    positions = questions * targets
    tiles = (HEAD // 8, positions // 128, 8, 128)

    hidden_t = jnp.swapaxes(hidden, 1, 2)
    value_table = exchange(
        pack_values(owner, counts, adapter_down_weight, hidden_t, values), "grp"
    )
    latent_tile = jnp.sum(value_table[:, span : span + 8, :].astype(F32), axis=0).astype(BF16)
    slot_key = value_table[:, span + 8, :slots_dev].astype(jnp.int32).reshape(total_slots)
    key_table = exchange(with_tile(pack_keys(keys, 8), latent_tile, span), "grp")

    slot_ids = jnp.arange(total_slots, dtype=jnp.int32)
    same = (slot_key[:, None] == slot_key[None, :]) & (slot_ids[None, :] < slot_ids[:, None])
    rank = jnp.sum(same.astype(jnp.int32), axis=1)
    place = slot_key * per_question + rank
    wanted = jnp.arange(questions * per_question, dtype=jnp.int32)
    hit = (place[None, :] == wanted[:, None]) & (slot_key < questions)[None, :]
    chosen = jnp.sum(jnp.where(hit, slot_ids[None, :], 0), axis=1)

    step_ids = lax.broadcasted_iota(jnp.int32, (questions, 1, targets), 2)
    keep = step_ids < target_length[:, None, None]
    upstream_t = jnp.swapaxes(context_gradient, 1, 2)
    upstream_t = jnp.where(keep, upstream_t, jnp.zeros_like(upstream_t))
    latent_t = untiled(key_table[:, span:, :], tiles).reshape(HEAD, questions, targets)
    raised = jnp.einsum("rd,rqt->qdt", adapter_up_weight, latent_t, preferred_element_type=F32)
    frozen_t = jnp.swapaxes(frozen_query_projection, 1, 2)
    query_t = (frozen_t.astype(F32) + raised).astype(BF16)

    sizes = (per_question, slots_dev, span)
    stats, rows = attend_stats(chosen, query_t, upstream_t, key_table, value_table, *sizes)
    all_stats = to_all(stats, "tp")
    dq_parts, value_grads = query_value_grads(
        chosen, query_t, upstream_t, adapter_up_weight, all_stats, rows, group_count, *sizes
    )
    grads = key_grads(chosen, query_t, upstream_t, all_stats, rows, group_count, *sizes)
    value_back = exchange(value_grads, "grp")
    latent_grad_tile = jnp.sum(value_back[:, span:, :].astype(F32), axis=0).astype(BF16)
    grad_values = unpack(value_back, slots_dev, span)
    key_back = exchange(with_tile(grads, latent_grad_tile, span), "grp")
    grad_keys = unpack(key_back, slots_dev, span)
    latent_grad = untiled(key_back[:, span:, :], tiles).reshape(HEAD, questions, targets)
    grad_a = jnp.einsum("qdt,rqt->dr", hidden_t, latent_grad, preferred_element_type=F32)

    dq_t = scatter_sum_tp(dq_parts).astype(BF16).reshape(HEAD, questions, piece)
    adapted = jnp.transpose(dq_t, (1, 2, 0))
    start = lax.axis_index("tp") * piece
    latent_cut = lax.dynamic_slice_in_dim(latent_t, start, piece, 2)
    grad_b = jnp.einsum("rqt,dqt->rd", latent_cut, dq_t, preferred_element_type=F32)
    got = to_all(jnp.concatenate([grad_a, grad_b], axis=1), ("sect", "tp"))
    got, grad_keys = lax.optimization_barrier((got, grad_keys))
    grads = jnp.sum(got, axis=0)
    return (adapted, grad_keys, grad_values, grads[:, :HEAD], grads[:, HEAD:])


def solution(mesh):
    return jax.shard_map(
        local,
        mesh=mesh,
        in_specs=(
            P(("sect", "grp"), "tp", None),
            P(("sect", "grp"), "tp", None),
            P("sect", None, "grp"),
            P("sect", None, "grp"),
            P("sect", None, "grp"),
            P("grp", None),
            P(None, "grp"),
            P(("sect", "grp")),
            P(("sect", "grp")),
            P("sect"),
        ),
        out_specs=(
            P("sect", "tp", "grp"),
            P(("sect", "grp"), "tp", None),
            P(("sect", "grp"), "tp", None),
            P("grp", None),
            P(None, "grp"),
        ),
        check_vma=False,
    )
```

time: 211 us -> 207 us (0.981)
  waiting for transfers between devices: 109 us -> 103 us
  local copies, waits for them, and re-layouts: 8.56 us -> 4.89 us
  starting transfers between devices: 56.5 us -> 59.2 us
  Pallas kernels: 24.8 us -> 27.2 us
    all_to_all x5, waiting for transfers between devices: 104 us -> 98.5 us  [exchange(): lax.all_to_all(x, axis, split_axis=0, concat_axis=0, tiled=True, axis_ind...]
    unnamed x34 -> x20, local copies, waits for them, and re-layouts: 5.21 us -> 1.53 us
    all_to_all x5, starting transfers between devices: 48.7 us -> 51.4 us  [exchange(): lax.all_to_all(x, axis, split_axis=0, concat_axis=0, tiled=True, axis_ind...]
where the time goes in v5:
time: 207 us; the launch traced here: 206 us
  waiting for transfers between devices  103 us (50%)
  starting transfers between devices  59.2 us (29%)
  Pallas kernels  27.2 us (13%)
  blocking collectives  8.65 us (4%)
  local copies, waits for them, and re-layouts  4.89 us (2%)
    all_to_all x5, waiting for transfers between devices, exchange(): lax.all_to_all(x, axis, split_axis=0, concat_axis=0, tiled=True, axis_ind...  98.5 us
    all_to_all x5, starting transfers between devices, exchange(): lax.all_to_all(x, axis, split_axis=0, concat_axis=0, tiled=True, axis_ind...  51.4 us
    all_to_all x1, blocking collectives, exchange(): lax.all_to_all(x, axis, split_axis=0, concat_axis=0, tiled=True, axis_ind...  8.65 us
    ppermute x3, starting transfers between devices, scatter_sum_tp(): lax.ppermute(sent, 'tp', [(i, (i + k) % size) for i in range(size)])  7.81 us
    pallas_call x1, Pallas kernels, query_value_grads(): pl.pallas_call(functools.partial(query_value_kernel, per_question, slots,...  7 us
    pallas_call x1, Pallas kernels, key_grads(): pl.pallas_call(functools.partial(key_kernel, per_question, slots, span),...  5.71 us
    pallas_call x1, Pallas kernels, attend_stats(): pl.pallas_call(functools.partial(stats_kernel, per_question, slots, span)...  4.7 us
    ppermute x3, waiting for transfers between devices, scatter_sum_tp(): lax.ppermute(sent, 'tp', [(i, (i + k) % size) for i in range(size)])  4.55 us
  transfers between devices with their start and end apart: 8, of which 7 were waited for; matrix products, arithmetic and copies ran while one was open for 1% of the time, Pallas kernels for 6%

profile of v5, /device:TPU:1, one launch (start us, length us, event | category | flops | bytes accessed | tf_op | source)
XLA Modules:
  0.0 206.0 jit_solution(6009771813592555348)
XLA Ops:
  1.3 3.9 %pack_values.1 = bf16[16,4,80,128]{3,2,1,0:T(8,128)(2,1)} custom-call(s32[2]{0:T(128)} %owner_ref.1, s32[1]{0:T(128)S(6)} %copy.42.counts_ref, bf16[64,64]{1,0:T(8,128)(2,1)} %down_ref.1, bf16[4,64,256]{2,1,0:T(8,128)(2,1)} %bitcast.53, bf16[2,64,4096]{2,1,0:T(8,128)(2,1)} %v_ref.1), custom_call_target="tpu_custom_call" | custom-call | flops 8388608 | bytes 2097152 | tf_op jit(solution)/shard_map/pack_values/pallas_call | solution.py:116
  5.1 17.3 %all-to-all-start = ((bf16[64,80,128]{2,1,0:T(8,128)(2,1)}), bf16[64,80,128]{2,1,0:T(8,128)(2,1)S(1)}, u32[]{:S(2)}, u32[]{:S(2)}) async-start(bf16[64,80,128]{2,1,0:T(8,128)(2,1)} %bitcast.52), calls=%async_computation | async-start | bytes 2621440 | tf_op jit(solution)/shard_map/all_to_all | solution.py:444
  22.4 2.0 pack_keys.1
  24.4 31.4 %all-to-all-done.v_ref = bf16[64,80,128]{2,1,0:T(8,128)(2,1)S(1)} async-done(((bf16[64,80,128]{2,1,0:T(8,128)(2,1)}), bf16[64,80,128]{2,1,0:T(8,128)(2,1)S(1)}, u32[]{:S(2)}, u32[]{:S(2)}) %all-to-all-start) | async-done | bytes 1310752 | tf_op jit(solution)/shard_map/all_to_all | solution.py:444
  55.9 0.7 broadcast_dynamic-update-slice_fusion.1
  56.6 8.0 %all-to-all-start.1 = ((bf16[64,72,128]{2,1,0:T(8,128)(2,1)}), bf16[64,72,128]{2,1,0:T(8,128)(2,1)S(1)}, u32[]{:S(2)}, u32[]{:S(2)}) async-start(bf16[64,72,128]{2,1,0:T(8,128)(2,1)} %broadcast_dynamic-update-slice_fusion.1), calls=%async_computation.1 | async-start | bytes 2359296 | tf_op jit(solution)/shard_map/all_to_all | solution.py:444
  65.0 0.2 convert_reduce_fusion
  65.3 29.1 %all-to-all-done.1.k_ref = bf16[64,72,128]{2,1,0:T(8,128)(2,1)S(1)} async-done(((bf16[64,72,128]{2,1,0:T(8,128)(2,1)}), bf16[64,72,128]{2,1,0:T(8,128)(2,1)S(1)}, u32[]{:S(2)}, u32[]{:S(2)}) %all-to-all-start.1) | async-done | bytes 1179680 | tf_op jit(solution)/shard_map/all_to_all | solution.py:444
  94.5 0.2 fusion.1.q_ref
  94.8 4.7 %stats.1 = (f32[4,8,256]{2,1,0:T(8,128)S(1)}, bf16[4,1792,128]{2,1,0:T(8,128)(2,1)S(1)}) custom-call(s32[112]{0:T(128)S(1)} %select_reduce_fusion.chosen_ref, bf16[4,64,256]{2,1,0:T(8,128)(2,1)S(1)} %fusion.1.q_ref, bf16[4,64,256]{2,1,0:T(8,128)(2,1)S(1)} %select_bitcast_fusion.u_ref, bf16[64,72,128]{2,1,0:T(8,128)(2,1)S(1)} %all-to-all-done.1.k_ref, ...), custom_call_target="tpu_custom_call" | custom-call | flops 939524096 | bytes 2359296 | tf_op jit(solution)/shard_map/stats/pallas_call | solution.py:324
  99.5 8.7 %all_to_all.30.s_ref = f32[4,4,8,256]{3,2,1,0:T(8,128)S(1)} all-to-all(f32[4,4,8,256]{3,2,1,0:T(8,128)S(1)} %broadcast_in_dim.35), channel_id=1, replica_groups=mesh['sect'=2,'grp'=64,'tp'=4] {'tp'}, dimensions={0} | all-to-all | bytes 262144 | tf_op jit(solution)/shard_map/all_to_all | solution.py:444
  108.2 7.0 %query_value_grads.1 = (f32[4,64,256]{2,1,0:T(8,128)}, bf16[64,72,128]{2,1,0:T(8,128)(2,1)}) custom-call(s32[112]{0:T(128)S(1)} %select_reduce_fusion.chosen_ref, bf16[4,64,256]{2,1,0:T(8,128)(2,1)S(1)} %fusion.1.q_ref, bf16[4,64,256]{2,1,0:T(8,128)(2,1)S(1)} %select_bitcast_fusion.u_ref, bf16[64,64]{1,0:T(8,128)(2,1)S(1)} %copy-done.1, ...), custom_call_target="tpu_custom_call" | custom-call | flops 2818572288 | bytes 3670016 | tf_op jit(solution)/shard_map/query_value_grads/pallas_call | solution.py:360
  115.2 7.8 %all-to-all-start.3 = ((bf16[64,72,128]{2,1,0:T(8,128)(2,1)}), bf16[64,72,128]{2,1,0:T(8,128)(2,1)S(1)}, u32[]{:S(2)}, u32[]{:S(2)}) async-start(bf16[64,72,128]{2,1,0:T(8,128)(2,1)} %get-tuple-element.14), calls=%async_computation.3 | async-start | bytes 2359296 | tf_op jit(solution)/shard_map/all_to_all | solution.py:444
  123.0 1.5 copy-done.3
  124.5 5.7 %key_grads.1 = bf16[64,72,128]{2,1,0:T(8,128)(2,1)} custom-call(s32[112]{0:T(128)S(1)} %select_reduce_fusion.chosen_ref, bf16[4,64,256]{2,1,0:T(8,128)(2,1)S(1)} %fusion.1.q_ref, bf16[4,64,256]{2,1,0:T(8,128)(2,1)S(1)} %select_bitcast_fusion.u_ref, f32[4,4,8,256]{3,2,1,0:T(8,128)S(1)} %all_to_all.30.s_ref, bf16[4,1792,128]{2,1,0:T(8,128)(2,1)S(1)} %copy-done.3), custom_call_target="tpu_custom_call" | custom-call | flops 1879048192 | bytes 3670016 | tf_op jit(solution)/shard_map/key_grads/pallas_call | solution.py:399
  130.2 20.8 %all-to-all-done.3 = bf16[64,72,128]{2,1,0:T(8,128)(2,1)S(1)} async-done(((bf16[64,72,128]{2,1,0:T(8,128)(2,1)}), bf16[64,72,128]{2,1,0:T(8,128)(2,1)S(1)}, u32[]{:S(2)}, u32[]{:S(2)}) %all-to-all-start.3) | async-done | bytes 1179680 | tf_op jit(solution)/shard_map/all_to_all | solution.py:444
  151.1 0.7 broadcast_dynamic-update-slice_fusion
  151.8 7.8 %all-to-all-start.4 = ((bf16[64,72,128]{2,1,0:T(8,128)(2,1)}), bf16[64,72,128]{2,1,0:T(8,128)(2,1)S(1)}, u32[]{:S(2)}, u32[]{:S(2)}) async-start(bf16[64,72,128]{2,1,0:T(8,128)(2,1)} %broadcast_dynamic-update-slice_fusion), calls=%async_computation.4 | async-start | bytes 2359296 | tf_op jit(solution)/shard_map/all_to_all | solution.py:444
  159.7 2.8 %collective-permute-start.2 = (f32[64,256]{1,0:T(8,128)S(1)}, f32[64,256]{1,0:T(8,128)S(1)}, u32[]{:S(2)}, u32[]{:S(2)}) collective-permute-start(f32[64,256]{1,0:T(8,128)S(1)} %get-tuple-element.18), channel_id=1, source_target_pairs={{0,3},{1,0},{2,1},{3,2},{4,7},{5,4},{6,5},{7,6},{8,11},{9,8},{10,9... | collective-permute-start | bytes 196616 | tf_op jit(solution)/shard_map/ppermute | solution.py:435
  162.5 3.1 %collective-permute-start.1 = (f32[64,256]{1,0:T(8,128)S(1)}, f32[64,256]{1,0:T(8,128)S(1)}, u32[]{:S(2)}, u32[]{:S(2)}) collective-permute-start(f32[64,256]{1,0:T(8,128)S(1)} %get-tuple-element.19), channel_id=1, source_target_pairs={{0,2},{1,3},{2,0},{3,1},{4,6},{5,7},{6,4},{7,5},{8,10},{9,11},{10,... | collective-permute-start | bytes 196616 | tf_op jit(solution)/shard_map/ppermute | solution.py:435
  165.6 1.9 collective-permute-start
  167.6 1.5 collective-permute-done.1
  169.0 3.1 %collective-permute-done = f32[64,256]{1,0:T(8,128)S(1)} collective-permute-done((f32[64,256]{1,0:T(8,128)S(1)}, f32[64,256]{1,0:T(8,128)S(1)}, u32[]{:S(2)}, u32[]{:S(2)}) %collective-permute-start) | collective-permute-done | bytes 65568 | tf_op jit(solution)/shard_map/ppermute | solution.py:435
  172.3 0.3 convolution_bitcast_fusion
  172.5 14.6 %all-to-all-done.4 = bf16[64,72,128]{2,1,0:T(8,128)(2,1)S(1)} async-done(((bf16[64,72,128]{2,1,0:T(8,128)(2,1)}), bf16[64,72,128]{2,1,0:T(8,128)(2,1)S(1)}, u32[]{:S(2)}, u32[]{:S(2)}) %all-to-all-start.4) | async-done | bytes 1179680 | tf_op jit(solution)/shard_map/all_to_all | solution.py:444
  187.3 0.2 convolution_bitcast_fusion.1
  187.6 0.7 broadcast_in_dim.37
  188.3 10.5 %all-to-all-start.5 = ((f32[8,64,128]{2,1,0:T(8,128)}), f32[8,64,128]{2,1,0:T(8,128)S(1)}, u32[]{:S(2)}, u32[]{:S(2)}) async-start(f32[8,64,128]{2,1,0:T(8,128)} %broadcast_in_dim.37), calls=%async_computation.5 | async-start | bytes 524288 | tf_op jit(solution)/shard_map/all_to_all | solution.py:444
  198.8 1.9 unpack.3
  200.7 1.9 unpack.2
  202.7 2.7 %all-to-all-done.5 = f32[8,64,128]{2,1,0:T(8,128)S(1)} async-done(((f32[8,64,128]{2,1,0:T(8,128)}), f32[8,64,128]{2,1,0:T(8,128)S(1)}, u32[]{:S(2)}, u32[]{:S(2)}) %all-to-all-start.5) | async-done | bytes 262176 | tf_op jit(solution)/shard_map/all_to_all | solution.py:444
  205.4 0.7 fusion.14
  (42 shorter events, 1.1 us)
Async XLA Ops:
  5.1 17.3 %copy-start = (bf16[2,64,4096]{2,1,0:T(8,128)(2,1)S(1)}, bf16[2,64,4096]{2,1,0:T(8,128)(2,1)}, u32[]{:S(2)}) copy-start(bf16[2,64,4096]{2,1,0:T(8,128)(2,1)} %k_ref.1) | copy-start | bytes 3145732
  5.1 50.7 %all-to-all-start = ((bf16[64,80,128]{2,1,0:T(8,128)(2,1)}), bf16[64,80,128]{2,1,0:T(8,128)(2,1)S(1)}, u32[]{:S(2)}, u32[]{:S(2)}) async-start(bf16[64,80,128]{2,1,0:T(8,128)(2,1)} %bitcast.52), calls=%async_computation | async-start | bytes 2621440 | tf_op jit(solution)/shard_map/all_to_all | solution.py:444
  56.6 8.0 %copy-start.9 = (s32[4]{0:T(128)S(1)}, s32[4]{0:T(128)}, u32[]{:S(2)}) copy-start(s32[4]{0:T(128)} %param.19) | copy-start | bytes 52
  56.6 8.1 %copy-start.8 = (bf16[4,256,64]{1,2,0:T(8,128)(2,1)S(1)}, bf16[4,256,64]{1,2,0:T(8,128)(2,1)}, u32[]{:S(2)}) copy-start(bf16[4,256,64]{1,2,0:T(8,128)(2,1)} %param.13) | copy-start | bytes 393220
  56.6 37.9 %copy-start.1 = (bf16[64,64]{1,0:T(8,128)(2,1)S(1)}, bf16[64,64]{1,0:T(8,128)(2,1)}, u32[]{:S(2)}) copy-start(bf16[64,64]{1,0:T(8,128)(2,1)} %w_ref.1) | copy-start | bytes 24580
  56.6 37.9 %copy-start.7 = (bf16[4,256,64]{1,2,0:T(8,128)(2,1)S(1)}, bf16[4,256,64]{1,2,0:T(8,128)(2,1)}, u32[]{:S(2)}) copy-start(bf16[4,256,64]{1,2,0:T(8,128)(2,1)} %param.12) | copy-start | bytes 393220
  56.6 37.8 %all-to-all-start.1 = ((bf16[64,72,128]{2,1,0:T(8,128)(2,1)}), bf16[64,72,128]{2,1,0:T(8,128)(2,1)S(1)}, u32[]{:S(2)}, u32[]{:S(2)}) async-start(bf16[64,72,128]{2,1,0:T(8,128)(2,1)} %broadcast_dynamic-update-slice_fusion.1), calls=%async_computation.1 | async-start | bytes 2359296 | tf_op jit(solution)/shard_map/all_to_all | solution.py:444
  99.5 15.7 %copy-start.2 = (bf16[4,1792,128]{2,1,0:T(8,128)(2,1)}, bf16[4,1792,128]{2,1,0:T(8,128)(2,1)S(1)}, u32[]{:S(2)}) copy-start(bf16[4,1792,128]{2,1,0:T(8,128)(2,1)S(1)} %get-tuple-element.12.rows_ref) | copy-start | bytes 5505028
  115.2 35.8 %all-to-all-start.3 = ((bf16[64,72,128]{2,1,0:T(8,128)(2,1)}), bf16[64,72,128]{2,1,0:T(8,128)(2,1)S(1)}, u32[]{:S(2)}, u32[]{:S(2)}) async-start(bf16[64,72,128]{2,1,0:T(8,128)(2,1)} %get-tuple-element.14), calls=%async_computation.3 | async-start | bytes 2359296 | tf_op jit(solution)/shard_map/all_to_all | solution.py:444
  123.0 1.5 copy-start.3
  151.8 7.9 %copy-start.5 = (f32[4,64,256]{2,1,0:T(8,128)S(1)}, f32[4,64,256]{2,1,0:T(8,128)}, u32[]{:S(2)}) copy-start(f32[4,64,256]{2,1,0:T(8,128)} %get-tuple-element.13) | copy-start | bytes 786436
  151.8 35.4 %all-to-all-start.4 = ((bf16[64,72,128]{2,1,0:T(8,128)(2,1)}), bf16[64,72,128]{2,1,0:T(8,128)(2,1)S(1)}, u32[]{:S(2)}, u32[]{:S(2)}) async-start(bf16[64,72,128]{2,1,0:T(8,128)(2,1)} %broadcast_dynamic-update-slice_fusion), calls=%async_computation.4 | async-start | bytes 2359296 | tf_op jit(solution)/shard_map/all_to_all | solution.py:444
  159.6 27.7 %copy-start.4 = (bf16[4,256,64]{1,2,0:T(8,128)(2,1)S(1)}, bf16[4,256,64]{1,2,0:T(8,128)(2,1)}, u32[]{:S(2)}) copy-start(bf16[4,256,64]{1,2,0:T(8,128)(2,1)} %param.14) | copy-start | bytes 393220
  159.7 7.9 %collective-permute-start.2 = (f32[64,256]{1,0:T(8,128)S(1)}, f32[64,256]{1,0:T(8,128)S(1)}, u32[]{:S(2)}, u32[]{:S(2)}) collective-permute-start(f32[64,256]{1,0:T(8,128)S(1)} %get-tuple-element.18), channel_id=1, source_target_pairs={{0,3},{1,0},{2,1},{3,2},{4,7},{5,4},{6,5},{7,6},{8,11},{9,8},{10,9... | collective-permute-start | bytes 196616 | tf_op jit(solution)/shard_map/ppermute | solution.py:435
  162.5 6.5 %collective-permute-start.1 = (f32[64,256]{1,0:T(8,128)S(1)}, f32[64,256]{1,0:T(8,128)S(1)}, u32[]{:S(2)}, u32[]{:S(2)}) collective-permute-start(f32[64,256]{1,0:T(8,128)S(1)} %get-tuple-element.19), channel_id=1, source_target_pairs={{0,2},{1,3},{2,0},{3,1},{4,6},{5,7},{6,4},{7,5},{8,10},{9,11},{10,... | collective-permute-start | bytes 196616 | tf_op jit(solution)/shard_map/ppermute | solution.py:435
  165.6 6.5 %collective-permute-start = (f32[64,256]{1,0:T(8,128)S(1)}, f32[64,256]{1,0:T(8,128)S(1)}, u32[]{:S(2)}, u32[]{:S(2)}) collective-permute-start(f32[64,256]{1,0:T(8,128)S(1)} %get-tuple-element.17), channel_id=1, source_target_pairs={{0,1},{1,2},{2,3},{3,0},{4,5},{5,6},{6,7},{7,4},{8,9},{9,10},{10,1... | collective-permute-start | bytes 196616 | tf_op jit(solution)/shard_map/ppermute | solution.py:435
  172.2 28.5 %copy-start.6 = (bf16[64,256]{0,1:T(8,128)(2,1)}, bf16[64,256]{0,1:T(8,128)(2,1)S(1)}, u32[]{:S(2)}) copy-start(bf16[64,256]{0,1:T(8,128)(2,1)S(1)} %copy.31) | copy-start | bytes 98308
  188.3 17.0 %all-to-all-start.5 = ((f32[8,64,128]{2,1,0:T(8,128)}), f32[8,64,128]{2,1,0:T(8,128)S(1)}, u32[]{:S(2)}, u32[]{:S(2)}) async-start(f32[8,64,128]{2,1,0:T(8,128)} %broadcast_in_dim.37), calls=%async_computation.5 | async-start | bytes 524288 | tf_op jit(solution)/shard_map/all_to_all | solution.py:444

commit v6 on v5

--- a/solution.py
+++ b/solution.py
@@ -14,20 +14,33 @@
 ALL_VMEM = 62 * 1024 * 1024
 
 
-def reverse(index, size):
-    bits = size.bit_length() - 1
-    return sum(((index >> bit) & 1) << (bits - 1 - bit) for bit in range(bits))
+ORDER = (4, 5, 2, 1, 3, 0)
+
+
+def member_at(position):
+    return sum(((position >> j) & 1) << bit for j, bit in enumerate(ORDER))
+
+
+def position_of(member):
+    return sum(((member >> bit) & 1) << j for j, bit in enumerate(ORDER))
+
+
+PACK_STEPS = 2
+
+
+def block_of(head):
+    position = position_of(head)
+    return position // 4, 0, position % 2
 
 
 def pack_rows(x_ref, o_ref):
     slots, span, width = x_ref.shape
-    heads = width // HEAD
     for pair in range(width // (2 * HEAD)):
         low = pair * 2 * HEAD
         parts = [x_ref[slot, :, low : low + 2 * HEAD] for slot in range(slots)]
         for side in range(2):
             cut = slice(side * HEAD, (side + 1) * HEAD)
-            o_ref[reverse(2 * pair + side, heads), 0, :span, :] = jnp.concatenate(
+            o_ref[*block_of(2 * pair + side), :span, :] = jnp.concatenate(
                 [part[:, cut] for part in parts], axis=1
             )
 
@@ -40,8 +53,6 @@
     pack_rows(v_ref, o_ref)
     span = v_ref.shape[1]
     questions, _, targets = hidden_ref.shape
-    blocks, steps = o_ref.shape[0], pl.num_programs(0)
-    halves = targets // 128
     lanes = lax.broadcasted_iota(jnp.int32, (8, 128), 1)
     tags = jnp.zeros(lanes.shape, jnp.int32)
     for slot in range(owner_ref.shape[0]):
@@ -50,47 +61,42 @@
     tags = tags.astype(F32)
     down = down_ref[...]
     bands = down.shape[1] // 8
-    per_band = blocks // bands
-    step = reverse(pl.program_id(0), PACK_STEPS)
-    for turn in range(per_band):
-        part = turn * steps + step
-        start = pl.multiple_of(lax.rem(part, halves) * 128, 128)
-        latent = lax.dot_general(
-            down,
-            hidden_ref[part // halves, :, pl.ds(start, 128)],
-            (((0,), (0,)), ((), ())),
-            preferred_element_type=F32,
-        )
-        for band in range(bands):
-            tile = latent[band * 8 : (band + 1) * 8]
-            o_ref[band * per_band + turn, 0, span : span + 16, :] = jnp.concatenate(
-                [tile, tags], axis=0
-            ).astype(o_ref.dtype)
+    outer, _, inner, _, _ = o_ref.shape
+    turns, halves = outer // bands, targets // 128
+    for turn in range(turns):
+        for j in range(inner):
+            part = (turn * PACK_STEPS + pl.program_id(0)) * inner + j
+            start = pl.multiple_of(lax.rem(part, halves) * 128, 128)
+            latent = lax.dot_general(
+                down,
+                hidden_ref[part // halves, :, pl.ds(start, 128)],
+                (((0,), (0,)), ((), ())),
+                preferred_element_type=F32,
+            )
+            for band in range(bands):
+                tile = latent[band * 8 : (band + 1) * 8]
+                o_ref[band * turns + turn, 0, j, span : span + 16, :] = jnp.concatenate(
+                    [tile, tags], axis=0
+                ).astype(o_ref.dtype)
 
 
 def unpack_kernel(i_ref, o_ref):
     slots, span, width = o_ref.shape
-    heads = width // HEAD
     for pair in range(width // (2 * HEAD)):
         low = pair * 2 * HEAD
-        even = i_ref[reverse(2 * pair, heads), 0, :span, :]
-        odd = i_ref[reverse(2 * pair + 1, heads), 0, :span, :]
+        even = i_ref[*block_of(2 * pair), :span, :]
+        odd = i_ref[*block_of(2 * pair + 1), :span, :]
         for slot in range(slots):
             side = slice(slot * HEAD, (slot + 1) * HEAD)
             o_ref[slot, :, low : low + 2 * HEAD] = jnp.concatenate([even[:, side], odd[:, side]], axis=1)
 
 
-PACK_STEPS = 4
-
-
 def pack_specs(slots, span, width, rows):
     heads = width // HEAD
-    blocks = heads // PACK_STEPS
-    part = pl.BlockSpec((slots, span, blocks * HEAD), lambda i: (0, 0, i))
-    table = pl.BlockSpec(
-        (blocks, 1, rows, slots * HEAD), lambda i: (0, reverse(i, PACK_STEPS), 0, 0)
-    )
-    return part, table, (blocks, PACK_STEPS, rows, slots * HEAD)
+    shape = (heads // 4, PACK_STEPS, 2, rows, slots * HEAD)
+    part = pl.BlockSpec((slots, span, width // PACK_STEPS), lambda i: (0, 0, i))
+    table = pl.BlockSpec((shape[0], 1) + shape[2:], lambda i: (0, i, 0, 0, 0))
+    return part, table, shape
 
 
 def pack_keys(keys, spare):
@@ -440,7 +446,7 @@
     order = None
     if axis == "grp":
         size = lax.axis_size(axis)
-        order = [[reverse(i, size) for i in range(size)]]
+        order = [[member_at(i) for i in range(size)]]
     return lax.all_to_all(
         x, axis, split_axis=0, concat_axis=0, tiled=True, axis_index_groups=order
     )

time: 207 us -> 205 us (level)
  waiting for transfers between devices: 103 us -> 112 us
  starting transfers between devices: 59.2 us -> 52 us
  Pallas kernels: 27.2 us -> 23.9 us
    all_to_all x5, waiting for transfers between devices: 98.5 us -> 107 us  [exchange(): lax.all_to_all(x, axis, split_axis=0, concat_axis=0, tiled=True, axis_ind...]
    all_to_all x5, starting transfers between devices: 51.4 us -> 44.1 us  [exchange(): lax.all_to_all(x, axis, split_axis=0, concat_axis=0, tiled=True, axis_ind...]
  transfers between devices with their start and end apart: 8 -> 8, of which waited for: 7 -> 7; matrix products, arithmetic and copies ran while one was open for 1% -> 1% of each run, Pallas kernels for 6% -> 5%
where the time goes in v6:
time: 205 us; the launch traced here: 204 us
  waiting for transfers between devices  112 us (55%)
  starting transfers between devices  52 us (25%)
  Pallas kernels  23.9 us (12%)
  blocking collectives  8.71 us (4%)
  local copies, waits for them, and re-layouts  4.89 us (2%)
    all_to_all x5, waiting for transfers between devices, exchange(): lax.all_to_all(x, axis, split_axis=0, concat_axis=0, tiled=True, axis_ind...  107 us
    all_to_all x5, starting transfers between devices, exchange(): lax.all_to_all(x, axis, split_axis=0, concat_axis=0, tiled=True, axis_ind...  44.1 us
    all_to_all x1, blocking collectives, exchange(): lax.all_to_all(x, axis, split_axis=0, concat_axis=0, tiled=True, axis_ind...  8.71 us
    ppermute x3, starting transfers between devices, scatter_sum_tp(): lax.ppermute(sent, 'tp', [(i, (i + k) % size) for i in range(size)])  7.81 us
    pallas_call x1, Pallas kernels, query_value_grads(): pl.pallas_call(functools.partial(query_value_kernel, per_question, slots,...  6.99 us
    pallas_call x1, Pallas kernels, key_grads(): pl.pallas_call(functools.partial(key_kernel, per_question, slots, span),...  5.71 us
    pallas_call x1, Pallas kernels, attend_stats(): pl.pallas_call(functools.partial(stats_kernel, per_question, slots, span)...  4.69 us
    ppermute x3, waiting for transfers between devices, scatter_sum_tp(): lax.ppermute(sent, 'tp', [(i, (i + k) % size) for i in range(size)])  4.55 us
  transfers between devices with their start and end apart: 8, of which 7 were waited for; matrix products, arithmetic and copies ran while one was open for 1% of the time, Pallas kernels for 5%

profile of v6, /device:TPU:1, one launch (start us, length us, event | category | flops | bytes accessed | tf_op | source)
XLA Modules:
  0.0 204.5 jit_solution(8481130938739321646)
XLA Ops:
  1.3 2.5 %pack_values.1 = bf16[16,2,2,80,128]{4,3,2,1,0:T(8,128)(2,1)} custom-call(s32[2]{0:T(128)} %owner_ref.1, s32[1]{0:T(128)S(6)} %copy.42.counts_ref, bf16[64,64]{1,0:T(8,128)(2,1)} %down_ref.1, bf16[4,64,256]{2,1,0:T(8,128)(2,1)} %bitcast.53, bf16[2,64,4096]{2,1,0:T(8,128)(2,1)} %v_ref.1), custom_call_target="tpu_custom_call" | custom-call | flops 8388608 | bytes 2097152 | tf_op jit(solution)/shard_map/pack_values/pallas_call | solution.py:122
  3.8 17.3 %all-to-all-start = ((bf16[64,80,128]{2,1,0:T(8,128)(2,1)}), bf16[64,80,128]{2,1,0:T(8,128)(2,1)S(1)}, u32[]{:S(2)}, u32[]{:S(2)}) async-start(bf16[64,80,128]{2,1,0:T(8,128)(2,1)} %bitcast.52), calls=%async_computation | async-start | bytes 2621440 | tf_op jit(solution)/shard_map/all_to_all | solution.py:450
  21.1 1.3 pack_keys.1
  22.4 33.8 %all-to-all-done.v_ref = bf16[64,80,128]{2,1,0:T(8,128)(2,1)S(1)} async-done(((bf16[64,80,128]{2,1,0:T(8,128)(2,1)}), bf16[64,80,128]{2,1,0:T(8,128)(2,1)S(1)}, u32[]{:S(2)}, u32[]{:S(2)}) %all-to-all-start) | async-done | bytes 1310752 | tf_op jit(solution)/shard_map/all_to_all | solution.py:450
  56.2 0.7 broadcast_dynamic-update-slice_fusion.1
  56.9 6.4 %all-to-all-start.1 = ((bf16[64,72,128]{2,1,0:T(8,128)(2,1)}), bf16[64,72,128]{2,1,0:T(8,128)(2,1)S(1)}, u32[]{:S(2)}, u32[]{:S(2)}) async-start(bf16[64,72,128]{2,1,0:T(8,128)(2,1)} %broadcast_dynamic-update-slice_fusion.1), calls=%async_computation.1 | async-start | bytes 2359296 | tf_op jit(solution)/shard_map/all_to_all | solution.py:450
  63.8 0.2 convert_reduce_fusion
  64.1 31.2 %all-to-all-done.1.k_ref = bf16[64,72,128]{2,1,0:T(8,128)(2,1)S(1)} async-done(((bf16[64,72,128]{2,1,0:T(8,128)(2,1)}), bf16[64,72,128]{2,1,0:T(8,128)(2,1)S(1)}, u32[]{:S(2)}, u32[]{:S(2)}) %all-to-all-start.1) | async-done | bytes 1179680 | tf_op jit(solution)/shard_map/all_to_all | solution.py:450
  95.4 0.2 fusion.1.q_ref
  95.7 4.7 %stats.1 = (f32[4,8,256]{2,1,0:T(8,128)S(1)}, bf16[4,1792,128]{2,1,0:T(8,128)(2,1)S(1)}) custom-call(s32[112]{0:T(128)S(1)} %select_reduce_fusion.chosen_ref, bf16[4,64,256]{2,1,0:T(8,128)(2,1)S(1)} %fusion.1.q_ref, bf16[4,64,256]{2,1,0:T(8,128)(2,1)S(1)} %select_bitcast_fusion.u_ref, bf16[64,72,128]{2,1,0:T(8,128)(2,1)S(1)} %all-to-all-done.1.k_ref, ...), custom_call_target="tpu_custom_call" | custom-call | flops 939524096 | bytes 2359296 | tf_op jit(solution)/shard_map/stats/pallas_call | solution.py:330
  100.4 8.7 %all_to_all.30.s_ref = f32[4,4,8,256]{3,2,1,0:T(8,128)S(1)} all-to-all(f32[4,4,8,256]{3,2,1,0:T(8,128)S(1)} %broadcast_in_dim.35), channel_id=1, replica_groups=mesh['sect'=2,'grp'=64,'tp'=4] {'tp'}, dimensions={0} | all-to-all | bytes 262144 | tf_op jit(solution)/shard_map/all_to_all | solution.py:450
  109.1 7.0 %query_value_grads.1 = (f32[4,64,256]{2,1,0:T(8,128)}, bf16[64,72,128]{2,1,0:T(8,128)(2,1)}) custom-call(s32[112]{0:T(128)S(1)} %select_reduce_fusion.chosen_ref, bf16[4,64,256]{2,1,0:T(8,128)(2,1)S(1)} %fusion.1.q_ref, bf16[4,64,256]{2,1,0:T(8,128)(2,1)S(1)} %select_bitcast_fusion.u_ref, bf16[64,64]{1,0:T(8,128)(2,1)S(1)} %copy-done.1, ...), custom_call_target="tpu_custom_call" | custom-call | flops 2818572288 | bytes 3670016 | tf_op jit(solution)/shard_map/query_value_grads/pallas_call | solution.py:366
  116.1 5.8 %all-to-all-start.3 = ((bf16[64,72,128]{2,1,0:T(8,128)(2,1)}), bf16[64,72,128]{2,1,0:T(8,128)(2,1)S(1)}, u32[]{:S(2)}, u32[]{:S(2)}) async-start(bf16[64,72,128]{2,1,0:T(8,128)(2,1)} %get-tuple-element.14), calls=%async_computation.3 | async-start | bytes 2359296 | tf_op jit(solution)/shard_map/all_to_all | solution.py:450
  121.9 1.5 copy-done.3
  123.4 5.7 %key_grads.1 = bf16[64,72,128]{2,1,0:T(8,128)(2,1)} custom-call(s32[112]{0:T(128)S(1)} %select_reduce_fusion.chosen_ref, bf16[4,64,256]{2,1,0:T(8,128)(2,1)S(1)} %fusion.1.q_ref, bf16[4,64,256]{2,1,0:T(8,128)(2,1)S(1)} %select_bitcast_fusion.u_ref, f32[4,4,8,256]{3,2,1,0:T(8,128)S(1)} %all_to_all.30.s_ref, bf16[4,1792,128]{2,1,0:T(8,128)(2,1)S(1)} %copy-done.3), custom_call_target="tpu_custom_call" | custom-call | flops 1879048192 | bytes 3670016 | tf_op jit(solution)/shard_map/key_grads/pallas_call | solution.py:405
  129.1 23.4 %all-to-all-done.3 = bf16[64,72,128]{2,1,0:T(8,128)(2,1)S(1)} async-done(((bf16[64,72,128]{2,1,0:T(8,128)(2,1)}), bf16[64,72,128]{2,1,0:T(8,128)(2,1)S(1)}, u32[]{:S(2)}, u32[]{:S(2)}) %all-to-all-start.3) | async-done | bytes 1179680 | tf_op jit(solution)/shard_map/all_to_all | solution.py:450
  152.6 0.7 broadcast_dynamic-update-slice_fusion
  153.3 5.2 %all-to-all-start.4 = ((bf16[64,72,128]{2,1,0:T(8,128)(2,1)}), bf16[64,72,128]{2,1,0:T(8,128)(2,1)S(1)}, u32[]{:S(2)}, u32[]{:S(2)}) async-start(bf16[64,72,128]{2,1,0:T(8,128)(2,1)} %broadcast_dynamic-update-slice_fusion), calls=%async_computation.4 | async-start | bytes 2359296 | tf_op jit(solution)/shard_map/all_to_all | solution.py:450
  158.5 2.8 %collective-permute-start.2 = (f32[64,256]{1,0:T(8,128)S(1)}, f32[64,256]{1,0:T(8,128)S(1)}, u32[]{:S(2)}, u32[]{:S(2)}) collective-permute-start(f32[64,256]{1,0:T(8,128)S(1)} %get-tuple-element.18), channel_id=1, source_target_pairs={{0,3},{1,0},{2,1},{3,2},{4,7},{5,4},{6,5},{7,6},{8,11},{9,8},{10,9... | collective-permute-start | bytes 196616 | tf_op jit(solution)/shard_map/ppermute | solution.py:441
  161.3 3.1 %collective-permute-start.1 = (f32[64,256]{1,0:T(8,128)S(1)}, f32[64,256]{1,0:T(8,128)S(1)}, u32[]{:S(2)}, u32[]{:S(2)}) collective-permute-start(f32[64,256]{1,0:T(8,128)S(1)} %get-tuple-element.19), channel_id=1, source_target_pairs={{0,2},{1,3},{2,0},{3,1},{4,6},{5,7},{6,4},{7,5},{8,10},{9,11},{10,... | collective-permute-start | bytes 196616 | tf_op jit(solution)/shard_map/ppermute | solution.py:441
  164.4 1.9 collective-permute-start
  166.4 1.6 collective-permute-done.1
  168.0 3.0 %collective-permute-done = f32[64,256]{1,0:T(8,128)S(1)} collective-permute-done((f32[64,256]{1,0:T(8,128)S(1)}, f32[64,256]{1,0:T(8,128)S(1)}, u32[]{:S(2)}, u32[]{:S(2)}) %collective-permute-start) | collective-permute-done | bytes 65568 | tf_op jit(solution)/shard_map/ppermute | solution.py:441
  171.1 0.3 convolution_bitcast_fusion
  171.4 15.2 %all-to-all-done.4 = bf16[64,72,128]{2,1,0:T(8,128)(2,1)S(1)} async-done(((bf16[64,72,128]{2,1,0:T(8,128)(2,1)}), bf16[64,72,128]{2,1,0:T(8,128)(2,1)S(1)}, u32[]{:S(2)}, u32[]{:S(2)}) %all-to-all-start.4) | async-done | bytes 1179680 | tf_op jit(solution)/shard_map/all_to_all | solution.py:450
  186.7 0.2 convolution_bitcast_fusion.1
  187.0 0.7 broadcast_in_dim.37
  187.7 9.5 %all-to-all-start.5 = ((f32[8,64,128]{2,1,0:T(8,128)}), f32[8,64,128]{2,1,0:T(8,128)S(1)}, u32[]{:S(2)}, u32[]{:S(2)}) async-start(f32[8,64,128]{2,1,0:T(8,128)} %broadcast_in_dim.37), calls=%async_computation.5 | async-start | bytes 524288 | tf_op jit(solution)/shard_map/all_to_all | solution.py:450
  197.2 1.3 unpack.3
  198.6 1.3 unpack.2
  199.9 3.9 %all-to-all-done.5 = f32[8,64,128]{2,1,0:T(8,128)S(1)} async-done(((f32[8,64,128]{2,1,0:T(8,128)}), f32[8,64,128]{2,1,0:T(8,128)S(1)}, u32[]{:S(2)}, u32[]{:S(2)}) %all-to-all-start.5) | async-done | bytes 262176 | tf_op jit(solution)/shard_map/all_to_all | solution.py:450
  203.8 0.7 fusion.14
  (42 shorter events, 1.1 us)
Async XLA Ops:
  3.8 17.3 %copy-start = (bf16[2,64,4096]{2,1,0:T(8,128)(2,1)S(1)}, bf16[2,64,4096]{2,1,0:T(8,128)(2,1)}, u32[]{:S(2)}) copy-start(bf16[2,64,4096]{2,1,0:T(8,128)(2,1)} %k_ref.1) | copy-start | bytes 3145732
  3.8 52.4 %all-to-all-start = ((bf16[64,80,128]{2,1,0:T(8,128)(2,1)}), bf16[64,80,128]{2,1,0:T(8,128)(2,1)S(1)}, u32[]{:S(2)}, u32[]{:S(2)}) async-start(bf16[64,80,128]{2,1,0:T(8,128)(2,1)} %bitcast.52), calls=%async_computation | async-start | bytes 2621440 | tf_op jit(solution)/shard_map/all_to_all | solution.py:450
  56.9 6.5 %copy-start.9 = (s32[4]{0:T(128)S(1)}, s32[4]{0:T(128)}, u32[]{:S(2)}) copy-start(s32[4]{0:T(128)} %param.19) | copy-start | bytes 52
  56.9 6.5 %copy-start.8 = (bf16[4,256,64]{1,2,0:T(8,128)(2,1)S(1)}, bf16[4,256,64]{1,2,0:T(8,128)(2,1)}, u32[]{:S(2)}) copy-start(bf16[4,256,64]{1,2,0:T(8,128)(2,1)} %param.13) | copy-start | bytes 393220
  56.9 38.5 %copy-start.1 = (bf16[64,64]{1,0:T(8,128)(2,1)S(1)}, bf16[64,64]{1,0:T(8,128)(2,1)}, u32[]{:S(2)}) copy-start(bf16[64,64]{1,0:T(8,128)(2,1)} %w_ref.1) | copy-start | bytes 24580
  56.9 38.5 %copy-start.7 = (bf16[4,256,64]{1,2,0:T(8,128)(2,1)S(1)}, bf16[4,256,64]{1,2,0:T(8,128)(2,1)}, u32[]{:S(2)}) copy-start(bf16[4,256,64]{1,2,0:T(8,128)(2,1)} %param.12) | copy-start | bytes 393220
  56.9 38.3 %all-to-all-start.1 = ((bf16[64,72,128]{2,1,0:T(8,128)(2,1)}), bf16[64,72,128]{2,1,0:T(8,128)(2,1)S(1)}, u32[]{:S(2)}, u32[]{:S(2)}) async-start(bf16[64,72,128]{2,1,0:T(8,128)(2,1)} %broadcast_dynamic-update-slice_fusion.1), calls=%async_computation.1 | async-start | bytes 2359296 | tf_op jit(solution)/shard_map/all_to_all | solution.py:450
  100.4 15.7 %copy-start.2 = (bf16[4,1792,128]{2,1,0:T(8,128)(2,1)}, bf16[4,1792,128]{2,1,0:T(8,128)(2,1)S(1)}, u32[]{:S(2)}) copy-start(bf16[4,1792,128]{2,1,0:T(8,128)(2,1)S(1)} %get-tuple-element.12.rows_ref) | copy-start | bytes 5505028
  116.1 36.4 %all-to-all-start.3 = ((bf16[64,72,128]{2,1,0:T(8,128)(2,1)}), bf16[64,72,128]{2,1,0:T(8,128)(2,1)S(1)}, u32[]{:S(2)}, u32[]{:S(2)}) async-start(bf16[64,72,128]{2,1,0:T(8,128)(2,1)} %get-tuple-element.14), calls=%async_computation.3 | async-start | bytes 2359296 | tf_op jit(solution)/shard_map/all_to_all | solution.py:450
  121.9 1.5 copy-start.3
  153.3 5.2 %copy-start.5 = (f32[4,64,256]{2,1,0:T(8,128)S(1)}, f32[4,64,256]{2,1,0:T(8,128)}, u32[]{:S(2)}) copy-start(f32[4,64,256]{2,1,0:T(8,128)} %get-tuple-element.13) | copy-start | bytes 786436
  153.3 33.3 %all-to-all-start.4 = ((bf16[64,72,128]{2,1,0:T(8,128)(2,1)}), bf16[64,72,128]{2,1,0:T(8,128)(2,1)S(1)}, u32[]{:S(2)}, u32[]{:S(2)}) async-start(bf16[64,72,128]{2,1,0:T(8,128)(2,1)} %broadcast_dynamic-update-slice_fusion), calls=%async_computation.4 | async-start | bytes 2359296 | tf_op jit(solution)/shard_map/all_to_all | solution.py:450
  158.4 28.3 %copy-start.4 = (bf16[4,256,64]{1,2,0:T(8,128)(2,1)S(1)}, bf16[4,256,64]{1,2,0:T(8,128)(2,1)}, u32[]{:S(2)}) copy-start(bf16[4,256,64]{1,2,0:T(8,128)(2,1)} %param.14) | copy-start | bytes 393220
  158.5 7.9 %collective-permute-start.2 = (f32[64,256]{1,0:T(8,128)S(1)}, f32[64,256]{1,0:T(8,128)S(1)}, u32[]{:S(2)}, u32[]{:S(2)}) collective-permute-start(f32[64,256]{1,0:T(8,128)S(1)} %get-tuple-element.18), channel_id=1, source_target_pairs={{0,3},{1,0},{2,1},{3,2},{4,7},{5,4},{6,5},{7,6},{8,11},{9,8},{10,9... | collective-permute-start | bytes 196616 | tf_op jit(solution)/shard_map/ppermute | solution.py:441
  161.3 6.6 %collective-permute-start.1 = (f32[64,256]{1,0:T(8,128)S(1)}, f32[64,256]{1,0:T(8,128)S(1)}, u32[]{:S(2)}, u32[]{:S(2)}) collective-permute-start(f32[64,256]{1,0:T(8,128)S(1)} %get-tuple-element.19), channel_id=1, source_target_pairs={{0,2},{1,3},{2,0},{3,1},{4,6},{5,7},{6,4},{7,5},{8,10},{9,11},{10,... | collective-permute-start | bytes 196616 | tf_op jit(solution)/shard_map/ppermute | solution.py:441
  164.4 6.5 %collective-permute-start = (f32[64,256]{1,0:T(8,128)S(1)}, f32[64,256]{1,0:T(8,128)S(1)}, u32[]{:S(2)}, u32[]{:S(2)}) collective-permute-start(f32[64,256]{1,0:T(8,128)S(1)} %get-tuple-element.17), channel_id=1, source_target_pairs={{0,1},{1,2},{2,3},{3,0},{4,5},{5,6},{6,7},{7,4},{8,9},{9,10},{10,1... | collective-permute-start | bytes 196616 | tf_op jit(solution)/shard_map/ppermute | solution.py:441
  171.1 27.5 %copy-start.6 = (bf16[64,256]{0,1:T(8,128)(2,1)}, bf16[64,256]{0,1:T(8,128)(2,1)S(1)}, u32[]{:S(2)}) copy-start(bf16[64,256]{0,1:T(8,128)(2,1)S(1)} %copy.31) | copy-start | bytes 98308
  187.7 16.0 %all-to-all-start.5 = ((f32[8,64,128]{2,1,0:T(8,128)}), f32[8,64,128]{2,1,0:T(8,128)S(1)}, u32[]{:S(2)}, u32[]{:S(2)}) async-start(f32[8,64,128]{2,1,0:T(8,128)} %broadcast_in_dim.37), calls=%async_computation.5 | async-start | bytes 524288 | tf_op jit(solution)/shard_map/all_to_all | solution.py:450

commit v7 on v6

--- a/solution.py
+++ b/solution.py
@@ -157,8 +157,8 @@
     )(table.reshape(shape))
 
 
-STATS_CHUNK = 4
-GRAD_CHUNK = 14
+STATS_CHUNK = 2
+GRAD_CHUNK = 28
 
 
 def two_sided(q_ref, u_ref):
@@ -202,16 +202,25 @@
         mass = mass * scale + jnp.sum(exp_scores, axis=0, keepdims=True)
         dot = dot * scale + jnp.sum(exp_scores * prob_grad, axis=0, keepdims=True)
         top = new_top
-    o_ref[0] = jnp.concatenate([top, mass, dot, jnp.zeros((5, targets), F32)], axis=0)
+
+    @pl.when(question == 0)
+    def _():
+        o_ref[...] = jnp.zeros_like(o_ref)
+
+    for i, row in enumerate((top, mass, dot)):
+        o_ref[pl.ds(i * pl.num_programs(0) + question, 1), :] = row
 
 
 def row_stats(s_ref):
-    members = s_ref.shape[0]
-    tops = [s_ref[i, 0, 0:1, :] for i in range(members)]
+    members, question = s_ref.shape[0], pl.program_id(0)
+    tops, masses, dots = [
+        [s_ref[m, pl.ds(i * pl.num_programs(0) + question, 1), :] for m in range(members)]
+        for i in range(3)
+    ]
     top = functools.reduce(jnp.maximum, tops)
     scales = [jnp.exp(t - top) for t in tops]
-    inverse = 1.0 / sum(s_ref[i, 0, 1:2, :] * scales[i] for i in range(members))
-    delta = sum(s_ref[i, 0, 2:3, :] * scales[i] for i in range(members)) * inverse
+    inverse = 1.0 / sum(masses[i] * scales[i] for i in range(members))
+    delta = sum(dots[i] * scales[i] for i in range(members)) * inverse
     return top, inverse, delta
 
 
@@ -323,6 +332,7 @@
 def attend_stats(chosen, query_t, upstream_t, key_table, value_table, per_question, slots, span):
     questions, size, targets = query_t.shape
     one = pl.BlockSpec((1, size, targets), lambda q, c: (q, 0, 0))
+    stat_rows = -(-3 * questions // 8) * 8
     tables = [
         pl.BlockSpec(table.shape, lambda q, c: (0, 0, 0)) for table in (key_table, value_table)
     ]
@@ -334,12 +344,12 @@
             grid=(questions,),
             in_specs=[one, one, *tables],
             out_specs=[
-                pl.BlockSpec((1, 8, targets), lambda q, c: (q, 0, 0)),
+                pl.BlockSpec((stat_rows, targets), lambda q, c: (0, 0)),
                 pl.BlockSpec((1, keys, 2 * size), lambda q, c: (q, 0, 0)),
             ],
         ),
         out_shape=[
-            jax.ShapeDtypeStruct((questions, 8, targets), F32),
+            jax.ShapeDtypeStruct((stat_rows, targets), F32),
             jax.ShapeDtypeStruct((questions, keys, 2 * size), BF16),
         ],
         compiler_params=pltpu.CompilerParams(vmem_limit_bytes=VMEM_LIMIT),
@@ -372,7 +382,7 @@
                 one,
                 one,
                 pl.BlockSpec(up_weight.shape, lambda q, c: (0, 0)),
-                pl.BlockSpec((peers, 1, 8, targets), lambda q, c: (0, q, 0, 0)),
+                pl.BlockSpec(stats.shape, lambda q, c: (0, 0, 0)),
                 whole,
             ],
             out_specs=[
@@ -410,7 +420,7 @@
             in_specs=[
                 one,
                 one,
-                pl.BlockSpec((peers, 1, 8, targets), lambda q, c: (0, q, 0, 0)),
+                pl.BlockSpec(stats.shape, lambda q, c: (0, 0, 0)),
                 whole,
             ],
             out_specs=pl.BlockSpec(out, lambda q, c: (0, 0, 0)),

time: 205 us -> 205 us (level)
  no operation moved by 1% of the time
where the time goes in v7:
time: 205 us; the launch traced here: 204 us
  waiting for transfers between devices  112 us (55%)
  starting transfers between devices  52 us (25%)
  Pallas kernels  23.6 us (12%)
  blocking collectives  8.32 us (4%)
  local copies, waits for them, and re-layouts  4.89 us (2%)
    all_to_all x5, waiting for transfers between devices, exchange(): lax.all_to_all(x, axis, split_axis=0, concat_axis=0, tiled=True, axis_ind...  107 us
    all_to_all x5, starting transfers between devices, exchange(): lax.all_to_all(x, axis, split_axis=0, concat_axis=0, tiled=True, axis_ind...  44.2 us
    all_to_all x1, blocking collectives, exchange(): lax.all_to_all(x, axis, split_axis=0, concat_axis=0, tiled=True, axis_ind...  8.32 us
    ppermute x3, starting transfers between devices, scatter_sum_tp(): lax.ppermute(sent, 'tp', [(i, (i + k) % size) for i in range(size)])  7.82 us
    pallas_call x1, Pallas kernels, query_value_grads(): pl.pallas_call(functools.partial(query_value_kernel, per_question, slots,...  6.95 us
    pallas_call x1, Pallas kernels, key_grads(): pl.pallas_call(functools.partial(key_kernel, per_question, slots, span),...  5.68 us
    ppermute x3, waiting for transfers between devices, scatter_sum_tp(): lax.ppermute(sent, 'tp', [(i, (i + k) % size) for i in range(size)])  4.55 us
    pallas_call x1, Pallas kernels, attend_stats(): pl.pallas_call(functools.partial(stats_kernel, per_question, slots, span)...  4.48 us
  transfers between devices with their start and end apart: 8, of which 7 were waited for; matrix products, arithmetic and copies ran while one was open for 1% of the time, Pallas kernels for 5%

profile of v7, /device:TPU:1, one launch (start us, length us, event | category | flops | bytes accessed | tf_op | source)
XLA Modules:
  0.0 203.9 jit_solution(5648909019943819194)
XLA Ops:
  1.3 2.5 %pack_values.1 = bf16[16,2,2,80,128]{4,3,2,1,0:T(8,128)(2,1)} custom-call(s32[2]{0:T(128)} %owner_ref.1, s32[1]{0:T(128)S(6)} %copy.42.counts_ref, bf16[64,64]{1,0:T(8,128)(2,1)} %down_ref.1, bf16[4,64,256]{2,1,0:T(8,128)(2,1)} %bitcast.53, bf16[2,64,4096]{2,1,0:T(8,128)(2,1)} %v_ref.1), custom_call_target="tpu_custom_call" | custom-call | flops 8388608 | bytes 2097152 | tf_op jit(solution)/shard_map/pack_values/pallas_call | solution.py:122
  3.8 17.3 %all-to-all-start = ((bf16[64,80,128]{2,1,0:T(8,128)(2,1)}), bf16[64,80,128]{2,1,0:T(8,128)(2,1)S(1)}, u32[]{:S(2)}, u32[]{:S(2)}) async-start(bf16[64,80,128]{2,1,0:T(8,128)(2,1)} %bitcast.52), calls=%async_computation | async-start | bytes 2621440 | tf_op jit(solution)/shard_map/all_to_all | solution.py:460
  21.1 1.3 pack_keys.1
  22.4 33.8 %all-to-all-done.v_ref = bf16[64,80,128]{2,1,0:T(8,128)(2,1)S(1)} async-done(((bf16[64,80,128]{2,1,0:T(8,128)(2,1)}), bf16[64,80,128]{2,1,0:T(8,128)(2,1)S(1)}, u32[]{:S(2)}, u32[]{:S(2)}) %all-to-all-start) | async-done | bytes 1310752 | tf_op jit(solution)/shard_map/all_to_all | solution.py:460
  56.2 0.7 broadcast_dynamic-update-slice_fusion.1
  56.9 6.4 %all-to-all-start.1 = ((bf16[64,72,128]{2,1,0:T(8,128)(2,1)}), bf16[64,72,128]{2,1,0:T(8,128)(2,1)S(1)}, u32[]{:S(2)}, u32[]{:S(2)}) async-start(bf16[64,72,128]{2,1,0:T(8,128)(2,1)} %broadcast_dynamic-update-slice_fusion.1), calls=%async_computation.1 | async-start | bytes 2359296 | tf_op jit(solution)/shard_map/all_to_all | solution.py:460
  63.8 0.2 convert_reduce_fusion
  64.1 31.2 %all-to-all-done.1.k_ref = bf16[64,72,128]{2,1,0:T(8,128)(2,1)S(1)} async-done(((bf16[64,72,128]{2,1,0:T(8,128)(2,1)}), bf16[64,72,128]{2,1,0:T(8,128)(2,1)S(1)}, u32[]{:S(2)}, u32[]{:S(2)}) %all-to-all-start.1) | async-done | bytes 1179680 | tf_op jit(solution)/shard_map/all_to_all | solution.py:460
  95.4 0.2 fusion.1.q_ref
  95.7 4.5 %stats.1 = (f32[16,256]{1,0:T(8,128)S(1)}, bf16[4,1792,128]{2,1,0:T(8,128)(2,1)S(1)}) custom-call(s32[112]{0:T(128)S(1)} %select_reduce_fusion.chosen_ref, bf16[4,64,256]{2,1,0:T(8,128)(2,1)S(1)} %fusion.1.q_ref, bf16[4,64,256]{2,1,0:T(8,128)(2,1)S(1)} %select_bitcast_fusion.u_ref, bf16[64,72,128]{2,1,0:T(8,128)(2,1)S(1)} %all-to-all-done.1.k_ref, ...), custom_call_target="tpu_custom_call" | custom-call | flops 939524096 | bytes 2359296 | tf_op jit(solution)/shard_map/stats/pallas_call | solution.py:340
  100.2 8.3 %all_to_all.30.s_ref = f32[4,16,256]{2,1,0:T(8,128)S(1)} all-to-all(f32[4,16,256]{2,1,0:T(8,128)S(1)} %broadcast_in_dim.35), channel_id=1, replica_groups=mesh['sect'=2,'grp'=64,'tp'=4] {'tp'}, dimensions={0} | all-to-all | bytes 131072 | tf_op jit(solution)/shard_map/all_to_all | solution.py:460
  108.5 6.9 %query_value_grads.1 = (f32[4,64,256]{2,1,0:T(8,128)}, bf16[64,72,128]{2,1,0:T(8,128)(2,1)}) custom-call(s32[112]{0:T(128)S(1)} %select_reduce_fusion.chosen_ref, bf16[4,64,256]{2,1,0:T(8,128)(2,1)S(1)} %fusion.1.q_ref, bf16[4,64,256]{2,1,0:T(8,128)(2,1)S(1)} %select_bitcast_fusion.u_ref, bf16[64,64]{1,0:T(8,128)(2,1)S(1)} %copy-done.1, ...), custom_call_target="tpu_custom_call" | custom-call | flops 2818572288 | bytes 3670016 | tf_op jit(solution)/shard_map/query_value_grads/pallas_call | solution.py:376
  115.4 5.9 %all-to-all-start.3 = ((bf16[64,72,128]{2,1,0:T(8,128)(2,1)}), bf16[64,72,128]{2,1,0:T(8,128)(2,1)S(1)}, u32[]{:S(2)}, u32[]{:S(2)}) async-start(bf16[64,72,128]{2,1,0:T(8,128)(2,1)} %get-tuple-element.14), calls=%async_computation.3 | async-start | bytes 2359296 | tf_op jit(solution)/shard_map/all_to_all | solution.py:460
  121.3 1.5 copy-done.3
  122.8 5.7 %key_grads.1 = bf16[64,72,128]{2,1,0:T(8,128)(2,1)} custom-call(s32[112]{0:T(128)S(1)} %select_reduce_fusion.chosen_ref, bf16[4,64,256]{2,1,0:T(8,128)(2,1)S(1)} %fusion.1.q_ref, bf16[4,64,256]{2,1,0:T(8,128)(2,1)S(1)} %select_bitcast_fusion.u_ref, f32[4,16,256]{2,1,0:T(8,128)S(1)} %all_to_all.30.s_ref, bf16[4,1792,128]{2,1,0:T(8,128)(2,1)S(1)} %copy-done.3), custom_call_target="tpu_custom_call" | custom-call | flops 1879048192 | bytes 3670016 | tf_op jit(solution)/shard_map/key_grads/pallas_call | solution.py:415
  128.5 23.4 %all-to-all-done.3 = bf16[64,72,128]{2,1,0:T(8,128)(2,1)S(1)} async-done(((bf16[64,72,128]{2,1,0:T(8,128)(2,1)}), bf16[64,72,128]{2,1,0:T(8,128)(2,1)S(1)}, u32[]{:S(2)}, u32[]{:S(2)}) %all-to-all-start.3) | async-done | bytes 1179680 | tf_op jit(solution)/shard_map/all_to_all | solution.py:460
  152.0 0.7 broadcast_dynamic-update-slice_fusion
  152.7 5.2 %all-to-all-start.4 = ((bf16[64,72,128]{2,1,0:T(8,128)(2,1)}), bf16[64,72,128]{2,1,0:T(8,128)(2,1)S(1)}, u32[]{:S(2)}, u32[]{:S(2)}) async-start(bf16[64,72,128]{2,1,0:T(8,128)(2,1)} %broadcast_dynamic-update-slice_fusion), calls=%async_computation.4 | async-start | bytes 2359296 | tf_op jit(solution)/shard_map/all_to_all | solution.py:460
  158.0 2.8 %collective-permute-start.2 = (f32[64,256]{1,0:T(8,128)S(1)}, f32[64,256]{1,0:T(8,128)S(1)}, u32[]{:S(2)}, u32[]{:S(2)}) collective-permute-start(f32[64,256]{1,0:T(8,128)S(1)} %get-tuple-element.18), channel_id=1, source_target_pairs={{0,3},{1,0},{2,1},{3,2},{4,7},{5,4},{6,5},{7,6},{8,11},{9,8},{10,9... | collective-permute-start | bytes 196616 | tf_op jit(solution)/shard_map/ppermute | solution.py:451
  160.8 3.1 %collective-permute-start.1 = (f32[64,256]{1,0:T(8,128)S(1)}, f32[64,256]{1,0:T(8,128)S(1)}, u32[]{:S(2)}, u32[]{:S(2)}) collective-permute-start(f32[64,256]{1,0:T(8,128)S(1)} %get-tuple-element.19), channel_id=1, source_target_pairs={{0,2},{1,3},{2,0},{3,1},{4,6},{5,7},{6,4},{7,5},{8,10},{9,11},{10,... | collective-permute-start | bytes 196616 | tf_op jit(solution)/shard_map/ppermute | solution.py:451
  163.9 1.9 collective-permute-start
  165.8 1.6 collective-permute-done.1
  167.4 3.0 %collective-permute-done = f32[64,256]{1,0:T(8,128)S(1)} collective-permute-done((f32[64,256]{1,0:T(8,128)S(1)}, f32[64,256]{1,0:T(8,128)S(1)}, u32[]{:S(2)}, u32[]{:S(2)}) %collective-permute-start) | collective-permute-done | bytes 65568 | tf_op jit(solution)/shard_map/ppermute | solution.py:451
  170.5 0.3 convolution_bitcast_fusion
  170.8 15.2 %all-to-all-done.4 = bf16[64,72,128]{2,1,0:T(8,128)(2,1)S(1)} async-done(((bf16[64,72,128]{2,1,0:T(8,128)(2,1)}), bf16[64,72,128]{2,1,0:T(8,128)(2,1)S(1)}, u32[]{:S(2)}, u32[]{:S(2)}) %all-to-all-start.4) | async-done | bytes 1179680 | tf_op jit(solution)/shard_map/all_to_all | solution.py:460
  186.2 0.2 convolution_bitcast_fusion.1
  186.4 0.7 broadcast_in_dim.37
  187.1 9.5 %all-to-all-start.5 = ((f32[8,64,128]{2,1,0:T(8,128)}), f32[8,64,128]{2,1,0:T(8,128)S(1)}, u32[]{:S(2)}, u32[]{:S(2)}) async-start(f32[8,64,128]{2,1,0:T(8,128)} %broadcast_in_dim.37), calls=%async_computation.5 | async-start | bytes 524288 | tf_op jit(solution)/shard_map/all_to_all | solution.py:460
  196.6 1.3 unpack.3
  198.0 1.3 unpack.2
  199.3 3.9 %all-to-all-done.5 = f32[8,64,128]{2,1,0:T(8,128)S(1)} async-done(((f32[8,64,128]{2,1,0:T(8,128)}), f32[8,64,128]{2,1,0:T(8,128)S(1)}, u32[]{:S(2)}, u32[]{:S(2)}) %all-to-all-start.5) | async-done | bytes 262176 | tf_op jit(solution)/shard_map/all_to_all | solution.py:460
  203.2 0.7 fusion.14
  (42 shorter events, 1.1 us)
Async XLA Ops:
  3.8 17.3 %copy-start = (bf16[2,64,4096]{2,1,0:T(8,128)(2,1)S(1)}, bf16[2,64,4096]{2,1,0:T(8,128)(2,1)}, u32[]{:S(2)}) copy-start(bf16[2,64,4096]{2,1,0:T(8,128)(2,1)} %k_ref.1) | copy-start | bytes 3145732
  3.8 52.4 %all-to-all-start = ((bf16[64,80,128]{2,1,0:T(8,128)(2,1)}), bf16[64,80,128]{2,1,0:T(8,128)(2,1)S(1)}, u32[]{:S(2)}, u32[]{:S(2)}) async-start(bf16[64,80,128]{2,1,0:T(8,128)(2,1)} %bitcast.52), calls=%async_computation | async-start | bytes 2621440 | tf_op jit(solution)/shard_map/all_to_all | solution.py:460
  56.9 6.5 %copy-start.9 = (s32[4]{0:T(128)S(1)}, s32[4]{0:T(128)}, u32[]{:S(2)}) copy-start(s32[4]{0:T(128)} %param.19) | copy-start | bytes 52
  56.9 6.5 %copy-start.8 = (bf16[4,256,64]{1,2,0:T(8,128)(2,1)S(1)}, bf16[4,256,64]{1,2,0:T(8,128)(2,1)}, u32[]{:S(2)}) copy-start(bf16[4,256,64]{1,2,0:T(8,128)(2,1)} %param.13) | copy-start | bytes 393220
  56.9 38.5 %copy-start.1 = (bf16[64,64]{1,0:T(8,128)(2,1)S(1)}, bf16[64,64]{1,0:T(8,128)(2,1)}, u32[]{:S(2)}) copy-start(bf16[64,64]{1,0:T(8,128)(2,1)} %w_ref.1) | copy-start | bytes 24580
  56.9 38.5 %copy-start.7 = (bf16[4,256,64]{1,2,0:T(8,128)(2,1)S(1)}, bf16[4,256,64]{1,2,0:T(8,128)(2,1)}, u32[]{:S(2)}) copy-start(bf16[4,256,64]{1,2,0:T(8,128)(2,1)} %param.12) | copy-start | bytes 393220
  56.9 38.3 %all-to-all-start.1 = ((bf16[64,72,128]{2,1,0:T(8,128)(2,1)}), bf16[64,72,128]{2,1,0:T(8,128)(2,1)S(1)}, u32[]{:S(2)}, u32[]{:S(2)}) async-start(bf16[64,72,128]{2,1,0:T(8,128)(2,1)} %broadcast_dynamic-update-slice_fusion.1), calls=%async_computation.1 | async-start | bytes 2359296 | tf_op jit(solution)/shard_map/all_to_all | solution.py:460
  100.1 15.3 %copy-start.2 = (bf16[4,1792,128]{2,1,0:T(8,128)(2,1)}, bf16[4,1792,128]{2,1,0:T(8,128)(2,1)S(1)}, u32[]{:S(2)}) copy-start(bf16[4,1792,128]{2,1,0:T(8,128)(2,1)S(1)} %get-tuple-element.12.rows_ref) | copy-start | bytes 5505028
  115.4 36.5 %all-to-all-start.3 = ((bf16[64,72,128]{2,1,0:T(8,128)(2,1)}), bf16[64,72,128]{2,1,0:T(8,128)(2,1)S(1)}, u32[]{:S(2)}, u32[]{:S(2)}) async-start(bf16[64,72,128]{2,1,0:T(8,128)(2,1)} %get-tuple-element.14), calls=%async_computation.3 | async-start | bytes 2359296 | tf_op jit(solution)/shard_map/all_to_all | solution.py:460
  121.3 1.5 copy-start.3
  152.7 5.2 %copy-start.5 = (f32[4,64,256]{2,1,0:T(8,128)S(1)}, f32[4,64,256]{2,1,0:T(8,128)}, u32[]{:S(2)}) copy-start(f32[4,64,256]{2,1,0:T(8,128)} %get-tuple-element.13) | copy-start | bytes 786436
  152.7 33.3 %all-to-all-start.4 = ((bf16[64,72,128]{2,1,0:T(8,128)(2,1)}), bf16[64,72,128]{2,1,0:T(8,128)(2,1)S(1)}, u32[]{:S(2)}, u32[]{:S(2)}) async-start(bf16[64,72,128]{2,1,0:T(8,128)(2,1)} %broadcast_dynamic-update-slice_fusion), calls=%async_computation.4 | async-start | bytes 2359296 | tf_op jit(solution)/shard_map/all_to_all | solution.py:460
  157.9 28.3 %copy-start.4 = (bf16[4,256,64]{1,2,0:T(8,128)(2,1)S(1)}, bf16[4,256,64]{1,2,0:T(8,128)(2,1)}, u32[]{:S(2)}) copy-start(bf16[4,256,64]{1,2,0:T(8,128)(2,1)} %param.14) | copy-start | bytes 393220
  158.0 7.9 %collective-permute-start.2 = (f32[64,256]{1,0:T(8,128)S(1)}, f32[64,256]{1,0:T(8,128)S(1)}, u32[]{:S(2)}, u32[]{:S(2)}) collective-permute-start(f32[64,256]{1,0:T(8,128)S(1)} %get-tuple-element.18), channel_id=1, source_target_pairs={{0,3},{1,0},{2,1},{3,2},{4,7},{5,4},{6,5},{7,6},{8,11},{9,8},{10,9... | collective-permute-start | bytes 196616 | tf_op jit(solution)/shard_map/ppermute | solution.py:451
  160.8 6.6 %collective-permute-start.1 = (f32[64,256]{1,0:T(8,128)S(1)}, f32[64,256]{1,0:T(8,128)S(1)}, u32[]{:S(2)}, u32[]{:S(2)}) collective-permute-start(f32[64,256]{1,0:T(8,128)S(1)} %get-tuple-element.19), channel_id=1, source_target_pairs={{0,2},{1,3},{2,0},{3,1},{4,6},{5,7},{6,4},{7,5},{8,10},{9,11},{10,... | collective-permute-start | bytes 196616 | tf_op jit(solution)/shard_map/ppermute | solution.py:451
  163.9 6.5 %collective-permute-start = (f32[64,256]{1,0:T(8,128)S(1)}, f32[64,256]{1,0:T(8,128)S(1)}, u32[]{:S(2)}, u32[]{:S(2)}) collective-permute-start(f32[64,256]{1,0:T(8,128)S(1)} %get-tuple-element.17), channel_id=1, source_target_pairs={{0,1},{1,2},{2,3},{3,0},{4,5},{5,6},{6,7},{7,4},{8,9},{9,10},{10,1... | collective-permute-start | bytes 196616 | tf_op jit(solution)/shard_map/ppermute | solution.py:451
  170.5 27.5 %copy-start.6 = (bf16[64,256]{0,1:T(8,128)(2,1)}, bf16[64,256]{0,1:T(8,128)(2,1)S(1)}, u32[]{:S(2)}) copy-start(bf16[64,256]{0,1:T(8,128)(2,1)S(1)} %copy.31) | copy-start | bytes 98308
  187.1 16.1 %all-to-all-start.5 = ((f32[8,64,128]{2,1,0:T(8,128)}), f32[8,64,128]{2,1,0:T(8,128)S(1)}, u32[]{:S(2)}, u32[]{:S(2)}) async-start(f32[8,64,128]{2,1,0:T(8,128)} %broadcast_in_dim.37), calls=%async_computation.5 | async-start | bytes 524288 | tf_op jit(solution)/shard_map/all_to_all | solution.py:460
